TPU v7x, 32 devices: a whole 2x2x4 slice. The times are simulated.
32 devices in a mesh: group: 4 (over y, x), fsdp: 8 (over z, core).
Axes of the slice: x: 2, y: 2, z: 4, core: 2. Of those that a mesh axis runs over, the one named last changes fastest.
Arguments:
- activations: bfloat16 [4, 2048, 8192], P('group', 'fsdp'), may hold values from -6 to 6
- cotangent: bfloat16 [4, 2048, 512], P('group', 'fsdp'), may hold values from -0.25 to 0.25
- inner_weights: float32 [4, 8192, 512], P('group', 'fsdp'), may hold values from -6 to 6
- first_moment: float32 [4, 8192, 512], P('group', 'fsdp'), may hold values from -6 to 6
- second_moment: float32 [4, 8192, 512], P('group', 'fsdp'), may hold values from 0.5 to 4
- anchor: float32 [8192, 512], P('fsdp'), may hold values from -6 to 6
- outer_momentum: float32 [8192, 512], P('fsdp'), may hold values from -6 to 6
- fragment: int32 [1], replicated, may hold values from 0 to 3
Outputs:
- input_grad: bfloat16 [4, 2048, 8192], P('group', 'fsdp')
- new_inner: float32 [4, 8192, 512], P('group', 'fsdp')
- new_first: float32 [4, 8192, 512], P('group', 'fsdp')
- new_second: float32 [4, 8192, 512], P('group', 'fsdp')
- new_anchor: float32 [8192, 512], P('fsdp')
- new_momentum: float32 [8192, 512], P('fsdp')
All inputs are finite; a program needn't handle non-finite values.
Results may differ from a plain program's by a relative error of at most 0.006.
Values may be sent and summed in bfloat16 or wider, within the bound.
No kernel may reach another device: no remote copies, remote signals or barrier semaphores. Data moves between devices by JAX's collectives and lax.ppermute only.
A program may use at most 128 MiB of HBM per device.

v0:
```python
import jax
import jax.numpy as jnp
from jax import lax
from jax.sharding import PartitionSpec as P

HEAD = 128
STEP = 100


def per_device(
    activations,
    cotangent,
    inner_weights,
    first_moment,
    second_moment,
    anchor,
    outer_momentum,
    fragment,
):
    tokens_in = activations[0]
    upstream = cotangent[0]
    weights = inner_weights[0]
    low_weights = weights.astype(jnp.bfloat16)
    input_grad = lax.dot_general(
        upstream,
        lax.all_gather(low_weights, "fsdp", axis=0, tiled=True),
        (((1,), (1,)), ((), ())),
        preferred_element_type=jnp.float32,
    ).astype(jnp.bfloat16)
    gradient = lax.psum_scatter(
        lax.dot_general(
            tokens_in, upstream, (((0,), (0,)), ((), ())), preferred_element_type=jnp.float32
        ),
        "fsdp",
        scatter_dimension=0,
        tiled=True,
    )
    new_first = 0.9 * first_moment[0] + 0.1 * gradient
    new_second = 0.95 * second_moment[0] + 0.05 * gradient * gradient
    corr_one = 1.0 - 0.9**STEP
    corr_two = 1.0 - 0.95**STEP
    update = new_first / corr_one / (jnp.sqrt(new_second / corr_two) + 1e-08) + 0.1 * weights
    stepped = weights - 0.1 * update
    offset = fragment[0] * HEAD
    local_cols = lax.dynamic_slice_in_dim(stepped, offset, HEAD, 1)
    anchor_cols = lax.dynamic_slice_in_dim(anchor, offset, HEAD, 1)
    moment_cols = lax.dynamic_slice_in_dim(outer_momentum, offset, HEAD, 1)
    summed = lax.psum((anchor_cols - local_cols).astype(jnp.bfloat16), "group").astype(jnp.float32)
    average = summed / lax.axis_size("group")
    moment_new = 0.9 * moment_cols + average
    anchor_next = anchor_cols - 0.7 * (average + 0.9 * moment_new)
    new_momentum = lax.dynamic_update_slice_in_dim(outer_momentum, moment_new, offset, 1)
    new_anchor = lax.dynamic_update_slice_in_dim(anchor, anchor_next, offset, 1)
    new_inner = lax.dynamic_update_slice_in_dim(stepped, anchor_next, offset, 1)
    return (
        input_grad[None],
        new_inner[None],
        new_first[None],
        new_second[None],
        new_anchor,
        new_momentum,
    )


def solution(mesh):
    in_specs = (
        P("group", "fsdp", None),
        P("group", "fsdp", None),
        P("group", "fsdp", None),
        P("group", "fsdp", None),
        P("group", "fsdp", None),
        P("fsdp", None),
        P("fsdp", None),
        P(),
    )
    out_specs = (
        P("group", "fsdp", None),
        P("group", "fsdp", None),
        P("group", "fsdp", None),
        P("group", "fsdp", None),
        P("fsdp", None),
        P("fsdp", None),
    )
    return jax.shard_map(
        per_device, mesh=mesh, in_specs=in_specs, out_specs=out_specs, check_vma=False
    )
```

profile of v0, /device:TPU:0, one launch (start us, length us, event | category | flops | bytes accessed | tf_op | source)
XLA Modules:
  0.0 331.7 jit_solution(9196676631202798908)
XLA Ops:
  7.2 0.0 copy-start
  7.2 0.0 reduce-scatter.2.cloned.1.call-start
  7.2 3.2 copy.21
  10.5 1.3 copy.22
  11.8 1.6 copy-done.4
  13.4 8.1 %fusion.1 = f32[8192,512]{1,0:T(8,128)} fusion(bf16[1,256,8192]{2,1,0:T(8,128)(2,1)S(1)} %copy-done.4, bf16[1,256,512]{2,1,0:T(8,128)(2,1)S(1)} %copy-done), kind=kOutput, calls=%fused_computation.2 | convolution fusion | flops 2147483648 | bytes 21233664 | tf_op jit(solution)/shard_map/dot_general | solution.py:31
  21.5 0.0 reduce-scatter.2.cloned.1.call-update
  21.6 0.0 all-gather.2.cloned.1.call-start
  21.6 1.5 copy-done.1
  23.1 1.1 bitcast_convert_fusion
  24.2 0.0 all-gather.2.cloned.1.call-update
  24.3 0.0 all-reduce.2.cloned.1.call-start
  25.0 167.7 %reduce-scatter.2.cloned.1.call-done = f32[1024,512]{1,0:T(8,128)} async-done(((f32[8192,512]{1,0:T(8,128)}), f32[1024,512]{1,0:T(8,128)}) %reduce-scatter.2.cloned.1.call-update) | async-done | bytes 2097168 | tf_op jit(solution)/shard_map/reduce_scatter | solution.py:30
  192.7 6.4 %fusion.7 = (f32[1,1024,512]{2,1,0:T(8,128)}, f32[1024,512]{1,0:T(8,128)S(1)}, f32[1,1024,512]{2,1,0:T(8,128)}) fusion(f32[1024,512]{1,0:T(8,128)} %reduce-scatter.2.cloned.1.call-done, f32[1,1024,512]{2,1,0:T(8,128)} %param.12, f32[1,1024,512]{2,1,0:T(8,128)} %param.11, f32[1,1024,512]{2,1,0:T(8,128)S(1)} %copy-done.1), kind=kLoop, calls=%fused_computation.13 | loop fusion | flops 7864320 | bytes 14680064 | tf_op jit(solution)/shard_map/broadcast_in_dim | solution.py:59
  199.1 1.3 copy-done.5
  200.4 1.9 subtract_convert_fusion
  202.4 0.0 all-reduce.2.cloned.1.call-update
  202.4 0.0 copy-start.2
  202.4 72.9 %all-gather.2.cloned.1.call-done = bf16[8192,512]{1,0:T(8,128)(2,1)} async-done(((bf16[1024,512]{1,0:T(8,128)(2,1)}), bf16[8192,512]{1,0:T(8,128)(2,1)}) %all-gather.2.cloned.1.call-update) | async-done | bytes 8388624 | tf_op jit(solution)/shard_map/all_gather | solution.py:26
  275.3 7.8 %fusion = bf16[1,256,8192]{2,1,0:T(8,128)(2,1)} fusion(bf16[8192,512]{1,0:T(8,128)(2,1)} %all-gather.2.cloned.1.call-done, bf16[1,256,512]{2,1,0:T(8,128)(2,1)S(1)} %copy-done), kind=kOutput, calls=%fused_computation.1 | convolution fusion | flops 2149580800 | bytes 12845056 | tf_op jit(solution)/shard_map/dot_general | solution.py:24
  283.0 36.7 %all-reduce.2.cloned.1.call-done = bf16[1024,128]{1,0:T(8,128)(2,1)} async-done(((bf16[1024,128]{1,0:T(8,128)(2,1)}), bf16[1024,128]{1,0:T(8,128)(2,1)}) %all-reduce.2.cloned.1.call-update) | async-done | bytes 262160 | tf_op jit(solution)/shard_map/psum | solution.py:48
  319.7 2.1 bitcast_dynamic-update-slice_fusion
  321.8 2.1 fusion.8
  323.9 1.3 copy-done.3
  (8 shorter events, 0.0 us)
Async XLA Ops:
  7.2 4.6 %copy-start = (bf16[1,256,512]{2,1,0:T(8,128)(2,1)S(1)}, bf16[1,256,512]{2,1,0:T(8,128)(2,1)}, u32[]{:S(2)}) copy-start(bf16[1,256,512]{2,1,0:T(8,128)(2,1)} %param.9) | copy-start | bytes 786436
  7.2 3.3 copy-start.6
  7.2 185.5 %reduce-scatter.2.cloned.1.call-start = ((), (), s32[]{:S(2)}) async-start(), calls=%async_computation.2 | async-start | bytes 18874368 | tf_op jit(solution)/shard_map/reduce_scatter | solution.py:30
  10.5 2.9 copy-start.4
  21.5 1.6 copy-start.1
  21.6 253.7 %all-gather.2.cloned.1.call-start = ((), (), s32[]{:S(2)}) async-start(), calls=%async_computation.1 | async-start | bytes 9437184 | tf_op jit(solution)/shard_map/all_gather | solution.py:26
  24.3 295.4 %all-reduce.2.cloned.1.call-start = ((), (), s32[]{:S(2)}) async-start(), calls=%async_computation.3 | async-start | bytes 524288 | tf_op jit(solution)/shard_map/psum | solution.py:48
  199.1 1.3 copy-start.5
  202.4 117.3 %copy-start.2 = (f32[1024,512]{1,0:T(8,128)S(1)}, f32[1024,512]{1,0:T(8,128)}, u32[]{:S(2)}) copy-start(f32[1024,512]{1,0:T(8,128)} %copy.21) | copy-start | bytes 6291460
  323.9 1.3 copy-start.3
Sparse Core Ops, SparseCore 0:
  21.7 170.9 reduce-scatter.1
  194.8 80.3 all-gather.1
  278.2 41.4 all-reduce.1
where the time goes:
time: 332 us
  waiting for transfers between devices  277 us (83%)
  matrix products  15.9 us (5%)
  between operations  14.4 us (4%)
  other arithmetic  13.6 us (4%)
  local copies, waits for them, and re-layouts  10.3 us (3%)
    reduce_scatter x1, waiting for transfers between devices, per_device(): lax.psum_scatter(lax.dot_general(tokens_in, upstream, (((0,), (0,)), ((),...  168 us
    all_gather x1, waiting for transfers between devices, per_device(): lax.all_gather(low_weights, 'fsdp', axis=0, tiled=True)  72.9 us
    psum x1, waiting for transfers between devices, per_device(): lax.psum((anchor_cols - local_cols).astype(jnp.bfloat16), 'group')  36.7 us
    unnamed x16, local copies, waits for them, and re-layouts  10.3 us
    dot_general x1, matrix products, per_device(): lax.dot_general(tokens_in, upstream, (((0,), (0,)), ((), ())), preferred_...  8.12 us
    dot_general x1, matrix products, per_device(): lax.dot_general(upstream, lax.all_gather(low_weights, 'fsdp', axis=0, til...  7.77 us
  transfers between devices with their start and end apart: 3, of which 3 were waited for; matrix products, arithmetic and copies ran while one was open for 5% of the time, Pallas kernels for 0%

commit v1 on v0

v1 whole, which is shorter than its diff:
```python
import functools

import jax
import jax.numpy as jnp
from jax import lax
from jax.experimental import pallas as pl
from jax.experimental.pallas import tpu as pltpu
from jax.sharding import PartitionSpec as P

HEAD = 128
STEP = 100
CORR_ONE = 1.0 - 0.9**STEP
CORR_TWO = 1.0 - 0.95**STEP
PARTS = 2
TILE = 256
BF16 = jnp.bfloat16
F32 = jnp.float32


def plain(
    activations,
    cotangent,
    inner_weights,
    first_moment,
    second_moment,
    anchor,
    outer_momentum,
    fragment,
):
    tokens_in = activations[0]
    upstream = cotangent[0]
    weights = inner_weights[0]
    low_weights = weights.astype(BF16)
    input_grad = lax.dot_general(
        upstream,
        lax.all_gather(low_weights, "fsdp", axis=0, tiled=True),
        (((1,), (1,)), ((), ())),
        preferred_element_type=F32,
    ).astype(BF16)
    gradient = lax.psum_scatter(
        lax.dot_general(tokens_in, upstream, (((0,), (0,)), ((), ())), preferred_element_type=F32),
        "fsdp",
        scatter_dimension=0,
        tiled=True,
    )
    new_first = 0.9 * first_moment[0] + 0.1 * gradient
    new_second = 0.95 * second_moment[0] + 0.05 * gradient * gradient
    update = new_first / CORR_ONE / (jnp.sqrt(new_second / CORR_TWO) + 1e-08) + 0.1 * weights
    stepped = weights - 0.1 * update
    offset = fragment[0] * HEAD
    local_cols = lax.dynamic_slice_in_dim(stepped, offset, HEAD, 1)
    anchor_cols = lax.dynamic_slice_in_dim(anchor, offset, HEAD, 1)
    moment_cols = lax.dynamic_slice_in_dim(outer_momentum, offset, HEAD, 1)
    summed = lax.psum((anchor_cols - local_cols).astype(BF16), "group").astype(F32)
    average = summed / lax.axis_size("group")
    moment_new = 0.9 * moment_cols + average
    anchor_next = anchor_cols - 0.7 * (average + 0.9 * moment_new)
    new_momentum = lax.dynamic_update_slice_in_dim(outer_momentum, moment_new, offset, 1)
    new_anchor = lax.dynamic_update_slice_in_dim(anchor, anchor_next, offset, 1)
    new_inner = lax.dynamic_update_slice_in_dim(stepped, anchor_next, offset, 1)
    return (
        input_grad[None],
        new_inner[None],
        new_first[None],
        new_second[None],
        new_anchor,
        new_momentum,
    )


def rows_by_columns(act, cot):
    return lax.dot_general(act, cot, (((0,), (0,)), ((), ())), preferred_element_type=F32)


def call(body, scalars, grid, ins, outs, aliases=None, cost=(0, 0)):
    def spec(block, where):
        if block is None:
            return pl.BlockSpec(memory_space=pl.ANY)
        return pl.BlockSpec(block, where)

    return pl.pallas_call(
        body,
        grid_spec=pltpu.PrefetchScalarGridSpec(
            num_scalar_prefetch=1,
            grid=grid,
            in_specs=[spec(b, w) for _, b, w in ins],
            out_specs=[spec(b, w) for _, _, b, w in outs],
        ),
        out_shape=[jax.ShapeDtypeStruct(s, t) for s, t, _, _ in outs],
        input_output_aliases={1 + k: v for k, v in (aliases or {}).items()},
        cost_estimate=pl.CostEstimate(flops=cost[0], bytes_accessed=cost[1], transcendentals=0),
        compiler_params=pltpu.CompilerParams(vmem_limit_bytes=40 * 1024 * 1024),
    )(scalars, *[a for a, _, _ in ins])


def hop_body(s, up_act, up_sib, down_act, down_sib, cot, cot_sib, up_in, down_in, up_out, down_out):
    for k, (act, sib, src, dst) in enumerate(
        ((up_act, up_sib, up_in, up_out), (down_act, down_sib, down_in, down_out))
    ):

        @pl.when(s[2 * k] == 1)
        def _():
            dst[...] = src[...]

        @pl.when(s[2 * k] == 0)
        def _():
            part = rows_by_columns(act[...], cot[...]) + rows_by_columns(sib[...], cot_sib[...])
            dst[...] = (src[...].astype(F32) + part).astype(BF16)


def grad_body(s, cot, *refs):
    parts = (len(refs) - 1) // 2
    out = refs[-1]
    width = cot.shape[1] // parts
    for core in range(2):

        @pl.when(pl.program_id(0) == core)
        def _():
            total = None
            for j, block in enumerate(refs[core * parts : (core + 1) * parts]):
                term = lax.dot_general(
                    cot[:, j * width : (j + 1) * width],
                    block[...],
                    (((1,), (1,)), ((), ())),
                    preferred_element_type=F32,
                )
                total = term if total is None else total + term
            out[...] = total.astype(BF16)


def adam_body(first_part, s, act, sib, cot, cot_sib, up_in, down_in, w, m, v, anchor, *rest):
    outs = rest if first_part else rest[3:]
    inner, new_m, new_v = outs[:3]
    gradient = (
        rows_by_columns(act[...], cot[...])
        + rows_by_columns(sib[...], cot_sib[...])
        + up_in[...].astype(F32)
        + down_in[...].astype(F32)
    )
    first = 0.9 * m[...] + 0.1 * gradient
    second = 0.95 * v[...] + 0.05 * gradient * gradient
    update = first / CORR_ONE / (jnp.sqrt(second / CORR_TWO) + 1e-08) + 0.1 * w[...]
    stepped = w[...] - 0.1 * update
    new_m[...] = first
    new_v[...] = second
    inner[...] = stepped
    if first_part:
        for k in range(stepped.shape[1] // HEAD):

            @pl.when(s[2] == k)
            def _():
                diff = anchor[...] - stepped[:, k * HEAD : (k + 1) * HEAD]
                outs[3][...] = diff.astype(BF16)


def outer_body(s, own, one, two, three, anchor, moment, *rest):
    inner, new_anchor, new_moment = rest[3:]
    total = (own[...].astype(F32) + one[...].astype(F32)) + (
        two[...].astype(F32) + three[...].astype(F32)
    )
    average = total / 4.0
    momentum = 0.9 * moment[...] + average
    moved = anchor[...] - 0.7 * (average + 0.9 * momentum)
    new_moment[...] = momentum
    new_anchor[...] = moved
    inner[...] = moved


def line(
    activations,
    cotangent,
    inner_weights,
    first_moment,
    second_moment,
    anchor,
    outer_momentum,
    fragment,
):
    act, cot, weights = activations[0], cotangent[0], inner_weights[0]
    moment, second = first_moment[0], second_moment[0]
    tokens, width = act.shape
    rows, columns = weights.shape
    chips = lax.axis_size("fsdp") // 2
    part = columns // PARTS
    tiles = rows // TILE
    me = lax.axis_index("fsdp")
    z, core = me // 2, me % 2
    head = fragment[0]
    chunk_of = [(head * HEAD // part + j) % PARTS for j in range(PARTS)]

    up = [(i, i + 2) for i in range(2 * chips - 2)]
    down = [(i + 2, i) for i in range(2 * chips - 2)]
    swap = [(i, i ^ 1) for i in range(2 * chips)]

    def scalars(*values):
        return jnp.stack([jnp.asarray(v, jnp.int32) for v in values])

    low = [weights[:, j * part : (j + 1) * part].astype(BF16) for j in range(PARTS)]
    ups = [[lax.ppermute(x, "fsdp", up) for x in low]]
    downs = [[lax.ppermute(x, "fsdp", down) for x in low]]
    cot_sib = lax.ppermute(cot, "fsdp", swap)
    act_sib = lax.ppermute(act, "fsdp", swap)

    def act_spec(at):
        return (tokens, TILE), lambda i, s: (0, s[at] * tiles + i)

    def cot_spec(at):
        return (tokens, part), lambda i, s: (0, s[at])

    def whole_spec():
        return (TILE, part), lambda i, s: (i, 0)

    def hop(step, j):
        zd = chips - 1 - z
        d_up = jnp.clip(chips - step + z, 0, chips - 1)
        d_down = jnp.clip(step - 1 - zd, 0, chips - 1)
        s = scalars(step <= z, 2 * d_up + core, step <= zd, 2 * d_down + core, chunk_of[j])
        return call(
            hop_body,
            s,
            (tiles,),
            [
                (act, *act_spec(1)),
                (act_sib, *act_spec(1)),
                (act, *act_spec(3)),
                (act_sib, *act_spec(3)),
                (cot, *cot_spec(4)),
                (cot_sib, *cot_spec(4)),
                (ups[step - 1][j], *whole_spec()),
                (downs[step - 1][j], *whole_spec()),
            ],
            [((rows, part), BF16, *whole_spec())] * 2,
            cost=(8 * tokens * rows * part, 2 * (4 * rows * part + 4 * rows * tokens)),
        )

    def grad(buffer, blocks, block_at):
        others = [lax.ppermute(x, "fsdp", swap) for x in blocks]
        s = scalars(2 * block_at + core, 2 * block_at + 1 - core)
        ins = [(cot, (tokens, columns), lambda i, s: (0, 0))]
        ins += [(x, (rows, part), lambda i, s: (0, 0)) for x in [*blocks, *others]]
        body = grad_body
        aliases = {}
        if buffer is not None:
            aliases = {len(ins): 0}
            ins += [(buffer, None, None)]

            def body(*refs):
                grad_body(*refs[:-2], refs[-1])

        return call(
            body,
            s,
            (2,),
            ins,
            [((tokens, width), BF16, (tokens, rows), lambda i, s: (0, s[i]))],
            aliases,
            cost=(4 * tokens * rows * columns, 4 * rows * columns + 4 * tokens * rows),
        )[0]

    for step in range(1, chips):
        sent = [hop(step, j) for j in range(PARTS)]
        ups.append([lax.ppermute(x[0], "fsdp", up) for x in sent])
        downs.append([lax.ppermute(x[1], "fsdp", down) for x in sent])

    def pick(flag, a, b):
        return [jnp.where(flag, x, y) for x, y in zip(a, b)]

    last = chips - 1
    grads = grad(None, pick(z > 0, ups[0], low), jnp.maximum(z - 1, 0))
    grads = grad(grads, pick(z < last, downs[0], low), jnp.minimum(z + 1, last))
    grads = grad(grads, pick(z < 2, downs[1], ups[1]), (z + 2) % chips)
    grads = grad(
        grads,
        pick(z == 0, downs[2], pick(z == last, ups[2], low)),
        jnp.where(z == 0, last, jnp.where(z == last, 0, z)),
    )

    def own_spec(at):
        return (TILE, part), lambda i, s: (i, s[at])

    def head_spec(at):
        return (TILE, HEAD), lambda i, s: (i, s[at])

    state = None
    for j in range(PARTS):
        s = scalars(me, chunk_of[j], head % (part // HEAD), head)
        ins = [
            (act, *act_spec(0)),
            (act_sib, *act_spec(0)),
            (cot, *cot_spec(1)),
            (cot_sib, *cot_spec(1)),
            (ups[last][j], *whole_spec()),
            (downs[last][j], *whole_spec()),
            (weights, *own_spec(1)),
            (moment, *own_spec(1)),
            (second, *own_spec(1)),
            (anchor, *head_spec(3)),
        ]
        outs = [((rows, columns), F32, *own_spec(1))] * 3
        aliases = {}
        if j == 0:
            outs += [((rows, HEAD), BF16, (TILE, HEAD), lambda i, s: (i, 0))]
        else:
            aliases = {len(ins) + k: k for k in range(3)}
            ins += [(x, None, None) for x in state]
        result = call(
            functools.partial(adam_body, j == 0),
            s,
            (tiles,),
            ins,
            outs,
            aliases,
            cost=(4 * tokens * rows * part, 28 * rows * part + 4 * rows * tokens),
        )
        state = result[:3]
        if j == 0:
            diff = result[3]
            others = [
                lax.ppermute(diff, "group", [(i, i ^ k) for i in range(4)]) for k in (1, 2, 3)
            ]
    diff_spec = ((TILE, HEAD), lambda i, s: (i, 0))
    inner, new_anchor, new_momentum = call(
        outer_body,
        scalars(head),
        (tiles,),
        [(x, *diff_spec) for x in [diff, *others]]
        + [(anchor, *head_spec(0)), (outer_momentum, *head_spec(0))]
        + [(x, None, None) for x in (state[0], anchor, outer_momentum)],
        [((rows, columns), F32, *head_spec(0))] * 3,
        {6: 0, 7: 1, 8: 2},
        cost=(0, 32 * rows * HEAD),
    )
    return grads[None], inner[None], state[1][None], state[2][None], new_anchor, new_momentum


def solution(mesh):
    in_specs = (
        P("group", "fsdp", None),
        P("group", "fsdp", None),
        P("group", "fsdp", None),
        P("group", "fsdp", None),
        P("group", "fsdp", None),
        P("fsdp", None),
        P("fsdp", None),
        P(),
    )
    out_specs = (
        P("group", "fsdp", None),
        P("group", "fsdp", None),
        P("group", "fsdp", None),
        P("group", "fsdp", None),
        P("fsdp", None),
        P("fsdp", None),
    )
    short = mesh.shape["fsdp"] == 8 and mesh.shape["group"] == 4
    return jax.shard_map(
        line if short else plain,
        mesh=mesh,
        in_specs=in_specs,
        out_specs=out_specs,
        check_vma=False,
    )
```

time: 332 us -> 162 us (0.49)
  waiting for transfers between devices: 277 us -> 19.9 us
  starting transfers between devices: 0.12 us -> 53.2 us
  Pallas kernels: 0 us -> 52.5 us
  local copies, waits for them, and re-layouts: 10.3 us -> 27.1 us
  matrix products: 15.9 us -> 0 us
  between operations: 14.4 us -> 1.86 us
  other arithmetic: 13.6 us -> 6.3 us
    reduce_scatter x1 -> x0, waiting for transfers between devices: 168 us -> none  [per_device(): lax.psum_scatter(lax.dot_general(tokens_in, upstream, (((0,), (0,)), ((),...]
    all_gather x1 -> x0, waiting for transfers between devices: 72.9 us -> none  [per_device(): lax.all_gather(low_weights, 'fsdp', axis=0, tiled=True)]
    ppermute x0 -> x29, starting transfers between devices: none -> 53.2 us  [the longest x6 26.8 us: line(): ups.append([lax.ppermute(x[0], 'fsdp', up) for x in sent])]
    pallas_call x0 -> x13, Pallas kernels: none -> 52.5 us  [call(): pl.pallas_call(body, grid_spec=pltpu.PrefetchScalarGridSpec(num_scalar_pr...]
    psum x1 -> x0, waiting for transfers between devices: 36.7 us -> none  [per_device(): lax.psum((anchor_cols - local_cols).astype(jnp.bfloat16), 'group')]
    ppermute x0 -> x29, waiting for transfers between devices: none -> 19.9 us  [the longest x6 11 us: line(): downs.append([lax.ppermute(x[1], 'fsdp', down) for x in sent])]
    dot_general x2 -> x0, matrix products: 15.9 us -> none  [the longest x1 8.12 us: per_device(): lax.dot_general(tokens_in, upstream, (((0,), (0,)), ((), ())), preferred_...]
    unnamed x16 -> x74, local copies, waits for them, and re-layouts: 10.3 us -> 25.4 us
  transfers between devices with their start and end apart: 3 -> 29, of which waited for: 3 -> 4; matrix products, arithmetic and copies ran while one was open for 5% -> 7% of each run, Pallas kernels for 0% -> 31%
where the time goes in v1:
time: 162 us; the launch traced here: 161 us
  starting transfers between devices  53.2 us (33%)
  Pallas kernels  52.5 us (32%)
  local copies, waits for them, and re-layouts  27.1 us (17%)
  waiting for transfers between devices  19.9 us (12%)
  other arithmetic  6.3 us (4%)
  between operations  1.86 us (1%)
    pallas_call x13, Pallas kernels, call(): pl.pallas_call(body, grid_spec=pltpu.PrefetchScalarGridSpec(num_scalar_pr...  52.5 us
    ppermute x6, starting transfers between devices, line(): ups.append([lax.ppermute(x[0], 'fsdp', up) for x in sent])  26.8 us
    unnamed x74, local copies, waits for them, and re-layouts  25.4 us
    ppermute x6, waiting for transfers between devices, line(): downs.append([lax.ppermute(x[1], 'fsdp', down) for x in sent])  11 us
    ppermute x2, starting transfers between devices, line(): ups = [[lax.ppermute(x, 'fsdp', up) for x in low]]  9.49 us
    ppermute x6, starting transfers between devices, line(): downs.append([lax.ppermute(x[1], 'fsdp', down) for x in sent])  7.86 us
    ppermute x2, waiting for transfers between devices, line(): ups = [[lax.ppermute(x, 'fsdp', up) for x in low]]  4.45 us
    ppermute x2, waiting for transfers between devices, line(): downs = [[lax.ppermute(x, 'fsdp', down) for x in low]]  4.36 us
  transfers between devices with their start and end apart: 29, of which 4 were waited for; matrix products, arithmetic and copies ran while one was open for 7% of the time, Pallas kernels for 31%

profile of v1, /device:TPU:0, one launch (start us, length us, event | category | flops | bytes accessed | tf_op | source)
XLA Modules:
  0.0 160.8 jit_solution(12484834897644565219)
XLA Ops:
  4.1 4.9 %collective-permute-start.2 = (bf16[1024,256]{1,0:T(8,128)(2,1)}, bf16[1024,256]{1,0:T(8,128)(2,1)S(1)}, u32[]{:S(2)}, u32[]{:S(2)}) collective-permute-start(bf16[1024,256]{1,0:T(8,128)(2,1)} %get-tuple-element.57), channel_id=1, source_target_pairs={{0,2},{1,3},{2,4},{3,5},{4,6},{5,7},{8,10},{9,11},{10,12},{11,13},... | collective-permute-start | bytes 1572872 | tf_op jit(solution)/shard_map/ppermute | solution.py:199
  10.3 4.6 %collective-permute-start.8 = (bf16[1024,256]{1,0:T(8,128)(2,1)}, bf16[1024,256]{1,0:T(8,128)(2,1)S(1)}, u32[]{:S(2)}, u32[]{:S(2)}) collective-permute-start(bf16[1024,256]{1,0:T(8,128)(2,1)} %get-tuple-element.56), channel_id=1, source_target_pairs={{0,2},{1,3},{2,4},{3,5},{4,6},{5,7},{8,10},{9,11},{10,12},{11,13},... | collective-permute-start | bytes 1572872 | tf_op jit(solution)/shard_map/ppermute | solution.py:199
  17.1 4.4 %collective-permute-done.2.up_in = bf16[1024,256]{1,0:T(8,128)(2,1)S(1)} collective-permute-done((bf16[1024,256]{1,0:T(8,128)(2,1)}, bf16[1024,256]{1,0:T(8,128)(2,1)S(1)}, u32[]{:S(2)}, u32[]{:S(2)}) %collective-permute-start.2) | collective-permute-done | bytes 524320 | tf_op jit(solution)/shard_map/ppermute | solution.py:199
  21.6 4.4 %collective-permute-done.3.down_in = bf16[1024,256]{1,0:T(8,128)(2,1)S(1)} collective-permute-done((bf16[1024,256]{1,0:T(8,128)(2,1)}, bf16[1024,256]{1,0:T(8,128)(2,1)S(1)}, u32[]{:S(2)}, u32[]{:S(2)}) %collective-permute-start.3) | collective-permute-done | bytes 524320 | tf_op jit(solution)/shard_map/ppermute | solution.py:200
  28.1 4.9 %shard_map.127 = (bf16[1024,256]{1,0:T(8,128)(2,1)}, bf16[1024,256]{1,0:T(8,128)(2,1)}) custom-call(s32[5]{0:T(128)S(1)} %stack.163.s, bf16[256,8192]{1,0:T(8,128)(2,1)S(1)} %bitcast.40, bf16[256,8192]{1,0:T(8,128)(2,1)} %collective-permute-done.up_sib.down_sib.sib, bf16[256,8192]{1,0:T(8,128)(2,1)S(1)} %bitcast.41, ...), custom_call_target="tpu_custom_call" | custom-call | flops 536870912 | bytes 4194304 | tf_op jit(solution)/shard_map/pallas_call | solution.py:81
  33.0 2.9 %collective-permute-start.4 = (bf16[1024,256]{1,0:T(8,128)(2,1)}, bf16[1024,256]{1,0:T(8,128)(2,1)S(1)}, u32[]{:S(2)}, u32[]{:S(2)}) collective-permute-start(bf16[1024,256]{1,0:T(8,128)(2,1)} %get-tuple-element.28), channel_id=1, source_target_pairs={{0,2},{1,3},{2,4},{3,5},{4,6},{5,7},{8,10},{9,11},{10,12},{11,13},... | collective-permute-start | bytes 1572872 | tf_op jit(solution)/shard_map/ppermute | solution.py:262
  37.3 4.6 %shard_map.129 = (bf16[1024,256]{1,0:T(8,128)(2,1)}, bf16[1024,256]{1,0:T(8,128)(2,1)}) custom-call(s32[5]{0:T(128)S(1)} %stack.166.s, bf16[256,8192]{1,0:T(8,128)(2,1)S(1)} %bitcast.42, bf16[256,8192]{1,0:T(8,128)(2,1)} %collective-permute-done.up_sib.down_sib.sib, bf16[256,8192]{1,0:T(8,128)(2,1)S(1)} %bitcast.43, ...), custom_call_target="tpu_custom_call" | custom-call | flops 536870912 | bytes 4194304 | tf_op jit(solution)/shard_map/pallas_call | solution.py:81
  41.9 4.0 %collective-permute-start.10 = (bf16[1024,256]{1,0:T(8,128)(2,1)}, bf16[1024,256]{1,0:T(8,128)(2,1)S(1)}, u32[]{:S(2)}, u32[]{:S(2)}) collective-permute-start(bf16[1024,256]{1,0:T(8,128)(2,1)} %get-tuple-element.32), channel_id=1, source_target_pairs={{0,2},{1,3},{2,4},{3,5},{4,6},{5,7},{8,10},{9,11},{10,12},{11,13},... | collective-permute-start | bytes 1572872 | tf_op jit(solution)/shard_map/ppermute | solution.py:262
  47.5 3.7 %collective-permute-done.5.down_in = bf16[1024,256]{1,0:T(8,128)(2,1)} collective-permute-done((bf16[1024,256]{1,0:T(8,128)(2,1)}, bf16[1024,256]{1,0:T(8,128)(2,1)}, u32[]{:S(2)}, u32[]{:S(2)}) %collective-permute-start.5) | collective-permute-done | bytes 524320 | tf_op jit(solution)/shard_map/ppermute | solution.py:263
  53.4 3.8 %shard_map.128 = (bf16[1024,256]{1,0:T(8,128)(2,1)S(1)}, bf16[1024,256]{1,0:T(8,128)(2,1)S(1)}) custom-call(s32[5]{0:T(128)S(1)} %stack.156.s, bf16[256,8192]{1,0:T(8,128)(2,1)S(1)} %bitcast.44, bf16[256,8192]{1,0:T(8,128)(2,1)} %collective-permute-done.up_sib.down_sib.sib, bf16[256,8192]{1,0:T(8,128)(2,1)S(1)} %bitcast.45, ...), custom_call_target="tpu_custom_call" | custom-call | flops 536870912 | bytes 4194304 | tf_op jit(solution)/shard_map/pallas_call | solution.py:81
  58.5 4.6 %collective-permute-start.7 = (bf16[1024,256]{1,0:T(8,128)(2,1)S(1)}, bf16[1024,256]{1,0:T(8,128)(2,1)S(1)}, u32[]{:S(2)}, u32[]{:S(2)}) collective-permute-start(bf16[1024,256]{1,0:T(8,128)(2,1)S(1)} %get-tuple-element.31), channel_id=1, source_target_pairs={{0,2},{1,3},{2,4},{3,5},{4,6},{5,7},{8,10},{9,11},{10,12},{11,13},... | collective-permute-start | bytes 1572872 | tf_op jit(solution)/shard_map/ppermute | solution.py:262
  63.1 3.7 %shard_map.130 = (bf16[1024,256]{1,0:T(8,128)(2,1)S(1)}, bf16[1024,256]{1,0:T(8,128)(2,1)S(1)}) custom-call(s32[5]{0:T(128)S(1)} %stack.165.s, bf16[256,8192]{1,0:T(8,128)(2,1)S(1)} %bitcast.46, bf16[256,8192]{1,0:T(8,128)(2,1)} %collective-permute-done.up_sib.down_sib.sib, bf16[256,8192]{1,0:T(8,128)(2,1)S(1)} %bitcast.47, ...), custom_call_target="tpu_custom_call" | custom-call | flops 536870912 | bytes 4194304 | tf_op jit(solution)/shard_map/pallas_call | solution.py:81
  68.3 4.6 %collective-permute-start.13 = (bf16[1024,256]{1,0:T(8,128)(2,1)S(1)}, bf16[1024,256]{1,0:T(8,128)(2,1)S(1)}, u32[]{:S(2)}, u32[]{:S(2)}) collective-permute-start(bf16[1024,256]{1,0:T(8,128)(2,1)S(1)} %get-tuple-element.35), channel_id=1, source_target_pairs={{0,2},{1,3},{2,4},{3,5},{4,6},{5,7},{8,10},{9,11},{10,12},{11,13},... | collective-permute-start | bytes 1572872 | tf_op jit(solution)/shard_map/ppermute | solution.py:262
  75.8 7.3 %collective-permute-done.12.down_in = bf16[1024,256]{1,0:T(8,128)(2,1)S(1)} collective-permute-done((bf16[1024,256]{1,0:T(8,128)(2,1)S(1)}, bf16[1024,256]{1,0:T(8,128)(2,1)S(1)}, u32[]{:S(2)}, u32[]{:S(2)}) %collective-permute-start.12) | collective-permute-done | bytes 524320 | tf_op jit(solution)/shard_map/ppermute | solution.py:263
  90.0 4.6 %shard_map.135 = (bf16[1024,256]{1,0:T(8,128)(2,1)}, bf16[1024,256]{1,0:T(8,128)(2,1)}) custom-call(s32[5]{0:T(128)S(1)} %stack.185.s, bf16[256,8192]{1,0:T(8,128)(2,1)S(1)} %bitcast.48, bf16[256,8192]{1,0:T(8,128)(2,1)} %collective-permute-done.up_sib.down_sib.sib, bf16[256,8192]{1,0:T(8,128)(2,1)S(1)} %bitcast.49, ...), custom_call_target="tpu_custom_call" | custom-call | flops 536870912 | bytes 4194304 | tf_op jit(solution)/shard_map/pallas_call | solution.py:81
  94.6 4.9 %collective-permute-start.22 = (bf16[1024,256]{1,0:T(8,128)(2,1)}, bf16[1024,256]{1,0:T(8,128)(2,1)}, u32[]{:S(2)}, u32[]{:S(2)}) collective-permute-start(bf16[1024,256]{1,0:T(8,128)(2,1)} %get-tuple-element.36), channel_id=1, source_target_pairs={{0,2},{1,3},{2,4},{3,5},{4,6},{5,7},{8,10},{9,11},{10,12},{11,13},... | collective-permute-start | bytes 1572872 | tf_op jit(solution)/shard_map/ppermute | solution.py:262
  105.1 4.6 %shard_map.137 = (bf16[1024,256]{1,0:T(8,128)(2,1)}, bf16[1024,256]{1,0:T(8,128)(2,1)}) custom-call(s32[5]{0:T(128)S(1)} %stack.187.s, bf16[256,8192]{1,0:T(8,128)(2,1)S(1)} %bitcast.50, bf16[256,8192]{1,0:T(8,128)(2,1)} %collective-permute-done.up_sib.down_sib.sib, bf16[256,8192]{1,0:T(8,128)(2,1)S(1)} %bitcast.51, ...), custom_call_target="tpu_custom_call" | custom-call | flops 536870912 | bytes 4194304 | tf_op jit(solution)/shard_map/pallas_call | solution.py:81
  109.9 5.8 %collective-permute-start.27 = (bf16[1024,256]{1,0:T(8,128)(2,1)}, bf16[1024,256]{1,0:T(8,128)(2,1)}, u32[]{:S(2)}, u32[]{:S(2)}) collective-permute-start(bf16[1024,256]{1,0:T(8,128)(2,1)} %get-tuple-element.39), channel_id=1, source_target_pairs={{0,2},{1,3},{2,4},{3,5},{4,6},{5,7},{8,10},{9,11},{10,12},{11,13},... | collective-permute-start | bytes 1572872 | tf_op jit(solution)/shard_map/ppermute | solution.py:262
  124.9 5.6 %shard_map.136 = (f32[1024,512]{1,0:T(8,128)}, f32[1024,512]{1,0:T(8,128)}, f32[1024,512]{1,0:T(8,128)}, bf16[1024,128]{1,0:T(8,128)(2,1)S(1)}) custom-call(s32[4]{0:T(128)S(1)} %add_add_fusion.s, bf16[256,8192]{1,0:T(8,128)(2,1)S(1)} %bitcast.52, bf16[256,8192]{1,0:T(8,128)(2,1)} %collective-permute-done.up_sib.down_sib.sib, bf16[256,512]{1,0:T(8,128)(2,1)S(1)} %bitcast.61, ...), custom_call_target="tpu_custom_call" | custom-call | flops 268435456 | bytes 8388608 | tf_op jit(solution)/shard_map/pallas_call | solution.py:81
  140.0 5.4 %shard_map.138 = (f32[1024,512]{1,0:T(8,128)}, f32[1024,512]{1,0:T(8,128)}, f32[1024,512]{1,0:T(8,128)}) custom-call(s32[4]{0:T(128)S(1)} %add_add_fusion.1.s, bf16[256,8192]{1,0:T(8,128)(2,1)S(1)} %bitcast.53, bf16[256,8192]{1,0:T(8,128)(2,1)} %collective-permute-done.up_sib.down_sib.sib, ...), custom_call_target="tpu_custom_call", output_to_operand_aliasing={{0}: (11, {}), {1}: (12, {}), {2}: (13, {})} | custom-call | flops 268435456 | bytes 8388608 | tf_op jit(solution)/shard_map/pallas_call | solution.py:81
  145.4 3.7 %shard_map.131.refs_6_ = bf16[256,8192]{1,0:T(8,128)(2,1)} custom-call(s32[2]{0:T(128)S(1)} %pad_add_fusion.3.s, bf16[256,512]{1,0:T(8,128)(2,1)S(1)} %bitcast.63, bf16[1024,256]{1,0:T(8,128)(2,1)} %get-tuple-element.55.refs_0_, bf16[1024,256]{1,0:T(8,128)(2,1)S(1)} %get-tuple-element.50.refs_1_, bf16[1024,256]{1,0:T(8,128)(2,1)} %collective-permute-done.20.refs_2_, ...), custom_call_target="tpu_custom_call" | custom-call | flops 536870912 | bytes 3145728 | tf_op jit(solution)/shard_map/pallas_call | solution.py:81
  149.1 3.9 %shard_map.132.refs_6_ = bf16[256,8192]{1,0:T(8,128)(2,1)} custom-call(s32[2]{0:T(128)S(1)} %pad_add_fusion.2.refs_0_, bf16[256,512]{1,0:T(8,128)(2,1)S(1)} %bitcast.64, bf16[1024,256]{1,0:T(8,128)(2,1)} %get-tuple-element.52.refs_2_, bf16[1024,256]{1,0:T(8,128)(2,1)} %get-tuple-element.54.refs_3_, ...), custom_call_target="tpu_custom_call", output_to_operand_aliasing={{}: (6, {})} | custom-call | flops 536870912 | bytes 3145728 | tf_op jit(solution)/shard_map/pallas_call | solution.py:81
  153.0 3.5 %shard_map.133.refs_6_ = bf16[256,8192]{1,0:T(8,128)(2,1)} custom-call(s32[2]{0:T(128)S(1)} %pad_add_fusion.1.refs_0_, bf16[256,512]{1,0:T(8,128)(2,1)S(1)} %bitcast.65, bf16[1024,256]{1,0:T(8,128)(2,1)S(1)} %copy-done.18, bf16[1024,256]{1,0:T(8,128)(2,1)S(1)} %copy-done.20, ...), custom_call_target="tpu_custom_call", output_to_operand_aliasing={{}: (6, {})} | custom-call | flops 536870912 | bytes 3145728 | tf_op jit(solution)/shard_map/pallas_call | solution.py:81
  156.5 2.3 %shard_map.134 = bf16[256,8192]{1,0:T(8,128)(2,1)} custom-call(s32[2]{0:T(128)S(1)} %pad_add_fusion.refs_0_, bf16[256,512]{1,0:T(8,128)(2,1)S(1)} %bitcast.66, bf16[1024,256]{1,0:T(8,128)(2,1)S(1)} %copy-done.15, bf16[1024,256]{1,0:T(8,128)(2,1)S(1)} %copy-done.16, ...), custom_call_target="tpu_custom_call", output_to_operand_aliasing={{}: (6, {})} | custom-call | flops 536870912 | bytes 3145728 | tf_op jit(solution)/shard_map/pallas_call | solution.py:81
  (138 shorter events, 52.2 us)
Async XLA Ops:
  0.6 25.3 %collective-permute-start = (bf16[256,8192]{1,0:T(8,128)(2,1)}, bf16[256,8192]{1,0:T(8,128)(2,1)}, u32[]{:S(2)}, u32[]{:S(2)}) collective-permute-start(bf16[256,8192]{1,0:T(8,128)(2,1)} %bitcast.39), channel_id=1, source_target_pairs={{0,1},{1,0},{2,3},{3,2},{4,5},{5,4},{6,7},{7,6},{8,9},{9,8},{10,11... | collective-permute-start | bytes 12582920 | tf_op jit(solution)/shard_map/ppermute | solution.py:202
  4.1 17.5 %collective-permute-start.2 = (bf16[1024,256]{1,0:T(8,128)(2,1)}, bf16[1024,256]{1,0:T(8,128)(2,1)S(1)}, u32[]{:S(2)}, u32[]{:S(2)}) collective-permute-start(bf16[1024,256]{1,0:T(8,128)(2,1)} %get-tuple-element.57), channel_id=1, source_target_pairs={{0,2},{1,3},{2,4},{3,5},{4,6},{5,7},{8,10},{9,11},{10,12},{11,13},... | collective-permute-start | bytes 1572872 | tf_op jit(solution)/shard_map/ppermute | solution.py:199
  9.0 16.9 %collective-permute-start.3 = (bf16[1024,256]{1,0:T(8,128)(2,1)}, bf16[1024,256]{1,0:T(8,128)(2,1)S(1)}, u32[]{:S(2)}, u32[]{:S(2)}) collective-permute-start(bf16[1024,256]{1,0:T(8,128)(2,1)} %get-tuple-element.57), channel_id=1, source_target_pairs={{2,0},{3,1},{4,2},{5,3},{6,4},{7,5},{10,8},{11,9},{12,10},{13,11},... | collective-permute-start | bytes 1572872 | tf_op jit(solution)/shard_map/ppermute | solution.py:200
  10.3 26.9 %collective-permute-start.8 = (bf16[1024,256]{1,0:T(8,128)(2,1)}, bf16[1024,256]{1,0:T(8,128)(2,1)S(1)}, u32[]{:S(2)}, u32[]{:S(2)}) collective-permute-start(bf16[1024,256]{1,0:T(8,128)(2,1)} %get-tuple-element.56), channel_id=1, source_target_pairs={{0,2},{1,3},{2,4},{3,5},{4,6},{5,7},{8,10},{9,11},{10,12},{11,13},... | collective-permute-start | bytes 1572872 | tf_op jit(solution)/shard_map/ppermute | solution.py:199
  14.9 22.4 %collective-permute-start.9 = (bf16[1024,256]{1,0:T(8,128)(2,1)}, bf16[1024,256]{1,0:T(8,128)(2,1)S(1)}, u32[]{:S(2)}, u32[]{:S(2)}) collective-permute-start(bf16[1024,256]{1,0:T(8,128)(2,1)} %get-tuple-element.56), channel_id=1, source_target_pairs={{2,0},{3,1},{4,2},{5,3},{6,4},{7,5},{10,8},{11,9},{12,10},{13,11},... | collective-permute-start | bytes 1572872 | tf_op jit(solution)/shard_map/ppermute | solution.py:200
  41.9 21.2 %collective-permute-start.10 = (bf16[1024,256]{1,0:T(8,128)(2,1)}, bf16[1024,256]{1,0:T(8,128)(2,1)S(1)}, u32[]{:S(2)}, u32[]{:S(2)}) collective-permute-start(bf16[1024,256]{1,0:T(8,128)(2,1)} %get-tuple-element.32), channel_id=1, source_target_pairs={{0,2},{1,3},{2,4},{3,5},{4,6},{5,7},{8,10},{9,11},{10,12},{11,13},... | collective-permute-start | bytes 1572872 | tf_op jit(solution)/shard_map/ppermute | solution.py:262
  46.0 17.1 %collective-permute-start.11 = (bf16[1024,256]{1,0:T(8,128)(2,1)}, bf16[1024,256]{1,0:T(8,128)(2,1)S(1)}, u32[]{:S(2)}, u32[]{:S(2)}) collective-permute-start(bf16[1024,256]{1,0:T(8,128)(2,1)} %get-tuple-element.33), channel_id=1, source_target_pairs={{2,0},{3,1},{4,2},{5,3},{6,4},{7,5},{10,8},{11,9},{12,10},{13,11},... | collective-permute-start | bytes 1572872 | tf_op jit(solution)/shard_map/ppermute | solution.py:263
  57.2 18.1 %collective-permute-start.6 = (bf16[1024,256]{1,0:T(8,128)(2,1)S(1)}, bf16[1024,256]{1,0:T(8,128)(2,1)S(1)}, u32[]{:S(2)}, u32[]{:S(2)}) collective-permute-start(bf16[1024,256]{1,0:T(8,128)(2,1)S(1)} %get-tuple-element.30), channel_id=1, source_target_pairs={{2,0},{3,1},{4,2},{5,3},{6,4},{7,5},{10,8},{11,9},{12,10},{13,11},... | collective-permute-start | bytes 1572872 | tf_op jit(solution)/shard_map/ppermute | solution.py:263
  58.5 17.3 %collective-permute-start.7 = (bf16[1024,256]{1,0:T(8,128)(2,1)S(1)}, bf16[1024,256]{1,0:T(8,128)(2,1)S(1)}, u32[]{:S(2)}, u32[]{:S(2)}) collective-permute-start(bf16[1024,256]{1,0:T(8,128)(2,1)S(1)} %get-tuple-element.31), channel_id=1, source_target_pairs={{0,2},{1,3},{2,4},{3,5},{4,6},{5,7},{8,10},{9,11},{10,12},{11,13},... | collective-permute-start | bytes 1572872 | tf_op jit(solution)/shard_map/ppermute | solution.py:262
  74.0 20.6 %collective-permute-start.16 = (bf16[1024,256]{1,0:T(8,128)(2,1)S(1)}, bf16[1024,256]{1,0:T(8,128)(2,1)}, u32[]{:S(2)}, u32[]{:S(2)}) collective-permute-start(bf16[1024,256]{1,0:T(8,128)(2,1)S(1)} %broadcast_select_fusion.5.refs_2_), channel_id=1, source_target_pairs={{0,1},{1,0},{2,3},{3,2},{4,5},{5,4},{6,7},{7,6},{8,9},{9,8},{10,11... | collective-permute-start | bytes 1572872 | tf_op jit(solution)/shard_map/ppermute | solution.py:237
  75.3 24.1 %collective-permute-start.17 = (bf16[1024,256]{1,0:T(8,128)(2,1)S(1)}, bf16[1024,256]{1,0:T(8,128)(2,1)}, u32[]{:S(2)}, u32[]{:S(2)}) collective-permute-start(bf16[1024,256]{1,0:T(8,128)(2,1)S(1)} %broadcast_select_fusion.4.refs_3_), channel_id=1, source_target_pairs={{0,1},{1,0},{2,3},{3,2},{4,5},{5,4},{6,7},{7,6},{8,9},{9,8},{10,11... | collective-permute-start | bytes 1572872 | tf_op jit(solution)/shard_map/ppermute | solution.py:237
  85.0 24.7 %collective-permute-start.18 = (bf16[1024,256]{1,0:T(8,128)(2,1)}, bf16[1024,256]{1,0:T(8,128)(2,1)}, u32[]{:S(2)}, u32[]{:S(2)}) collective-permute-start(bf16[1024,256]{1,0:T(8,128)(2,1)} %get-tuple-element.52.refs_2_), channel_id=1, source_target_pairs={{0,1},{1,0},{2,3},{3,2},{4,5},{5,4},{6,7},{7,6},{8,9},{9,8},{10,11... | collective-permute-start | bytes 1572872 | tf_op jit(solution)/shard_map/ppermute | solution.py:237
  85.0 24.9 %collective-permute-start.19 = (bf16[1024,256]{1,0:T(8,128)(2,1)}, bf16[1024,256]{1,0:T(8,128)(2,1)}, u32[]{:S(2)}, u32[]{:S(2)}) collective-permute-start(bf16[1024,256]{1,0:T(8,128)(2,1)} %get-tuple-element.54.refs_3_), channel_id=1, source_target_pairs={{0,1},{1,0},{2,3},{3,2},{4,5},{5,4},{6,7},{7,6},{8,9},{9,8},{10,11... | collective-permute-start | bytes 1572872 | tf_op jit(solution)/shard_map/ppermute | solution.py:237
  85.5 30.2 %collective-permute-start.20 = (bf16[1024,256]{1,0:T(8,128)(2,1)}, bf16[1024,256]{1,0:T(8,128)(2,1)}, u32[]{:S(2)}, u32[]{:S(2)}) collective-permute-start(bf16[1024,256]{1,0:T(8,128)(2,1)} %get-tuple-element.55.refs_0_), channel_id=1, source_target_pairs={{0,1},{1,0},{2,3},{3,2},{4,5},{5,4},{6,7},{7,6},{8,9},{9,8},{10,11... | collective-permute-start | bytes 1572872 | tf_op jit(solution)/shard_map/ppermute | solution.py:237
  94.6 22.7 %collective-permute-start.22 = (bf16[1024,256]{1,0:T(8,128)(2,1)}, bf16[1024,256]{1,0:T(8,128)(2,1)}, u32[]{:S(2)}, u32[]{:S(2)}) collective-permute-start(bf16[1024,256]{1,0:T(8,128)(2,1)} %get-tuple-element.36), channel_id=1, source_target_pairs={{0,2},{1,3},{2,4},{3,5},{4,6},{5,7},{8,10},{9,11},{10,12},{11,13},... | collective-permute-start | bytes 1572872 | tf_op jit(solution)/shard_map/ppermute | solution.py:262
  99.4 18.1 %collective-permute-start.23 = (bf16[1024,256]{1,0:T(8,128)(2,1)}, bf16[1024,256]{1,0:T(8,128)(2,1)}, u32[]{:S(2)}, u32[]{:S(2)}) collective-permute-start(bf16[1024,256]{1,0:T(8,128)(2,1)} %get-tuple-element.37), channel_id=1, source_target_pairs={{2,0},{3,1},{4,2},{5,3},{6,4},{7,5},{10,8},{11,9},{12,10},{13,11},... | collective-permute-start | bytes 1572872 | tf_op jit(solution)/shard_map/ppermute | solution.py:263
  109.7 20.8 %collective-permute-start.21 = (bf16[1024,256]{1,0:T(8,128)(2,1)S(1)}, bf16[1024,256]{1,0:T(8,128)(2,1)}, u32[]{:S(2)}, u32[]{:S(2)}) collective-permute-start(bf16[1024,256]{1,0:T(8,128)(2,1)S(1)} %get-tuple-element.50.refs_1_), channel_id=1, source_target_pairs={{0,1},{1,0},{2,3},{3,2},{4,5},{5,4},{6,7},{7,6},{8,9},{9,8},{10,11... | collective-permute-start | bytes 1572872 | tf_op jit(solution)/shard_map/ppermute | solution.py:237
  109.9 22.1 %collective-permute-start.27 = (bf16[1024,256]{1,0:T(8,128)(2,1)}, bf16[1024,256]{1,0:T(8,128)(2,1)}, u32[]{:S(2)}, u32[]{:S(2)}) collective-permute-start(bf16[1024,256]{1,0:T(8,128)(2,1)} %get-tuple-element.39), channel_id=1, source_target_pairs={{0,2},{1,3},{2,4},{3,5},{4,6},{5,7},{8,10},{9,11},{10,12},{11,13},... | collective-permute-start | bytes 1572872 | tf_op jit(solution)/shard_map/ppermute | solution.py:262
  115.7 17.8 %collective-permute-start.28 = (bf16[1024,256]{1,0:T(8,128)(2,1)}, bf16[1024,256]{1,0:T(8,128)(2,1)}, u32[]{:S(2)}, u32[]{:S(2)}) collective-permute-start(bf16[1024,256]{1,0:T(8,128)(2,1)} %get-tuple-element.40), channel_id=1, source_target_pairs={{2,0},{3,1},{4,2},{5,3},{6,4},{7,5},{10,8},{11,9},{12,10},{13,11},... | collective-permute-start | bytes 1572872 | tf_op jit(solution)/shard_map/ppermute | solution.py:263
  117.3 39.2 %collective-permute-start.14 = (bf16[1024,256]{1,0:T(8,128)(2,1)}, bf16[1024,256]{1,0:T(8,128)(2,1)S(1)}, u32[]{:S(2)}, u32[]{:S(2)}) collective-permute-start(bf16[1024,256]{1,0:T(8,128)(2,1)} %get-tuple-element.51.refs_2_), channel_id=1, source_target_pairs={{0,1},{1,0},{2,3},{3,2},{4,5},{5,4},{6,7},{7,6},{8,9},{9,8},{10,11... | collective-permute-start | bytes 1572872 | tf_op jit(solution)/shard_map/ppermute | solution.py:237
  117.5 39.0 %collective-permute-start.15 = (bf16[1024,256]{1,0:T(8,128)(2,1)}, bf16[1024,256]{1,0:T(8,128)(2,1)S(1)}, u32[]{:S(2)}, u32[]{:S(2)}) collective-permute-start(bf16[1024,256]{1,0:T(8,128)(2,1)} %get-tuple-element.53.refs_3_), channel_id=1, source_target_pairs={{0,1},{1,0},{2,3},{3,2},{4,5},{5,4},{6,7},{7,6},{8,9},{9,8},{10,11... | collective-permute-start | bytes 1572872 | tf_op jit(solution)/shard_map/ppermute | solution.py:237
  130.5 28.4 %collective-permute-start.24 = (bf16[1024,128]{1,0:T(8,128)(2,1)S(1)}, bf16[1024,128]{1,0:T(8,128)(2,1)S(1)}, u32[]{:S(2)}, u32[]{:S(2)}) collective-permute-start(bf16[1024,128]{1,0:T(8,128)(2,1)S(1)} %get-tuple-element.38.own), channel_id=1, source_target_pairs={{0,8},{8,0},{16,24},{24,16},{1,9},{9,1},{17,25},{25,17},{2,10},{10... | collective-permute-start | bytes 786440 | tf_op jit(solution)/shard_map/ppermute | solution.py:319
  132.0 26.9 %collective-permute-start.25 = (bf16[1024,128]{1,0:T(8,128)(2,1)S(1)}, bf16[1024,128]{1,0:T(8,128)(2,1)S(1)}, u32[]{:S(2)}, u32[]{:S(2)}) collective-permute-start(bf16[1024,128]{1,0:T(8,128)(2,1)S(1)} %get-tuple-element.38.own), channel_id=1, source_target_pairs={{0,16},{8,24},{16,0},{24,8},{1,17},{9,25},{17,1},{25,9},{2,18},{10... | collective-permute-start | bytes 786440 | tf_op jit(solution)/shard_map/ppermute | solution.py:319
  133.5 25.3 %collective-permute-start.26 = (bf16[1024,128]{1,0:T(8,128)(2,1)S(1)}, bf16[1024,128]{1,0:T(8,128)(2,1)S(1)}, u32[]{:S(2)}, u32[]{:S(2)}) collective-permute-start(bf16[1024,128]{1,0:T(8,128)(2,1)S(1)} %get-tuple-element.38.own), channel_id=1, source_target_pairs={{0,24},{8,16},{16,8},{24,0},{1,25},{9,17},{17,9},{25,1},{2,26},{10... | collective-permute-start | bytes 786440 | tf_op jit(solution)/shard_map/ppermute | solution.py:319
  (41 other events, 284.4 us)

commit v2 on v0

v2 whole, which is shorter than its diff:
```python
import functools

import jax
import jax.numpy as jnp
from jax import lax
from jax.experimental import pallas as pl
from jax.experimental.pallas import tpu as pltpu
from jax.sharding import PartitionSpec as P

HEAD = 128
STEP = 100
CORR_ONE = 1.0 - 0.9**STEP
CORR_TWO = 1.0 - 0.95**STEP
PARTS = ((0, 256), (256, 256))
TILE = 256
BF16 = jnp.bfloat16
F32 = jnp.float32


def plain(
    activations,
    cotangent,
    inner_weights,
    first_moment,
    second_moment,
    anchor,
    outer_momentum,
    fragment,
):
    tokens_in = activations[0]
    upstream = cotangent[0]
    weights = inner_weights[0]
    low_weights = weights.astype(BF16)
    input_grad = lax.dot_general(
        upstream,
        lax.all_gather(low_weights, "fsdp", axis=0, tiled=True),
        (((1,), (1,)), ((), ())),
        preferred_element_type=F32,
    ).astype(BF16)
    gradient = lax.psum_scatter(
        lax.dot_general(tokens_in, upstream, (((0,), (0,)), ((), ())), preferred_element_type=F32),
        "fsdp",
        scatter_dimension=0,
        tiled=True,
    )
    new_first = 0.9 * first_moment[0] + 0.1 * gradient
    new_second = 0.95 * second_moment[0] + 0.05 * gradient * gradient
    update = new_first / CORR_ONE / (jnp.sqrt(new_second / CORR_TWO) + 1e-08) + 0.1 * weights
    stepped = weights - 0.1 * update
    offset = fragment[0] * HEAD
    local_cols = lax.dynamic_slice_in_dim(stepped, offset, HEAD, 1)
    anchor_cols = lax.dynamic_slice_in_dim(anchor, offset, HEAD, 1)
    moment_cols = lax.dynamic_slice_in_dim(outer_momentum, offset, HEAD, 1)
    summed = lax.psum((anchor_cols - local_cols).astype(BF16), "group").astype(F32)
    average = summed / lax.axis_size("group")
    moment_new = 0.9 * moment_cols + average
    anchor_next = anchor_cols - 0.7 * (average + 0.9 * moment_new)
    new_momentum = lax.dynamic_update_slice_in_dim(outer_momentum, moment_new, offset, 1)
    new_anchor = lax.dynamic_update_slice_in_dim(anchor, anchor_next, offset, 1)
    new_inner = lax.dynamic_update_slice_in_dim(stepped, anchor_next, offset, 1)
    return (
        input_grad[None],
        new_inner[None],
        new_first[None],
        new_second[None],
        new_anchor,
        new_momentum,
    )


def rows_by_columns(act, cot):
    return lax.dot_general(act, cot, (((0,), (0,)), ((), ())), preferred_element_type=F32)


def vmem(*shape, dtype=F32):
    return pltpu.VMEM(shape, dtype)


def hbm(*shape, dtype=F32):
    return jax.ShapeDtypeStruct(shape, dtype)


class Held:
    def __init__(self, array):
        self.array = array


def call(body, scalars, ins, outs, scratch=(), aliases=None, after=(), us=1.0):
    arrays, specs = [scalars], [pl.BlockSpec(memory_space=pltpu.SMEM)]
    for x in ins:
        if isinstance(x, Held):
            arrays.append(pltpu.with_memory_space_constraint(x.array, pltpu.VMEM))
            specs.append(pl.BlockSpec(memory_space=pltpu.VMEM))
        else:
            arrays.append(pltpu.with_memory_space_constraint(x, pltpu.HBM))
            specs.append(pl.BlockSpec(memory_space=pltpu.HBM))
    first = len(arrays)
    arrays += [pltpu.with_memory_space_constraint(x, pltpu.VMEM) for x in after]
    specs += [pl.BlockSpec(memory_space=pltpu.VMEM)] * len(after)

    def inner(*refs):
        body(*refs[:first], *refs[first + len(after) :])

    return pl.pallas_call(
        inner,
        in_specs=specs,
        out_specs=[
            pl.BlockSpec(memory_space=pl.ANY if isinstance(o, jax.ShapeDtypeStruct) else pltpu.VMEM)
            for o in outs
        ],
        out_shape=list(outs),
        scratch_shapes=list(scratch),
        input_output_aliases={1 + k: v for k, v in (aliases or {}).items()},
        cost_estimate=pl.CostEstimate(
            flops=0, bytes_accessed=int(us * 3.4e6), transcendentals=0
        ),
        compiler_params=pltpu.CompilerParams(vmem_limit_bytes=12 * 1024 * 1024),
    )(*arrays)


def columns_of(ref, block, width):
    return ref.at[:, pl.ds(pl.multiple_of(block * width, width), width)]


def start(src, dst, sem):
    copy = pltpu.make_async_copy(src, dst, sem)
    copy.start()
    return copy


def turned(at, s, src, dst, sems, base, first=0):
    return [
        start(
            columns_of(src, s[at["heads"] + k], HEAD),
            dst.at[:, pl.ds(first + k * HEAD, HEAD)],
            sems.at[base + k],
        )
        for k in range(src.shape[1] // HEAD)
    ]


def ready_body(at, s, w, act, cot, *rest):
    *lows, w_v, packed, sems = rest
    rows = w.shape[0]
    step = rows // 4
    heads = w.shape[1] // HEAD
    wide = packed.shape[1] - cot.shape[1]
    first = [
        turned(
            at, s, w.at[pl.ds(i * step, step)], w_v.at[pl.ds(i * step, step)], sems, i * heads
        )
        for i in range(4)
    ]
    copies = [
        start(
            columns_of(act, 2 * d + 1 - s[at["core"]], rows),
            packed.at[:, pl.ds(d * rows, rows)],
            sems.at[4 * heads + d],
        )
        for d in range(wide // rows)
    ]
    copies += turned(at, s, cot, packed, sems, 4 * heads + len(copies), wide)
    for i in range(4):
        for copy in first[i]:
            copy.wait()
        here = pl.ds(i * step, step)
        for (offset, part), low in zip(PARTS, lows):
            low[here, :] = w_v[here, offset : offset + part].astype(BF16)
    for copy in copies:
        copy.wait()


def own_body(at, s, packed, act, anchor, moment, *rest):
    sums_ref, anchor_out, moment_out, act_s, held, sems = rest
    chips, _, rows = act_s.shape
    blocks = [
        start(columns_of(act, 2 * d + s[at["core"]], rows), act_s.at[d], sems.at[d])
        for d in range(chips)
    ]
    loads = [
        start(src, held.at[k], sems.at[chips + k]) for k, src in enumerate((anchor, moment))
    ]
    stores = []
    for d in range(chips):
        blocks[d].wait()
        for i in range(rows // TILE):
            sums_ref[pl.ds(d * rows + i * TILE, TILE), :] = rows_by_columns(
                act_s[d, :, i * TILE : (i + 1) * TILE], packed[:, chips * rows :]
            )
        if d == 1:
            for k, dst in enumerate((anchor_out, moment_out)):
                loads[k].wait()
                stores.append(start(held.at[k], dst, sems.at[chips + 2 + k]))
    for copy in stores:
        copy.wait()


def sibling_body(at, s, before, packed, m, v, anchor, moment, *rest):
    sums_ref, m_v, v_v, anchor_v, moment_v, sems = rest
    copies = []
    for src, dst in ((m, m_v), (v, v_v)):
        copies += turned(at, s, src, dst, sems, len(copies))
    for src, dst in ((anchor, anchor_v), (moment, moment_v)):
        copies.append(start(columns_of(src, s[at["heads"]], HEAD), dst, sems.at[len(copies)]))
    wide = sums_ref.shape[0]
    for i in range(wide // TILE):
        here = slice(i * TILE, (i + 1) * TILE)
        sums_ref[here, :] = before[here, :] + rows_by_columns(packed[:, here], packed[:, wide:])
    for copy in copies:
        copy.wait()


def hop_body(at, step, offset, s, sums_ref, from_o, from_e, *rest):
    to_e, to_o, picked = rest[-3:]
    older = rest[0] if step == 3 else None
    rows, part = to_e.shape
    columns = slice(offset, offset + part)
    base = at["hop"] + 4 * (step - 1)
    size = 64

    def each(body):
        @pl.loop(0, rows // size, unroll=4)
        def _(i):
            body(pl.multiple_of(i * size, size))

    for mode, block, src, dst in (
        (s[base], s[base + 1], from_o, to_e),
        (s[base + 2], s[base + 3], from_e, to_o),
    ):
        first = pl.multiple_of(block * rows, rows)

        @pl.when(mode == 0)
        def _():
            def body(r):
                dst[pl.ds(r, size), :] = sums_ref[pl.ds(first + r, size), columns].astype(BF16)

            each(body)

        @pl.when(mode == 1)
        def _():
            def body(r):
                here = pl.ds(r, size)
                added = src[here, :].astype(F32) + sums_ref[pl.ds(first + r, size), columns]
                dst[here, :] = added.astype(BF16)

            each(body)

        @pl.when(mode == 2)
        def _():
            def body(r):
                dst[pl.ds(r, size), :] = src[pl.ds(r, size), :]

            each(body)

    def keep(src):
        def body(r):
            picked[pl.ds(r, size), :] = src[pl.ds(r, size), :]

        each(body)

    if step == 1:
        keep(from_e)
    else:

        @pl.when(s[at["middle"]] == 1)
        def _():
            keep(from_o if older is None else older)

        @pl.when(s[at["middle"]] == 0)
        def _():
            keep(from_e)


def grad_body(at, which, s, packed, packed_sib, *rest):
    theirs, out, token, stage, sems = rest[-5:]
    rows = stage.shape[1]
    wide = packed.shape[1] - sum(part for _, part in PARTS)
    copies = []
    if which > 0:
        copies.append(
            start(
                rest[len(PARTS)], columns_of(out, s[at["grad"] + 2 * which - 1], rows), sems.at[1]
            )
        )
    for cot, dst in ((packed_sib, theirs), (packed, stage)):
        for i in range(rows // TILE):
            here = slice(i * TILE, (i + 1) * TILE)
            total = None
            for (offset, part), block in zip(PARTS, rest):
                term = lax.dot_general(
                    cot[:, wide + offset : wide + offset + part],
                    block[here, :],
                    (((1,), (1,)), ((), ())),
                    preferred_element_type=F32,
                )
                total = term if total is None else total + term
            dst[:, here] = total.astype(BF16)
    copies.append(start(stage, columns_of(out, s[at["grad"] + 2 * which], rows), sems.at[0]))
    token[...] = jnp.zeros_like(token)
    for copy in copies:
        copy.wait()


def adam_body(at, offset, s, sums_ref, from_e, from_o, w, m, v, *rest):
    stage, sems = rest[-2:]
    rows, part = from_e.shape
    if offset == 0:
        anchor, diff = rest[0], rest[4]
        outs = rest[1:4]
    else:
        outs = rest[3:6]
    columns = slice(offset, offset + part)
    size = 64 * 256 // part // 16 * 16
    base = pl.multiple_of(s[at["z"]] * rows, rows)
    copies = []
    for tile in range(rows // TILE):

        @pl.loop(0, TILE // size)
        def _(i):
            r = pl.multiple_of(tile * TILE + i * size, size)
            here = pl.ds(r, size)
            one = sums_ref[pl.ds(base + r, size), columns] + from_e[here, :].astype(F32)
            gradient = jnp.where(s[at["middle"]] == 1, one + from_o[here, :].astype(F32), one)
            weights = w[here, columns]
            first = 0.9 * m[here, columns] + 0.1 * gradient
            second = 0.95 * v[here, columns] + 0.05 * gradient * gradient
            update = first / CORR_ONE / (jnp.sqrt(second / CORR_TWO) + 1e-08) + 0.1 * weights
            stepped = weights - 0.1 * update
            stage[0, here, :] = stepped
            stage[1, here, :] = first
            stage[2, here, :] = second
            if offset == 0:
                diff[here, :] = (anchor[here, :] - stepped[:, :HEAD]).astype(BF16)

        there = pl.ds(tile * TILE, TILE)
        for k, out in enumerate(outs):
            for h in range(part // HEAD):
                copies.append(
                    start(
                        stage.at[k, there, pl.ds(h * HEAD, HEAD)],
                        columns_of(out.at[there], s[at["heads"] + offset // HEAD + h], HEAD),
                        sems.at[len(copies)],
                    )
                )
    for copy in copies:
        copy.wait()


def outer_body(at, s, own, one, two, three, anchor, moment, theirs, *rest):
    inner, new_anchor, new_moment, grads, stage, sems = rest[4:]
    rows = theirs.shape[1]
    copies = [start(theirs, columns_of(grads, s[at["grad"] + 7], rows), sems.at[3])]
    total = (own[...].astype(F32) + one[...].astype(F32)) + (
        two[...].astype(F32) + three[...].astype(F32)
    )
    average = total / 4.0
    momentum = 0.9 * moment[...] + average
    stage[0] = momentum
    stage[1] = anchor[...] - 0.7 * (average + 0.9 * momentum)
    copies += [
        start(stage.at[k], columns_of(out, s[at["heads"]], HEAD), sems.at[i])
        for i, (k, out) in enumerate(((0, new_moment), (1, new_anchor), (1, inner)))
    ]
    for copy in copies:
        copy.wait()


def line(
    activations,
    cotangent,
    inner_weights,
    first_moment,
    second_moment,
    anchor,
    outer_momentum,
    fragment,
):
    act, cot, weights = activations[0], cotangent[0], inner_weights[0]
    moment, second = first_moment[0], second_moment[0]
    tokens, width = act.shape
    rows, columns = weights.shape
    chips = lax.axis_size("fsdp") // 2
    me = lax.axis_index("fsdp")
    z, core = me // 2, me % 2
    head = fragment[0]
    last = chips - 1
    middle = (z > 0) & (z < last)
    even = z % 2 == 0
    zd = last - z

    def cross(i):
        return i ^ 1 if i // 2 in (0, last) else (i + 2 if i // 2 % 2 else i - 2)

    e_perm = [(i, i ^ 2) for i in range(2 * chips)]
    o_perm = [(i, cross(i)) for i in range(2 * chips)]
    swap = [(i, i ^ 1) for i in range(2 * chips)]

    values, at = [], {}

    def name(key, *numbers):
        at[key] = len(values)
        values.extend(jnp.asarray(v, jnp.int32) for v in numbers)

    name("z", z)
    name("core", core)
    name("middle", middle)
    name("heads", *[(head + k) % (columns // HEAD) for k in range(columns // HEAD)])
    name("grad", *[2 * (z ^ k) + c for k in range(chips) for c in (core, 1 - core)])
    hops = []
    for step in range(1, chips):
        up_mode = jnp.where(step <= z, 2, jnp.where(z == 0, 0, 1))
        down_mode = jnp.where(step <= zd, 2, jnp.where(zd == 0, 0, 1))
        up_to = jnp.clip(chips - step + z, 0, last)
        down_to = jnp.clip(step - 1 - zd, 0, last)
        hops += [
            jnp.where(even, up_mode, down_mode),
            jnp.where(even, up_to, down_to),
            jnp.where(middle, jnp.where(even, down_mode, up_mode), 2),
            jnp.where(even, down_to, up_to),
        ]
    name("hop", *hops)
    s = jnp.stack(values)

    def permute(x, perm, axis="fsdp"):
        return lax.ppermute(x, axis, perm)

    dma = pltpu.SemaphoreType.DMA
    from_e, from_o = [[]], [[]]
    heads = columns // HEAD
    *low, w_v, packed = call(
        functools.partial(ready_body, at),
        s,
        [weights, act, cot],
        [vmem(rows, part, dtype=BF16) for _, part in PARTS]
        + [vmem(rows, columns), vmem(tokens, chips * rows + columns, dtype=BF16)],
        [dma((5 * heads + chips,))],
        us=3.0,
    )
    for x in low:
        from_e[0].append(permute(x, e_perm))
        from_o[0].append(permute(x, o_perm))
    packed_sib = permute(packed, swap)

    sums_shape = vmem(chips * rows, columns)
    sums_own, new_anchor, new_momentum = call(
        functools.partial(own_body, at),
        s,
        [Held(packed), act, anchor, outer_momentum],
        [sums_shape, hbm(rows, columns), hbm(rows, columns)],
        [vmem(chips, tokens, rows, dtype=BF16), vmem(2, rows, columns), dma((chips + 4,))],
        us=5.0,
    )
    sums_both, m_v, v_v, anchor_v, moment_v = call(
        functools.partial(sibling_body, at),
        s,
        [Held(sums_own), Held(packed_sib), moment, second, anchor, outer_momentum],
        [sums_shape] + [vmem(rows, columns)] * 2 + [vmem(rows, HEAD)] * 2,
        [dma((2 * heads + 2,))],
        {0: 0},
        us=5.0,
    )

    def hop(step, j, after):
        offset, part = PARTS[j]
        ins = [Held(sums_both), Held(from_o[step - 1][j]), Held(from_e[step - 1][j])]
        if step == 3:
            ins += [Held(from_o[0][j])]
        return call(
            functools.partial(hop_body, at, step, offset),
            s,
            ins,
            [vmem(rows, part, dtype=BF16)] * 3,
            after=after,
        )

    def grad(which, before, own, after):
        ins = [Held(x) for x in [packed, packed_sib, *own]]
        aliases = {}
        if before is not None:
            theirs, buffer = before
            ins += [Held(theirs)]
            aliases = {len(ins): 1}
            ins += [buffer]
        theirs, buffer, token = call(
            functools.partial(grad_body, at, which),
            s,
            ins,
            [
                vmem(tokens, rows, dtype=BF16),
                hbm(tokens, width, dtype=BF16),
                vmem(8, 128),
            ],
            [vmem(tokens, rows, dtype=BF16), dma((2,))],
            aliases,
            after,
            us=2.1,
        )
        return (permute(theirs, swap), buffer), token

    grads, after, picked = None, (), low
    for step in range(1, chips):
        from_e.append([])
        from_o.append([])
        found = []
        for j in range(len(PARTS)):
            to_e, to_o, pick = hop(step, j, after)
            from_e[step].append(permute(to_e, e_perm))
            from_o[step].append(permute(to_o, o_perm))
            found.append(pick)
            after = ()
            if j == 0:
                grads, token = grad(step - 1, grads, picked, (to_e,))
                after = (token,)
        picked = found
    grads, token = grad(last, grads, picked, ())

    state, diff, others = None, None, None
    for j, (offset, part) in enumerate(PARTS):
        ins = [sums_both, from_e[last][j], from_o[last][j], w_v, m_v, v_v]
        outs = [hbm(rows, columns)] * 3
        aliases, after = {}, ()
        if j == 0:
            ins += [anchor_v]
            outs = outs + [vmem(rows, HEAD, dtype=BF16)]
            after = (token,)
        ins = [Held(x) for x in ins]
        if j > 0:
            aliases = {len(ins) + k: k for k in range(3)}
            ins += state
        result = call(
            functools.partial(adam_body, at, offset),
            s,
            ins,
            outs,
            [vmem(3, rows, part), dma((3 * rows // TILE * part // HEAD,))],
            aliases,
            after,
            us=2.8,
        )
        state = list(result[:3])
        if j == 0:
            diff = result[3]
            others = [permute(diff, [(i, i ^ k) for i in range(4)], "group") for k in (1, 2, 3)]
    inner, new_anchor, new_momentum, input_grad = call(
        functools.partial(outer_body, at),
        s,
        [Held(x) for x in [diff, *others, anchor_v, moment_v, grads[0]]]
        + [state[0], new_anchor, new_momentum, grads[1]],
        [hbm(rows, columns)] * 3 + [hbm(tokens, width, dtype=BF16)],
        [vmem(2, rows, HEAD), dma((4,))],
        {7: 0, 8: 1, 9: 2, 10: 3},
        us=2.0,
    )
    return input_grad[None], inner[None], state[1][None], state[2][None], new_anchor, new_momentum


def solution(mesh):
    in_specs = (
        P("group", "fsdp", None),
        P("group", "fsdp", None),
        P("group", "fsdp", None),
        P("group", "fsdp", None),
        P("group", "fsdp", None),
        P("fsdp", None),
        P("fsdp", None),
        P(),
    )
    out_specs = (
        P("group", "fsdp", None),
        P("group", "fsdp", None),
        P("group", "fsdp", None),
        P("group", "fsdp", None),
        P("fsdp", None),
        P("fsdp", None),
    )
    short = mesh.shape["fsdp"] == 8 and mesh.shape["group"] == 4
    return jax.shard_map(
        line if short else plain,
        mesh=mesh,
        in_specs=in_specs,
        out_specs=out_specs,
        check_vma=False,
    )
```

time: 332 us -> 111 us (0.33)
  waiting for transfers between devices: 277 us -> 49.6 us
  Pallas kernels: 0 us -> 33.6 us
  starting transfers between devices: 0.12 us -> 25.9 us
  matrix products: 15.9 us -> 0 us
  other arithmetic: 13.6 us -> 0 us
  between operations: 14.4 us -> 1.71 us
  local copies, waits for them, and re-layouts: 10.3 us -> 0.12 us
    reduce_scatter x1 -> x0, waiting for transfers between devices: 168 us -> none  [per_device(): lax.psum_scatter(lax.dot_general(tokens_in, upstream, (((0,), (0,)), ((),...]
    all_gather x1 -> x0, waiting for transfers between devices: 72.9 us -> none  [per_device(): lax.all_gather(low_weights, 'fsdp', axis=0, tiled=True)]
    ppermute x0 -> x24, waiting for transfers between devices: none -> 49.6 us  [permute(): return lax.ppermute(x, axis, perm)]
    psum x1 -> x0, waiting for transfers between devices: 36.7 us -> none  [per_device(): lax.psum((anchor_cols - local_cols).astype(jnp.bfloat16), 'group')]
    pallas_call x0 -> x16, Pallas kernels: none -> 33.6 us  [call(): pl.pallas_call(inner, in_specs=specs, out_specs=[pl.BlockSpec(memory_spac...]
    ppermute x0 -> x24, starting transfers between devices: none -> 25.9 us  [permute(): return lax.ppermute(x, axis, perm)]
    dot_general x2 -> x0, matrix products: 15.9 us -> none  [the longest x1 8.12 us: per_device(): lax.dot_general(tokens_in, upstream, (((0,), (0,)), ((), ())), preferred_...]
    unnamed x16 -> x0, local copies, waits for them, and re-layouts: 10.3 us -> none
  transfers between devices with their start and end apart: 3 -> 24, of which waited for: 3 -> 9; matrix products, arithmetic and copies ran while one was open for 5% -> 0% of each run, Pallas kernels for 0% -> 26%
where the time goes in v2:
time: 111 us
  waiting for transfers between devices  49.6 us (45%)
  Pallas kernels  33.6 us (30%)
  starting transfers between devices  25.9 us (23%)
  between operations  1.71 us (2%)
    ppermute x24, waiting for transfers between devices, permute(): return lax.ppermute(x, axis, perm)  49.6 us
    pallas_call x16, Pallas kernels, call(): pl.pallas_call(inner, in_specs=specs, out_specs=[pl.BlockSpec(memory_spac...  33.6 us
    ppermute x24, starting transfers between devices, permute(): return lax.ppermute(x, axis, perm)  25.9 us
  transfers between devices with their start and end apart: 24, of which 9 were waited for; matrix products, arithmetic and copies ran while one was open for 0% of the time, Pallas kernels for 26%

profile of v2, /device:TPU:0, one launch (start us, length us, event | category | flops | bytes accessed | tf_op | source)
XLA Modules:
  0.0 111.1 jit_solution(8048218452897509942)
XLA Ops:
  1.6 3.1 %shard_map.127 = (bf16[1024,256]{1,0:T(8,128)(2,1)S(1)}, bf16[1024,256]{1,0:T(8,128)(2,1)S(1)}, f32[1024,512]{1,0:T(8,128)S(1)}, bf16[256,4608]{1,0:T(8,128)(2,1)S(1)}) custom-call(s32[27]{0:T(128)S(1)} %stack.115.refs_0_, f32[1024,512]{1,0:T(8,128)} %bitcast.49, bf16[256,8192]{1,0:T(8,128)(2,1)} %bitcast.44, bf16[256,512]{1,0:T(8,128)(2,1)} %bitcast.52), custom_call_target="tpu_custom_call" | custom-call | bytes 10200000 | tf_op jit(solution)/shard_map/pallas_call | solution.py:104
  5.3 4.1 %collective-permute-start.2 = (bf16[1024,256]{1,0:T(8,128)(2,1)S(1)}, bf16[1024,256]{1,0:T(8,128)(2,1)S(1)}, u32[]{:S(2)}, u32[]{:S(2)}) collective-permute-start(bf16[1024,256]{1,0:T(8,128)(2,1)S(1)} %get-tuple-element.62.refs_3_), channel_id=1, source_target_pairs={{0,2},{1,3},{2,0},{3,1},{4,6},{5,7},{6,4},{7,5},{8,10},{9,11},{10,... | collective-permute-start | bytes 1572872 | tf_op jit(solution)/shard_map/ppermute | solution.py:425
  9.4 4.9 %shard_map.128 = (f32[4096,512]{1,0:T(8,128)S(1)}, f32[1024,512]{1,0:T(8,128)}, f32[1024,512]{1,0:T(8,128)}) custom-call(s32[27]{0:T(128)S(1)} %stack.115.refs_0_, bf16[256,4608]{1,0:T(8,128)(2,1)S(1)} %get-tuple-element.59.refs_1_, bf16[256,8192]{1,0:T(8,128)(2,1)} %bitcast.45, f32[1024,512]{1,0:T(8,128)} %refs_5_.1, f32[1024,512]{1,0:T(8,128)} %refs_6_.1), custom_call_target="tpu_custom_call" | custom-call | bytes 17000000 | tf_op jit(solution)/shard_map/pallas_call | solution.py:104
  14.3 4.9 %shard_map.129 = (f32[4096,512]{1,0:T(8,128)S(1)}, f32[1024,512]{1,0:T(8,128)S(1)}, f32[1024,512]{1,0:T(8,128)S(1)}, f32[1024,128]{1,0:T(8,128)S(1)}, f32[1024,128]{1,0:T(8,128)S(1)}) custom-call(s32[27]{0:T(128)S(1)} %stack.115.refs_0_, f32[4096,512]{1,0:T(8,128)S(1)} %get-tuple-element.60.refs_1_, ...), custom_call_target="tpu_custom_call", output_to_operand_aliasing={{0}: (1, {})} | custom-call | bytes 17000000 | tf_op jit(solution)/shard_map/pallas_call | solution.py:104
  19.2 2.9 %collective-permute-done.2.refs_3_ = bf16[1024,256]{1,0:T(8,128)(2,1)S(1)} collective-permute-done((bf16[1024,256]{1,0:T(8,128)(2,1)S(1)}, bf16[1024,256]{1,0:T(8,128)(2,1)S(1)}, u32[]{:S(2)}, u32[]{:S(2)}) %collective-permute-start.2) | collective-permute-done | bytes 524320 | tf_op jit(solution)/shard_map/ppermute | solution.py:425
  23.0 2.5 %collective-permute-start.4 = (bf16[1024,256]{1,0:T(8,128)(2,1)S(1)}, bf16[1024,256]{1,0:T(8,128)(2,1)S(1)}, u32[]{:S(2)}, u32[]{:S(2)}) collective-permute-start(bf16[1024,256]{1,0:T(8,128)(2,1)S(1)} %get-tuple-element.64.refs_5_), channel_id=1, source_target_pairs={{0,2},{1,3},{2,0},{3,1},{4,6},{5,7},{6,4},{7,5},{8,10},{9,11},{10,... | collective-permute-start | bytes 1572872 | tf_op jit(solution)/shard_map/ppermute | solution.py:425
  27.6 5.7 %collective-permute-done.10.refs_3_ = bf16[1024,256]{1,0:T(8,128)(2,1)S(1)} collective-permute-done((bf16[1024,256]{1,0:T(8,128)(2,1)S(1)}, bf16[1024,256]{1,0:T(8,128)(2,1)S(1)}, u32[]{:S(2)}, u32[]{:S(2)}) %collective-permute-start.10) | collective-permute-done | bytes 524320 | tf_op jit(solution)/shard_map/ppermute | solution.py:425
  34.2 2.5 %collective-permute-start.12 = (bf16[1024,256]{1,0:T(8,128)(2,1)S(1)}, bf16[1024,256]{1,0:T(8,128)(2,1)S(1)}, u32[]{:S(2)}, u32[]{:S(2)}) collective-permute-start(bf16[1024,256]{1,0:T(8,128)(2,1)S(1)} %get-tuple-element.77), channel_id=1, source_target_pairs={{0,2},{1,3},{2,0},{3,1},{4,6},{5,7},{6,4},{7,5},{8,10},{9,11},{10,... | collective-permute-start | bytes 1572872 | tf_op jit(solution)/shard_map/ppermute | solution.py:425
  36.7 7.9 %collective-permute-done.4.refs_3_ = bf16[1024,256]{1,0:T(8,128)(2,1)S(1)} collective-permute-done((bf16[1024,256]{1,0:T(8,128)(2,1)S(1)}, bf16[1024,256]{1,0:T(8,128)(2,1)S(1)}, u32[]{:S(2)}, u32[]{:S(2)}) %collective-permute-start.4) | collective-permute-done | bytes 524320 | tf_op jit(solution)/shard_map/ppermute | solution.py:425
  45.5 2.5 %collective-permute-start.6 = (bf16[1024,256]{1,0:T(8,128)(2,1)S(1)}, bf16[1024,256]{1,0:T(8,128)(2,1)S(1)}, u32[]{:S(2)}, u32[]{:S(2)}) collective-permute-start(bf16[1024,256]{1,0:T(8,128)(2,1)S(1)} %get-tuple-element.66.refs_7_), channel_id=1, source_target_pairs={{0,2},{1,3},{2,0},{3,1},{4,6},{5,7},{6,4},{7,5},{8,10},{9,11},{10,... | collective-permute-start | bytes 1572872 | tf_op jit(solution)/shard_map/ppermute | solution.py:425
  50.2 5.6 %collective-permute-done.12.refs_3_ = bf16[1024,256]{1,0:T(8,128)(2,1)S(1)} collective-permute-done((bf16[1024,256]{1,0:T(8,128)(2,1)S(1)}, bf16[1024,256]{1,0:T(8,128)(2,1)S(1)}, u32[]{:S(2)}, u32[]{:S(2)}) %collective-permute-start.12) | collective-permute-done | bytes 524320 | tf_op jit(solution)/shard_map/ppermute | solution.py:425
  56.7 2.5 %collective-permute-start.15 = (bf16[1024,256]{1,0:T(8,128)(2,1)S(1)}, bf16[1024,256]{1,0:T(8,128)(2,1)S(1)}, u32[]{:S(2)}, u32[]{:S(2)}) collective-permute-start(bf16[1024,256]{1,0:T(8,128)(2,1)S(1)} %get-tuple-element.84), channel_id=1, source_target_pairs={{0,2},{1,3},{2,0},{3,1},{4,6},{5,7},{6,4},{7,5},{8,10},{9,11},{10,... | collective-permute-start | bytes 1572872 | tf_op jit(solution)/shard_map/ppermute | solution.py:425
  59.2 7.8 %collective-permute-done.6.refs_3_ = bf16[1024,256]{1,0:T(8,128)(2,1)S(1)} collective-permute-done((bf16[1024,256]{1,0:T(8,128)(2,1)S(1)}, bf16[1024,256]{1,0:T(8,128)(2,1)S(1)}, u32[]{:S(2)}, u32[]{:S(2)}) %collective-permute-start.6) | collective-permute-done | bytes 524320 | tf_op jit(solution)/shard_map/ppermute | solution.py:425
  67.9 2.1 %shard_map.137 = (bf16[256,1024]{1,0:T(8,128)(2,1)S(1)}, bf16[256,8192]{1,0:T(8,128)(2,1)}, f32[8,128]{1,0:T(8,128)S(1)}) custom-call(s32[27]{0:T(128)S(1)} %stack.115.refs_0_, bf16[256,4608]{1,0:T(8,128)(2,1)S(1)} %get-tuple-element.59.refs_1_, bf16[256,4608]{1,0:T(8,128)(2,1)S(1)} %collective-permute-done.refs_2_, ...), custom_call_target="tpu_custom_call", output_to_operand_aliasing={{1}: (6, {})} | custom-call | bytes 7140000 | tf_op jit(solution)/shard_map/pallas_call | solution.py:104
  70.1 2.2 %collective-permute-start.7 = (bf16[1024,256]{1,0:T(8,128)(2,1)S(1)}, bf16[1024,256]{1,0:T(8,128)(2,1)S(1)}, u32[]{:S(2)}, u32[]{:S(2)}) collective-permute-start(bf16[1024,256]{1,0:T(8,128)(2,1)S(1)} %get-tuple-element.67.refs_7_), channel_id=1, source_target_pairs={{0,2},{1,3},{2,0},{3,1},{4,6},{5,7},{6,4},{7,5},{8,10},{9,11},{10,... | collective-permute-start | bytes 1572872 | tf_op jit(solution)/shard_map/ppermute | solution.py:425
  72.5 5.8 %collective-permute-done.15.refs_3_ = bf16[1024,256]{1,0:T(8,128)(2,1)S(1)} collective-permute-done((bf16[1024,256]{1,0:T(8,128)(2,1)S(1)}, bf16[1024,256]{1,0:T(8,128)(2,1)S(1)}, u32[]{:S(2)}, u32[]{:S(2)}) %collective-permute-start.15) | collective-permute-done | bytes 524320 | tf_op jit(solution)/shard_map/ppermute | solution.py:425
  79.1 2.2 %collective-permute-start.22 = (bf16[1024,256]{1,0:T(8,128)(2,1)S(1)}, bf16[1024,256]{1,0:T(8,128)(2,1)S(1)}, u32[]{:S(2)}, u32[]{:S(2)}) collective-permute-start(bf16[1024,256]{1,0:T(8,128)(2,1)S(1)} %get-tuple-element.97), channel_id=1, source_target_pairs={{0,2},{1,3},{2,0},{3,1},{4,6},{5,7},{6,4},{7,5},{8,10},{9,11},{10,... | collective-permute-start | bytes 1572872 | tf_op jit(solution)/shard_map/ppermute | solution.py:425
  81.3 2.1 %shard_map.139 = (bf16[256,1024]{1,0:T(8,128)(2,1)S(1)}, bf16[256,8192]{1,0:T(8,128)(2,1)}, f32[8,128]{1,0:T(8,128)S(1)}) custom-call(s32[27]{0:T(128)S(1)} %stack.115.refs_0_, bf16[256,4608]{1,0:T(8,128)(2,1)S(1)} %get-tuple-element.59.refs_1_, bf16[256,4608]{1,0:T(8,128)(2,1)S(1)} %collective-permute-done.refs_2_, ...), custom_call_target="tpu_custom_call", output_to_operand_aliasing={{1}: (6, {})} | custom-call | bytes 7140000 | tf_op jit(solution)/shard_map/pallas_call | solution.py:104
  84.0 5.5 %collective-permute-done.7.refs_2_ = bf16[1024,256]{1,0:T(8,128)(2,1)S(1)} collective-permute-done((bf16[1024,256]{1,0:T(8,128)(2,1)S(1)}, bf16[1024,256]{1,0:T(8,128)(2,1)S(1)}, u32[]{:S(2)}, u32[]{:S(2)}) %collective-permute-start.7) | collective-permute-done | bytes 524320 | tf_op jit(solution)/shard_map/ppermute | solution.py:425
  89.5 2.9 %shard_map.140 = (f32[1024,512]{1,0:T(8,128)}, f32[1024,512]{1,0:T(8,128)}, f32[1024,512]{1,0:T(8,128)}, bf16[1024,128]{1,0:T(8,128)(2,1)S(1)}) custom-call(s32[27]{0:T(128)S(1)} %stack.115.refs_0_, f32[4096,512]{1,0:T(8,128)S(1)} %get-tuple-element.61.refs_1_, bf16[1024,256]{1,0:T(8,128)(2,1)S(1)} %collective-permute-done.7.refs_2_, ...), custom_call_target="tpu_custom_call" | custom-call | bytes 9520000 | tf_op jit(solution)/shard_map/pallas_call | solution.py:104
  95.5 4.8 %collective-permute-done.22.refs_2_ = bf16[1024,256]{1,0:T(8,128)(2,1)S(1)} collective-permute-done((bf16[1024,256]{1,0:T(8,128)(2,1)S(1)}, bf16[1024,256]{1,0:T(8,128)(2,1)S(1)}, u32[]{:S(2)}, u32[]{:S(2)}) %collective-permute-start.22) | collective-permute-done | bytes 524320 | tf_op jit(solution)/shard_map/ppermute | solution.py:425
  100.3 2.4 %collective-permute-start.20 = (bf16[1024,128]{1,0:T(8,128)(2,1)S(1)}, bf16[1024,128]{1,0:T(8,128)(2,1)S(1)}, u32[]{:S(2)}, u32[]{:S(2)}) collective-permute-start(bf16[1024,128]{1,0:T(8,128)(2,1)S(1)} %get-tuple-element.94.refs_1_), channel_id=1, source_target_pairs={{0,24},{8,16},{16,8},{24,0},{1,25},{9,17},{17,9},{25,1},{2,26},{10... | collective-permute-start | bytes 786440 | tf_op jit(solution)/shard_map/ppermute | solution.py:425
  102.8 2.8 %shard_map.141 = (f32[1024,512]{1,0:T(8,128)}, f32[1024,512]{1,0:T(8,128)}, f32[1024,512]{1,0:T(8,128)}) custom-call(s32[27]{0:T(128)S(1)} %stack.115.refs_0_, f32[4096,512]{1,0:T(8,128)S(1)} %get-tuple-element.61.refs_1_, bf16[1024,256]{1,0:T(8,128)(2,1)S(1)} %collective-permute-done.22.refs_2_, ...), custom_call_target="tpu_custom_call", output_to_operand_aliasing={{0}: (7, {}), {1}: (8, {}), {2}: (9, {})} | custom-call | bytes 9520000 | tf_op jit(solution)/shard_map/pallas_call | solution.py:104
  105.6 3.5 %collective-permute-done.20.refs_4_ = bf16[1024,128]{1,0:T(8,128)(2,1)S(1)} collective-permute-done((bf16[1024,128]{1,0:T(8,128)(2,1)S(1)}, bf16[1024,128]{1,0:T(8,128)(2,1)S(1)}, u32[]{:S(2)}, u32[]{:S(2)}) %collective-permute-start.20) | collective-permute-done | bytes 262176 | tf_op jit(solution)/shard_map/ppermute | solution.py:425
  (41 shorter events, 16.0 us)
Async XLA Ops:
  4.7 9.7 %collective-permute-start = (bf16[256,4608]{1,0:T(8,128)(2,1)S(1)}, bf16[256,4608]{1,0:T(8,128)(2,1)S(1)}, u32[]{:S(2)}, u32[]{:S(2)}) collective-permute-start(bf16[256,4608]{1,0:T(8,128)(2,1)S(1)} %get-tuple-element.59.refs_1_), channel_id=1, source_target_pairs={{0,1},{1,0},{2,3},{3,2},{4,5},{5,4},{6,7},{7,6},{8,9},{9,8},{10,11... | collective-permute-start | bytes 7077896 | tf_op jit(solution)/shard_map/ppermute | solution.py:425
  5.2 14.0 %collective-permute-start.1 = (bf16[1024,256]{1,0:T(8,128)(2,1)S(1)}, bf16[1024,256]{1,0:T(8,128)(2,1)S(1)}, u32[]{:S(2)}, u32[]{:S(2)}) collective-permute-start(bf16[1024,256]{1,0:T(8,128)(2,1)S(1)} %get-tuple-element.62.refs_3_), channel_id=1, source_target_pairs={{0,1},{1,0},{2,4},{3,5},{4,2},{5,3},{6,7},{7,6},{8,9},{9,8},{10,12... | collective-permute-start | bytes 1572872 | tf_op jit(solution)/shard_map/ppermute | solution.py:425
  5.3 16.8 %collective-permute-start.2 = (bf16[1024,256]{1,0:T(8,128)(2,1)S(1)}, bf16[1024,256]{1,0:T(8,128)(2,1)S(1)}, u32[]{:S(2)}, u32[]{:S(2)}) collective-permute-start(bf16[1024,256]{1,0:T(8,128)(2,1)S(1)} %get-tuple-element.62.refs_3_), channel_id=1, source_target_pairs={{0,2},{1,3},{2,0},{3,1},{4,6},{5,7},{6,4},{7,5},{8,10},{9,11},{10,... | collective-permute-start | bytes 1572872 | tf_op jit(solution)/shard_map/ppermute | solution.py:425
  9.4 23.9 %collective-permute-start.10 = (bf16[1024,256]{1,0:T(8,128)(2,1)S(1)}, bf16[1024,256]{1,0:T(8,128)(2,1)S(1)}, u32[]{:S(2)}, u32[]{:S(2)}) collective-permute-start(bf16[1024,256]{1,0:T(8,128)(2,1)S(1)} %get-tuple-element.74.refs_4_), channel_id=1, source_target_pairs={{0,2},{1,3},{2,0},{3,1},{4,6},{5,7},{6,4},{7,5},{8,10},{9,11},{10,... | collective-permute-start | bytes 1572872 | tf_op jit(solution)/shard_map/ppermute | solution.py:425
  9.4 23.9 %collective-permute-start.9 = (bf16[1024,256]{1,0:T(8,128)(2,1)S(1)}, bf16[1024,256]{1,0:T(8,128)(2,1)S(1)}, u32[]{:S(2)}, u32[]{:S(2)}) collective-permute-start(bf16[1024,256]{1,0:T(8,128)(2,1)S(1)} %get-tuple-element.74.refs_4_), channel_id=1, source_target_pairs={{0,1},{1,0},{2,4},{3,5},{4,2},{5,3},{6,7},{7,6},{8,9},{9,8},{10,12... | collective-permute-start | bytes 1572872 | tf_op jit(solution)/shard_map/ppermute | solution.py:425
  22.9 13.8 %collective-permute-start.3 = (bf16[1024,256]{1,0:T(8,128)(2,1)S(1)}, bf16[1024,256]{1,0:T(8,128)(2,1)S(1)}, u32[]{:S(2)}, u32[]{:S(2)}) collective-permute-start(bf16[1024,256]{1,0:T(8,128)(2,1)S(1)} %get-tuple-element.63), channel_id=1, source_target_pairs={{0,1},{1,0},{2,4},{3,5},{4,2},{5,3},{6,7},{7,6},{8,9},{9,8},{10,12... | collective-permute-start | bytes 1572872 | tf_op jit(solution)/shard_map/ppermute | solution.py:425
  23.0 21.6 %collective-permute-start.4 = (bf16[1024,256]{1,0:T(8,128)(2,1)S(1)}, bf16[1024,256]{1,0:T(8,128)(2,1)S(1)}, u32[]{:S(2)}, u32[]{:S(2)}) collective-permute-start(bf16[1024,256]{1,0:T(8,128)(2,1)S(1)} %get-tuple-element.64.refs_5_), channel_id=1, source_target_pairs={{0,2},{1,3},{2,0},{3,1},{4,6},{5,7},{6,4},{7,5},{8,10},{9,11},{10,... | collective-permute-start | bytes 1572872 | tf_op jit(solution)/shard_map/ppermute | solution.py:425
  27.5 20.5 %collective-permute-start.13 = (bf16[256,1024]{1,0:T(8,128)(2,1)S(1)}, bf16[256,1024]{1,0:T(8,128)(2,1)S(1)}, u32[]{:S(2)}, u32[]{:S(2)}) collective-permute-start(bf16[256,1024]{1,0:T(8,128)(2,1)S(1)} %get-tuple-element.80), channel_id=1, source_target_pairs={{0,1},{1,0},{2,3},{3,2},{4,5},{5,4},{6,7},{7,6},{8,9},{9,8},{10,11... | collective-permute-start | bytes 1572872 | tf_op jit(solution)/shard_map/ppermute | solution.py:425
  34.1 16.1 %collective-permute-start.11 = (bf16[1024,256]{1,0:T(8,128)(2,1)S(1)}, bf16[1024,256]{1,0:T(8,128)(2,1)S(1)}, u32[]{:S(2)}, u32[]{:S(2)}) collective-permute-start(bf16[1024,256]{1,0:T(8,128)(2,1)S(1)} %get-tuple-element.76), channel_id=1, source_target_pairs={{0,1},{1,0},{2,4},{3,5},{4,2},{5,3},{6,7},{7,6},{8,9},{9,8},{10,12... | collective-permute-start | bytes 1572872 | tf_op jit(solution)/shard_map/ppermute | solution.py:425
  34.2 21.6 %collective-permute-start.12 = (bf16[1024,256]{1,0:T(8,128)(2,1)S(1)}, bf16[1024,256]{1,0:T(8,128)(2,1)S(1)}, u32[]{:S(2)}, u32[]{:S(2)}) collective-permute-start(bf16[1024,256]{1,0:T(8,128)(2,1)S(1)} %get-tuple-element.77), channel_id=1, source_target_pairs={{0,2},{1,3},{2,0},{3,1},{4,6},{5,7},{6,4},{7,5},{8,10},{9,11},{10,... | collective-permute-start | bytes 1572872 | tf_op jit(solution)/shard_map/ppermute | solution.py:425
  45.4 13.8 %collective-permute-start.5 = (bf16[1024,256]{1,0:T(8,128)(2,1)S(1)}, bf16[1024,256]{1,0:T(8,128)(2,1)S(1)}, u32[]{:S(2)}, u32[]{:S(2)}) collective-permute-start(bf16[1024,256]{1,0:T(8,128)(2,1)S(1)} %get-tuple-element.65), channel_id=1, source_target_pairs={{0,1},{1,0},{2,4},{3,5},{4,2},{5,3},{6,7},{7,6},{8,9},{9,8},{10,12... | collective-permute-start | bytes 1572872 | tf_op jit(solution)/shard_map/ppermute | solution.py:425
  45.5 21.6 %collective-permute-start.6 = (bf16[1024,256]{1,0:T(8,128)(2,1)S(1)}, bf16[1024,256]{1,0:T(8,128)(2,1)S(1)}, u32[]{:S(2)}, u32[]{:S(2)}) collective-permute-start(bf16[1024,256]{1,0:T(8,128)(2,1)S(1)} %get-tuple-element.66.refs_7_), channel_id=1, source_target_pairs={{0,2},{1,3},{2,0},{3,1},{4,6},{5,7},{6,4},{7,5},{8,10},{9,11},{10,... | collective-permute-start | bytes 1572872 | tf_op jit(solution)/shard_map/ppermute | solution.py:425
  50.1 17.7 %collective-permute-start.16 = (bf16[256,1024]{1,0:T(8,128)(2,1)S(1)}, bf16[256,1024]{1,0:T(8,128)(2,1)S(1)}, u32[]{:S(2)}, u32[]{:S(2)}) collective-permute-start(bf16[256,1024]{1,0:T(8,128)(2,1)S(1)} %get-tuple-element.87), channel_id=1, source_target_pairs={{0,1},{1,0},{2,3},{3,2},{4,5},{5,4},{6,7},{7,6},{8,9},{9,8},{10,11... | collective-permute-start | bytes 1572872 | tf_op jit(solution)/shard_map/ppermute | solution.py:425
  56.6 15.8 %collective-permute-start.14 = (bf16[1024,256]{1,0:T(8,128)(2,1)S(1)}, bf16[1024,256]{1,0:T(8,128)(2,1)S(1)}, u32[]{:S(2)}, u32[]{:S(2)}) collective-permute-start(bf16[1024,256]{1,0:T(8,128)(2,1)S(1)} %get-tuple-element.83), channel_id=1, source_target_pairs={{0,1},{1,0},{2,4},{3,5},{4,2},{5,3},{6,7},{7,6},{8,9},{9,8},{10,12... | collective-permute-start | bytes 1572872 | tf_op jit(solution)/shard_map/ppermute | solution.py:425
  56.7 21.6 %collective-permute-start.15 = (bf16[1024,256]{1,0:T(8,128)(2,1)S(1)}, bf16[1024,256]{1,0:T(8,128)(2,1)S(1)}, u32[]{:S(2)}, u32[]{:S(2)}) collective-permute-start(bf16[1024,256]{1,0:T(8,128)(2,1)S(1)} %get-tuple-element.84), channel_id=1, source_target_pairs={{0,2},{1,3},{2,0},{3,1},{4,6},{5,7},{6,4},{7,5},{8,10},{9,11},{10,... | collective-permute-start | bytes 1572872 | tf_op jit(solution)/shard_map/ppermute | solution.py:425
  70.0 11.3 %collective-permute-start.17 = (bf16[256,1024]{1,0:T(8,128)(2,1)S(1)}, bf16[256,1024]{1,0:T(8,128)(2,1)S(1)}, u32[]{:S(2)}, u32[]{:S(2)}) collective-permute-start(bf16[256,1024]{1,0:T(8,128)(2,1)S(1)} %get-tuple-element.91), channel_id=1, source_target_pairs={{0,1},{1,0},{2,3},{3,2},{4,5},{5,4},{6,7},{7,6},{8,9},{9,8},{10,11... | collective-permute-start | bytes 1572872 | tf_op jit(solution)/shard_map/ppermute | solution.py:425
  70.1 19.5 %collective-permute-start.7 = (bf16[1024,256]{1,0:T(8,128)(2,1)S(1)}, bf16[1024,256]{1,0:T(8,128)(2,1)S(1)}, u32[]{:S(2)}, u32[]{:S(2)}) collective-permute-start(bf16[1024,256]{1,0:T(8,128)(2,1)S(1)} %get-tuple-element.67.refs_7_), channel_id=1, source_target_pairs={{0,2},{1,3},{2,0},{3,1},{4,6},{5,7},{6,4},{7,5},{8,10},{9,11},{10,... | collective-permute-start | bytes 1572872 | tf_op jit(solution)/shard_map/ppermute | solution.py:425
  72.3 17.2 %collective-permute-start.8 = (bf16[1024,256]{1,0:T(8,128)(2,1)S(1)}, bf16[1024,256]{1,0:T(8,128)(2,1)S(1)}, u32[]{:S(2)}, u32[]{:S(2)}) collective-permute-start(bf16[1024,256]{1,0:T(8,128)(2,1)S(1)} %get-tuple-element.68), channel_id=1, source_target_pairs={{0,1},{1,0},{2,4},{3,5},{4,2},{5,3},{6,7},{7,6},{8,9},{9,8},{10,12... | collective-permute-start | bytes 1572872 | tf_op jit(solution)/shard_map/ppermute | solution.py:425
  79.1 21.2 %collective-permute-start.22 = (bf16[1024,256]{1,0:T(8,128)(2,1)S(1)}, bf16[1024,256]{1,0:T(8,128)(2,1)S(1)}, u32[]{:S(2)}, u32[]{:S(2)}) collective-permute-start(bf16[1024,256]{1,0:T(8,128)(2,1)S(1)} %get-tuple-element.97), channel_id=1, source_target_pairs={{0,2},{1,3},{2,0},{3,1},{4,6},{5,7},{6,4},{7,5},{8,10},{9,11},{10,... | collective-permute-start | bytes 1572872 | tf_op jit(solution)/shard_map/ppermute | solution.py:425
  81.3 21.4 %collective-permute-start.23 = (bf16[1024,256]{1,0:T(8,128)(2,1)S(1)}, bf16[1024,256]{1,0:T(8,128)(2,1)S(1)}, u32[]{:S(2)}, u32[]{:S(2)}) collective-permute-start(bf16[1024,256]{1,0:T(8,128)(2,1)S(1)} %get-tuple-element.98), channel_id=1, source_target_pairs={{0,1},{1,0},{2,4},{3,5},{4,2},{5,3},{6,7},{7,6},{8,9},{9,8},{10,12... | collective-permute-start | bytes 1572872 | tf_op jit(solution)/shard_map/ppermute | solution.py:425
  83.4 25.6 %collective-permute-start.21 = (bf16[256,1024]{1,0:T(8,128)(2,1)S(1)}, bf16[256,1024]{1,0:T(8,128)(2,1)S(1)}, u32[]{:S(2)}, u32[]{:S(2)}) collective-permute-start(bf16[256,1024]{1,0:T(8,128)(2,1)S(1)} %get-tuple-element.96), channel_id=1, source_target_pairs={{0,1},{1,0},{2,3},{3,2},{4,5},{5,4},{6,7},{7,6},{8,9},{9,8},{10,11... | collective-permute-start | bytes 1572872 | tf_op jit(solution)/shard_map/ppermute | solution.py:425
  92.4 13.2 %collective-permute-start.18 = (bf16[1024,128]{1,0:T(8,128)(2,1)S(1)}, bf16[1024,128]{1,0:T(8,128)(2,1)S(1)}, u32[]{:S(2)}, u32[]{:S(2)}) collective-permute-start(bf16[1024,128]{1,0:T(8,128)(2,1)S(1)} %get-tuple-element.94.refs_1_), channel_id=1, source_target_pairs={{0,8},{8,0},{16,24},{24,16},{1,9},{9,1},{17,25},{25,17},{2,10},{10... | collective-permute-start | bytes 786440 | tf_op jit(solution)/shard_map/ppermute | solution.py:425
  94.0 11.7 %collective-permute-start.19 = (bf16[1024,128]{1,0:T(8,128)(2,1)S(1)}, bf16[1024,128]{1,0:T(8,128)(2,1)S(1)}, u32[]{:S(2)}, u32[]{:S(2)}) collective-permute-start(bf16[1024,128]{1,0:T(8,128)(2,1)S(1)} %get-tuple-element.94.refs_1_), channel_id=1, source_target_pairs={{0,16},{8,24},{16,0},{24,8},{1,17},{9,25},{17,1},{25,9},{2,18},{10... | collective-permute-start | bytes 786440 | tf_op jit(solution)/shard_map/ppermute | solution.py:425
  100.3 8.8 %collective-permute-start.20 = (bf16[1024,128]{1,0:T(8,128)(2,1)S(1)}, bf16[1024,128]{1,0:T(8,128)(2,1)S(1)}, u32[]{:S(2)}, u32[]{:S(2)}) collective-permute-start(bf16[1024,128]{1,0:T(8,128)(2,1)S(1)} %get-tuple-element.94.refs_1_), channel_id=1, source_target_pairs={{0,24},{8,16},{16,8},{24,0},{1,25},{9,17},{17,9},{25,1},{2,26},{10... | collective-permute-start | bytes 786440 | tf_op jit(solution)/shard_map/ppermute | solution.py:425

commit v3 on v2

--- a/solution.py
+++ b/solution.py
@@ -128,84 +128,99 @@
     return copy
 
 
+def pieces(head):
+    return (0, HEAD, head), (HEAD, HEAD, head ^ 1), (2 * HEAD, 2 * HEAD, 1 - head // 2)
+
+
 def turned(at, s, src, dst, sems, base, first=0):
     return [
         start(
-            columns_of(src, s[at["heads"] + k], HEAD),
-            dst.at[:, pl.ds(first + k * HEAD, HEAD)],
+            columns_of(src, s[at["pieces"] + k], width),
+            dst.at[:, pl.ds(column + first, width)],
             sems.at[base + k],
         )
-        for k in range(src.shape[1] // HEAD)
+        for k, (column, width, _) in enumerate(pieces(0))
     ]
 
 
-def ready_body(at, s, w, act, cot, *rest):
-    *lows, w_v, packed, sems = rest
-    rows = w.shape[0]
-    step = rows // 4
-    heads = w.shape[1] // HEAD
-    wide = packed.shape[1] - cot.shape[1]
-    first = [
-        turned(
-            at, s, w.at[pl.ds(i * step, step)], w_v.at[pl.ds(i * step, step)], sems, i * heads
-        )
-        for i in range(4)
-    ]
+def cast_body(offset, s, w, low, wide, sems):
+    rows, part = low.shape
+    step = rows // 2
     copies = [
         start(
-            columns_of(act, 2 * d + 1 - s[at["core"]], rows),
-            packed.at[:, pl.ds(d * rows, rows)],
-            sems.at[4 * heads + d],
+            w.at[pl.ds(i * step, step), pl.ds(offset, part)],
+            wide.at[pl.ds(i * step, step)],
+            sems.at[i],
         )
-        for d in range(wide // rows)
+        for i in range(2)
     ]
-    copies += turned(at, s, cot, packed, sems, 4 * heads + len(copies), wide)
-    for i in range(4):
-        for copy in first[i]:
-            copy.wait()
-        here = pl.ds(i * step, step)
-        for (offset, part), low in zip(PARTS, lows):
-            low[here, :] = w_v[here, offset : offset + part].astype(BF16)
-    for copy in copies:
-        copy.wait()
-
-
-def own_body(at, s, packed, act, anchor, moment, *rest):
-    sums_ref, anchor_out, moment_out, act_s, held, sems = rest
+    for i, copy in enumerate(copies):
+        copy.wait()
+
+        @pl.loop(0, step // 64)
+        def _(n):
+            here = pl.ds(pl.multiple_of(i * step + n * 64, 64), 64)
+            low[here, :] = wide[here, :].astype(BF16)
+
+
+def load_blocks(at, s, act, cot, act_s, cot_v, sems):
+    heads = turned(at, s, cot, cot_v, sems, 0)
+    rows = act_s.shape[2]
+    blocks = [
+        start(columns_of(act, 2 * d + s[at["core"]], rows), act_s.at[d], sems.at[len(heads) + d])
+        for d in range(act_s.shape[0])
+    ]
+    return heads, blocks
+
+
+def own_body(at, s, act, cot, anchor, moment, *rest):
+    sums_ref, anchor_out, moment_out, act_s, cot_v, held, sems = rest
     chips, _, rows = act_s.shape
-    blocks = [
-        start(columns_of(act, 2 * d + s[at["core"]], rows), act_s.at[d], sems.at[d])
-        for d in range(chips)
-    ]
-    loads = [
-        start(src, held.at[k], sems.at[chips + k]) for k, src in enumerate((anchor, moment))
-    ]
+    heads, blocks = load_blocks(at, s, act, cot, act_s, cot_v, sems)
+    base = len(heads) + chips
+    loads = [start(src, held.at[k], sems.at[base + k]) for k, src in enumerate((anchor, moment))]
     stores = []
-    for d in range(chips):
-        blocks[d].wait()
+    for k, dst in enumerate((anchor_out, moment_out)):
+        loads[k].wait()
+        stores.append(start(held.at[k], dst, sems.at[base + 2 + k]))
+    for copy in heads + blocks:
+        copy.wait()
+
+    @pl.loop(0, chips)
+    def _(d):
         for i in range(rows // TILE):
-            sums_ref[pl.ds(d * rows + i * TILE, TILE), :] = rows_by_columns(
-                act_s[d, :, i * TILE : (i + 1) * TILE], packed[:, chips * rows :]
+            here = pl.ds(pl.multiple_of(d * rows + i * TILE, TILE), TILE)
+            sums_ref[here, :] = rows_by_columns(
+                act_s[d, :, i * TILE : (i + 1) * TILE], cot_v[...]
             )
-        if d == 1:
-            for k, dst in enumerate((anchor_out, moment_out)):
-                loads[k].wait()
-                stores.append(start(held.at[k], dst, sems.at[chips + 2 + k]))
+
     for copy in stores:
         copy.wait()
 
 
-def sibling_body(at, s, before, packed, m, v, anchor, moment, *rest):
-    sums_ref, m_v, v_v, anchor_v, moment_v, sems = rest
+def sibling_body(at, s, before, act, cot, w, m, v, anchor, moment, *rest):
+    sums_ref, w_v, m_v, v_v, anchor_v, moment_v, act_s, cot_v, sems = rest
+    chips, _, rows = act_s.shape
+    heads, blocks = load_blocks(at, s, act, cot, act_s, cot_v, sems)
+    base = len(heads) + chips
     copies = []
-    for src, dst in ((m, m_v), (v, v_v)):
-        copies += turned(at, s, src, dst, sems, len(copies))
+    for src, dst in ((w, w_v), (m, m_v), (v, v_v)):
+        copies += turned(at, s, src, dst, sems, base + len(copies))
     for src, dst in ((anchor, anchor_v), (moment, moment_v)):
-        copies.append(start(columns_of(src, s[at["heads"]], HEAD), dst, sems.at[len(copies)]))
-    wide = sums_ref.shape[0]
-    for i in range(wide // TILE):
-        here = slice(i * TILE, (i + 1) * TILE)
-        sums_ref[here, :] = before[here, :] + rows_by_columns(packed[:, here], packed[:, wide:])
+        copies.append(
+            start(columns_of(src, s[at["pieces"]], HEAD), dst, sems.at[base + len(copies)])
+        )
+    for copy in heads + blocks:
+        copy.wait()
+
+    @pl.loop(0, chips)
+    def _(d):
+        for i in range(rows // TILE):
+            here = pl.ds(pl.multiple_of(d * rows + i * TILE, TILE), TILE)
+            sums_ref[here, :] = before[here, :] + rows_by_columns(
+                act_s[d, :, i * TILE : (i + 1) * TILE], cot_v[...]
+            )
+
     for copy in copies:
         copy.wait()
 
@@ -219,7 +234,7 @@
     size = 64
 
     def each(body):
-        @pl.loop(0, rows // size, unroll=4)
+        @pl.loop(0, rows // size)
         def _(i):
             body(pl.multiple_of(i * size, size))
 
@@ -271,10 +286,9 @@
             keep(from_e)
 
 
-def grad_body(at, which, s, packed, packed_sib, *rest):
+def grad_body(at, which, s, cot_own, cot_sib, *rest):
     theirs, out, token, stage, sems = rest[-5:]
     rows = stage.shape[1]
-    wide = packed.shape[1] - sum(part for _, part in PARTS)
     copies = []
     if which > 0:
         copies.append(
@@ -282,13 +296,13 @@
                 rest[len(PARTS)], columns_of(out, s[at["grad"] + 2 * which - 1], rows), sems.at[1]
             )
         )
-    for cot, dst in ((packed_sib, theirs), (packed, stage)):
+    for cot, dst in ((cot_sib, theirs), (cot_own, stage)):
         for i in range(rows // TILE):
             here = slice(i * TILE, (i + 1) * TILE)
             total = None
             for (offset, part), block in zip(PARTS, rest):
                 term = lax.dot_general(
-                    cot[:, wide + offset : wide + offset + part],
+                    cot[:, offset : offset + part],
                     block[here, :],
                     (((1,), (1,)), ((), ())),
                     preferred_element_type=F32,
@@ -301,66 +315,102 @@
         copy.wait()
 
 
-def adam_body(at, offset, s, sums_ref, from_e, from_o, w, m, v, *rest):
+def adam(at, offset, first_row, s, sums_ref, from_e, from_o, w, m, v, put, count, width, taken):
+    columns = slice(offset, offset + width)
+    size = 128
+    base = pl.multiple_of(s[at["z"]] * from_e.shape[0], TILE)
+
+    @pl.loop(0, count // size)
+    def _(i):
+        r = pl.multiple_of(first_row + i * size, size)
+        here = pl.ds(r, size)
+        one = sums_ref[pl.ds(base + r, size), columns] + from_e[here, taken].astype(F32)
+        both = one + from_o[here, taken].astype(F32)
+        gradient = jnp.where(s[at["middle"]] == 1, both, one)
+        first = 0.9 * m[here, columns] + 0.1 * gradient
+        second = 0.95 * v[here, columns] + 0.05 * gradient * gradient
+        scaled = second * (1.0 / CORR_TWO)
+        below = scaled * lax.rsqrt(scaled) + 1e-08
+        over = pl.reciprocal(below, approx=True)
+        over = over * (2.0 - below * over)
+        stepped = (1.0 - 0.1 * 0.1) * w[here, columns] - first * (0.1 / CORR_ONE) * over
+        put(r, stepped, first, second)
+
+
+def head_body(at, s, sums_ref, from_e, from_o, w, m, v, anchor, upper, lower, first_v, second_v):
+    rows = anchor.shape[0]
+    for k, diff in enumerate((upper, lower)):
+        top = k * rows // 2
+
+        def put(r, stepped, first, second):
+            here = pl.ds(r, stepped.shape[0])
+            first_v[here, :] = first
+            second_v[here, :] = second
+            there = pl.ds(r - top, stepped.shape[0])
+            diff[there, :] = (anchor[here, :] - stepped).astype(BF16)
+
+        args = (from_e, from_o, w, m, v, put, rows // 2, HEAD, slice(0, HEAD))
+        adam(at, 0, top, s, sums_ref, *args)
+
+
+def rest_body(at, offset, part, within, s, sums_ref, from_e, from_o, w, m, v, *rest):
     stage, sems = rest[-2:]
-    rows, part = from_e.shape
-    if offset == 0:
-        anchor, diff = rest[0], rest[4]
-        outs = rest[1:4]
+    rows = from_e.shape[0]
+    copies = []
+    if within:
+        first_v, second_v, theirs = rest[:3]
+        *outs, grads, token = rest[4:-2]
+        for k, src in enumerate((first_v, second_v)):
+            there = columns_of(outs[1 + k], s[at["pieces"]], HEAD)
+            copies.append(start(src, there, sems.at[k]))
+        copies.append(start(theirs, columns_of(grads, s[at["grad"] + 7], rows), sems.at[2]))
     else:
-        outs = rest[3:6]
-    columns = slice(offset, offset + part)
-    size = 64 * 256 // part // 16 * 16
-    base = pl.multiple_of(s[at["z"]] * rows, rows)
-    copies = []
+        *outs, token = rest[3:-2]
+    token[...] = jnp.zeros_like(token)
+    piece = next(k for k, (column, *_) in enumerate(pieces(0)) if column == offset)
+
+    def put(r, stepped, first, second):
+        here = pl.ds(r, stepped.shape[0])
+        stage[0, here, :] = stepped
+        stage[1, here, :] = first
+        stage[2, here, :] = second
+
     for tile in range(rows // TILE):
-
-        @pl.loop(0, TILE // size)
-        def _(i):
-            r = pl.multiple_of(tile * TILE + i * size, size)
-            here = pl.ds(r, size)
-            one = sums_ref[pl.ds(base + r, size), columns] + from_e[here, :].astype(F32)
-            gradient = jnp.where(s[at["middle"]] == 1, one + from_o[here, :].astype(F32), one)
-            weights = w[here, columns]
-            first = 0.9 * m[here, columns] + 0.1 * gradient
-            second = 0.95 * v[here, columns] + 0.05 * gradient * gradient
-            update = first / CORR_ONE / (jnp.sqrt(second / CORR_TWO) + 1e-08) + 0.1 * weights
-            stepped = weights - 0.1 * update
-            stage[0, here, :] = stepped
-            stage[1, here, :] = first
-            stage[2, here, :] = second
-            if offset == 0:
-                diff[here, :] = (anchor[here, :] - stepped[:, :HEAD]).astype(BF16)
-
+        args = (from_e, from_o, w, m, v, put, TILE, part, slice(within, within + part))
+        adam(at, offset, tile * TILE, s, sums_ref, *args)
         there = pl.ds(tile * TILE, TILE)
         for k, out in enumerate(outs):
-            for h in range(part // HEAD):
-                copies.append(
-                    start(
-                        stage.at[k, there, pl.ds(h * HEAD, HEAD)],
-                        columns_of(out.at[there], s[at["heads"] + offset // HEAD + h], HEAD),
-                        sems.at[len(copies)],
-                    )
+            copies.append(
+                start(
+                    stage.at[k, there],
+                    columns_of(out.at[there], s[at["pieces"] + piece], part),
+                    sems.at[len(copies)],
                 )
+            )
     for copy in copies:
         copy.wait()
 
 
-def outer_body(at, s, own, one, two, three, anchor, moment, theirs, *rest):
-    inner, new_anchor, new_moment, grads, stage, sems = rest[4:]
-    rows = theirs.shape[1]
-    copies = [start(theirs, columns_of(grads, s[at["grad"] + 7], rows), sems.at[3])]
-    total = (own[...].astype(F32) + one[...].astype(F32)) + (
-        two[...].astype(F32) + three[...].astype(F32)
-    )
-    average = total / 4.0
-    momentum = 0.9 * moment[...] + average
-    stage[0] = momentum
-    stage[1] = anchor[...] - 0.7 * (average + 0.9 * momentum)
-    copies += [
-        start(stage.at[k], columns_of(out, s[at["heads"]], HEAD), sems.at[i])
-        for i, (k, out) in enumerate(((0, new_moment), (1, new_anchor), (1, inner)))
-    ]
+def mix_body(s, own, other, out):
+    out[...] = (own[...].astype(F32) + other[...].astype(F32)).astype(BF16)
+
+
+def outer_body(at, s, upper, upper_in, lower, lower_in, anchor, moment, *rest):
+    inner, new_anchor, new_moment, stage, sems = rest[3:]
+    half = upper.shape[0]
+    copies = []
+    for n, (own, other) in enumerate(((upper, upper_in), (lower, lower_in))):
+        here = pl.ds(n * half, half)
+        average = (own[...].astype(F32) + other[...].astype(F32)) / 4.0
+        momentum = 0.9 * moment[here, :] + average
+        stage[0, here, :] = momentum
+        stage[1, here, :] = anchor[here, :] - 0.7 * (average + 0.9 * momentum)
+        copies += [
+            start(
+                stage.at[k, here], columns_of(out.at[here], s[at["pieces"]], HEAD), sems.at[3 * n + i]
+            )
+            for i, (k, out) in enumerate(((0, new_moment), (1, new_anchor), (1, inner)))
+        ]
     for copy in copies:
         copy.wait()
 
@@ -394,6 +444,7 @@
     e_perm = [(i, i ^ 2) for i in range(2 * chips)]
     o_perm = [(i, cross(i)) for i in range(2 * chips)]
     swap = [(i, i ^ 1) for i in range(2 * chips)]
+    x_perm, y_perm = [(i, i ^ 1) for i in range(4)], [(i, i ^ 2) for i in range(4)]
 
     values, at = [], {}
 
@@ -404,7 +455,7 @@
     name("z", z)
     name("core", core)
     name("middle", middle)
-    name("heads", *[(head + k) % (columns // HEAD) for k in range(columns // HEAD)])
+    name("pieces", *[block for _, _, block in pieces(head)])
     name("grad", *[2 * (z ^ k) + c for k in range(chips) for c in (core, 1 - core)])
     hops = []
     for step in range(1, chips):
@@ -426,36 +477,40 @@
 
     dma = pltpu.SemaphoreType.DMA
     from_e, from_o = [[]], [[]]
-    heads = columns // HEAD
-    *low, w_v, packed = call(
-        functools.partial(ready_body, at),
+    act_sib, cot_sib = permute(act, swap), permute(cot, swap)
+    (_, first), (offset, part) = PARTS
+    low = [weights[:, :first].astype(BF16)]
+    low += call(
+        functools.partial(cast_body, offset),
         s,
-        [weights, act, cot],
-        [vmem(rows, part, dtype=BF16) for _, part in PARTS]
-        + [vmem(rows, columns), vmem(tokens, chips * rows + columns, dtype=BF16)],
-        [dma((5 * heads + chips,))],
-        us=3.0,
+        [weights],
+        [vmem(rows, part, dtype=BF16)],
+        [vmem(rows, part), dma((2,))],
+        after=[cot_sib],
+        us=2.0,
     )
     for x in low:
         from_e[0].append(permute(x, e_perm))
         from_o[0].append(permute(x, o_perm))
-    packed_sib = permute(packed, swap)
 
     sums_shape = vmem(chips * rows, columns)
+    cot_shape = vmem(tokens, columns, dtype=BF16)
+    block_shape = vmem(chips, tokens, rows, dtype=BF16)
     sums_own, new_anchor, new_momentum = call(
         functools.partial(own_body, at),
         s,
-        [Held(packed), act, anchor, outer_momentum],
+        [act, Held(cot), anchor, outer_momentum],
         [sums_shape, hbm(rows, columns), hbm(rows, columns)],
-        [vmem(chips, tokens, rows, dtype=BF16), vmem(2, rows, columns), dma((chips + 4,))],
+        [block_shape, cot_shape, vmem(2, rows, columns), dma((chips + 7,))],
+        after=low[-1:],
         us=5.0,
     )
-    sums_both, m_v, v_v, anchor_v, moment_v = call(
+    sums_both, w_v, m_v, v_v, anchor_v, moment_v = call(
         functools.partial(sibling_body, at),
         s,
-        [Held(sums_own), Held(packed_sib), moment, second, anchor, outer_momentum],
-        [sums_shape] + [vmem(rows, columns)] * 2 + [vmem(rows, HEAD)] * 2,
-        [dma((2 * heads + 2,))],
+        [Held(sums_own), act_sib, Held(cot_sib), weights, moment, second, anchor, outer_momentum],
+        [sums_shape] + [vmem(rows, columns)] * 3 + [vmem(rows, HEAD)] * 2,
+        [block_shape, cot_shape, dma((chips + 14,))],
         {0: 0},
         us=5.0,
     )
@@ -474,7 +529,7 @@
         )
 
     def grad(which, before, own, after):
-        ins = [Held(x) for x in [packed, packed_sib, *own]]
+        ins = [Held(x) for x in [cot, cot_sib, *own]]
         aliases = {}
         if before is not None:
             theirs, buffer = before
@@ -514,41 +569,55 @@
         picked = found
     grads, token = grad(last, grads, picked, ())
 
-    state, diff, others = None, None, None
-    for j, (offset, part) in enumerate(PARTS):
-        ins = [sums_both, from_e[last][j], from_o[last][j], w_v, m_v, v_v]
-        outs = [hbm(rows, columns)] * 3
-        aliases, after = {}, ()
-        if j == 0:
-            ins += [anchor_v]
-            outs = outs + [vmem(rows, HEAD, dtype=BF16)]
-            after = (token,)
-        ins = [Held(x) for x in ins]
-        if j > 0:
-            aliases = {len(ins) + k: k for k in range(3)}
-            ins += state
-        result = call(
-            functools.partial(adam_body, at, offset),
-            s,
-            ins,
-            outs,
-            [vmem(3, rows, part), dma((3 * rows // TILE * part // HEAD,))],
-            aliases,
-            after,
-            us=2.8,
-        )
-        state = list(result[:3])
-        if j == 0:
-            diff = result[3]
-            others = [permute(diff, [(i, i ^ k) for i in range(4)], "group") for k in (1, 2, 3)]
-    inner, new_anchor, new_momentum, input_grad = call(
+    theirs, input_grad = grads
+    half = vmem(rows // 2, HEAD, dtype=BF16)
+    full = [hbm(rows, columns)] * 3
+
+    def inputs(j):
+        return [sums_both, from_e[last][j], from_o[last][j], w_v, m_v, v_v]
+
+    upper, lower, first_v, second_v = call(
+        functools.partial(head_body, at),
+        s,
+        [Held(x) for x in [*inputs(0), anchor_v]],
+        [half, half, vmem(rows, HEAD), vmem(rows, HEAD)],
+        after=(token,),
+        us=1.0,
+    )
+    upper_in = permute(upper, x_perm, "group")
+    lower_in = permute(lower, y_perm, "group")
+    *state, input_grad, token = call(
+        functools.partial(rest_body, at, HEAD, PARTS[0][1] - HEAD, HEAD),
+        s,
+        [Held(x) for x in [*inputs(0), first_v, second_v, theirs]] + [input_grad],
+        full + [hbm(tokens, width, dtype=BF16), vmem(8, 128)],
+        [vmem(3, rows, PARTS[0][1] - HEAD), dma((3 + 3 * rows // TILE,))],
+        {9: 3},
+        us=2.0,
+    )
+    upper = call(mix_body, s, [Held(upper), Held(upper_in)], [half], after=(token,), us=0.5)[0]
+    upper_in = permute(upper, y_perm, "group")
+    lower = call(mix_body, s, [Held(lower), Held(lower_in)], [half], after=(upper,), us=0.5)[0]
+    lower_in = permute(lower, x_perm, "group")
+    pairs = [upper, upper_in, lower, lower_in]
+    offset, part = PARTS[1]
+    *state, token = call(
+        functools.partial(rest_body, at, offset, part, 0),
+        s,
+        [Held(x) for x in inputs(1)] + state,
+        full + [vmem(8, 128)],
+        [vmem(3, rows, part), dma((3 * rows // TILE,))],
+        {6: 0, 7: 1, 8: 2},
+        after=(lower,),
+        us=3.0,
+    )
+    inner, new_anchor, new_momentum = call(
         functools.partial(outer_body, at),
         s,
-        [Held(x) for x in [diff, *others, anchor_v, moment_v, grads[0]]]
-        + [state[0], new_anchor, new_momentum, grads[1]],
-        [hbm(rows, columns)] * 3 + [hbm(tokens, width, dtype=BF16)],
-        [vmem(2, rows, HEAD), dma((4,))],
-        {7: 0, 8: 1, 9: 2, 10: 3},
+        [Held(x) for x in [*pairs, anchor_v, moment_v]] + [state[0], new_anchor, new_momentum],
+        [hbm(rows, columns)] * 3,
+        [vmem(2, rows, HEAD), dma((6,))],
+        {6: 0, 7: 1, 8: 2},
         us=2.0,
     )
     return input_grad[None], inner[None], state[1][None], state[2][None], new_anchor, new_momentum

time: 111 us -> 103 us (0.928)
  waiting for transfers between devices: 49.6 us -> 35.7 us
  starting transfers between devices: 25.9 us -> 28.8 us
  Pallas kernels: 33.6 us -> 35.1 us
  local copies, waits for them, and re-layouts: 0.12 us -> 1.44 us
    ppermute x24 -> x26, waiting for transfers between devices: 49.6 us -> 35.7 us  [permute(): return lax.ppermute(x, axis, perm)]
    ppermute x24 -> x26, starting transfers between devices: 25.9 us -> 28.8 us  [permute(): return lax.ppermute(x, axis, perm)]
    pallas_call x16 -> x19, Pallas kernels: 33.6 us -> 35.1 us  [call(): pl.pallas_call(inner, in_specs=specs, out_specs=[pl.BlockSpec(memory_spac...]
    slice x0 -> x1, local copies, waits for them, and re-layouts: none -> 1.32 us  [line(): low = [weights[:, :first].astype(BF16)]]
  transfers between devices with their start and end apart: 24 -> 26, of which waited for: 9 -> 9; matrix products, arithmetic and copies ran while one was open for 0% -> 1% of each run, Pallas kernels for 26% -> 32%
where the time goes in v3:
time: 103 us
  waiting for transfers between devices  35.7 us (35%)
  Pallas kernels  35.1 us (34%)
  starting transfers between devices  28.8 us (28%)
  between operations  1.62 us (2%)
  local copies, waits for them, and re-layouts  1.44 us (1%)
    ppermute x26, waiting for transfers between devices, permute(): return lax.ppermute(x, axis, perm)  35.7 us
    pallas_call x19, Pallas kernels, call(): pl.pallas_call(inner, in_specs=specs, out_specs=[pl.BlockSpec(memory_spac...  35.1 us
    ppermute x26, starting transfers between devices, permute(): return lax.ppermute(x, axis, perm)  28.8 us
  transfers between devices with their start and end apart: 26, of which 9 were waited for; matrix products, arithmetic and copies ran while one was open for 1% of the time, Pallas kernels for 32%

profile of v3, /device:TPU:0, one launch (start us, length us, event | category | flops | bytes accessed | tf_op | source)
XLA Modules:
  0.0 102.7 jit_solution(4735154297291579025)
XLA Ops:
  2.6 4.1 %collective-permute-start.3 = (bf16[1024,256]{1,0:T(8,128)(2,1)S(1)}, bf16[1024,256]{1,0:T(8,128)(2,1)S(1)}, u32[]{:S(2)}, u32[]{:S(2)}) collective-permute-start(bf16[1024,256]{1,0:T(8,128)(2,1)S(1)} %slice.7.refs_3_), channel_id=1, source_target_pairs={{0,2},{1,3},{2,0},{3,1},{4,6},{5,7},{6,4},{7,5},{8,10},{9,11},{10,... | collective-permute-start | bytes 1572872 | tf_op jit(solution)/shard_map/ppermute | solution.py:476
  7.5 1.7 %collective-permute-done.refs_2_.refs_3_ = bf16[256,512]{1,0:T(8,128)(2,1)S(1)} collective-permute-done((bf16[256,512]{1,0:T(8,128)(2,1)}, bf16[256,512]{1,0:T(8,128)(2,1)S(1)}, u32[]{:S(2)}, u32[]{:S(2)}) %collective-permute-start) | collective-permute-done | bytes 262176 | tf_op jit(solution)/shard_map/ppermute | solution.py:476
  9.2 1.8 %shard_map.127.refs_5_.refs_4_ = bf16[1024,256]{1,0:T(8,128)(2,1)S(1)} custom-call(s32[26]{0:T(128)S(1)} %stack.107.refs_0_, f32[1024,512]{1,0:T(8,128)} %bitcast.48, bf16[256,512]{1,0:T(8,128)(2,1)S(1)} %collective-permute-done.refs_2_.refs_3_), custom_call_target="tpu_custom_call" | custom-call | bytes 6800000 | tf_op jit(solution)/shard_map/pallas_call | solution.py:104
  11.2 3.7 %collective-permute-start.11 = (bf16[1024,256]{1,0:T(8,128)(2,1)S(1)}, bf16[1024,256]{1,0:T(8,128)(2,1)S(1)}, u32[]{:S(2)}, u32[]{:S(2)}) collective-permute-start(bf16[1024,256]{1,0:T(8,128)(2,1)S(1)} %shard_map.127.refs_5_.refs_4_), channel_id=1, source_target_pairs={{0,2},{1,3},{2,0},{3,1},{4,6},{5,7},{6,4},{7,5},{8,10},{9,11},{10,... | collective-permute-start | bytes 1572872 | tf_op jit(solution)/shard_map/ppermute | solution.py:476
  14.9 5.5 %shard_map.128 = (f32[4096,512]{1,0:T(8,128)S(1)}, f32[1024,512]{1,0:T(8,128)}, f32[1024,512]{1,0:T(8,128)}) custom-call(s32[26]{0:T(128)S(1)} %stack.107.refs_0_, bf16[256,8192]{1,0:T(8,128)(2,1)} %bitcast.52, bf16[256,512]{1,0:T(8,128)(2,1)S(1)} %bitcast.41, f32[1024,512]{1,0:T(8,128)} %refs_7_.1, f32[1024,512]{1,0:T(8,128)} %refs_8_.1, ...), custom_call_target="tpu_custom_call" | custom-call | bytes 17000000 | tf_op jit(solution)/shard_map/pallas_call | solution.py:104
  20.4 4.5 %shard_map.129 = (f32[4096,512]{1,0:T(8,128)S(1)}, f32[1024,512]{1,0:T(8,128)S(1)}, f32[1024,512]{1,0:T(8,128)S(1)}, f32[1024,512]{1,0:T(8,128)S(1)}, f32[1024,128]{1,0:T(8,128)S(1)}, /*index=5*/f32[1024,128]{1,0:T(8,128)S(1)}) custom-call(s32[26]{0:T(128)S(1)} %stack.107.refs_0_, ...), custom_call_target="tpu_custom_call", output_to_operand_aliasing={{0}: (1, {})} | custom-call | bytes 17000000 | tf_op jit(solution)/shard_map/pallas_call | solution.py:104
  25.9 2.0 %collective-permute-start.5 = (bf16[1024,256]{1,0:T(8,128)(2,1)S(1)}, bf16[1024,256]{1,0:T(8,128)(2,1)S(1)}, u32[]{:S(2)}, u32[]{:S(2)}) collective-permute-start(bf16[1024,256]{1,0:T(8,128)(2,1)S(1)} %get-tuple-element.63.refs_5_), channel_id=1, source_target_pairs={{0,2},{1,3},{2,0},{3,1},{4,6},{5,7},{6,4},{7,5},{8,10},{9,11},{10,... | collective-permute-start | bytes 1572872 | tf_op jit(solution)/shard_map/ppermute | solution.py:476
  28.0 2.1 %shard_map.133 = (bf16[256,1024]{1,0:T(8,128)(2,1)S(1)}, bf16[256,8192]{1,0:T(8,128)(2,1)}, f32[8,128]{1,0:T(8,128)S(1)}) custom-call(s32[26]{0:T(128)S(1)} %stack.107.refs_0_, bf16[256,512]{1,0:T(8,128)(2,1)S(1)} %bitcast.42, bf16[256,512]{1,0:T(8,128)(2,1)S(1)} %collective-permute-done.refs_2_.refs_3_, bf16[1024,256]{1,0:T(8,128)(2,1)S(1)} %slice.7.refs_3_, ...), custom_call_target="tpu_custom_call" | custom-call | bytes 7140000 | tf_op jit(solution)/shard_map/pallas_call | solution.py:104
  31.6 2.5 %collective-permute-start.13 = (bf16[1024,256]{1,0:T(8,128)(2,1)S(1)}, bf16[1024,256]{1,0:T(8,128)(2,1)S(1)}, u32[]{:S(2)}, u32[]{:S(2)}) collective-permute-start(bf16[1024,256]{1,0:T(8,128)(2,1)S(1)} %get-tuple-element.75), channel_id=1, source_target_pairs={{0,2},{1,3},{2,0},{3,1},{4,6},{5,7},{6,4},{7,5},{8,10},{9,11},{10,... | collective-permute-start | bytes 1572872 | tf_op jit(solution)/shard_map/ppermute | solution.py:476
  34.1 7.8 %collective-permute-done.5.refs_3_ = bf16[1024,256]{1,0:T(8,128)(2,1)S(1)} collective-permute-done((bf16[1024,256]{1,0:T(8,128)(2,1)S(1)}, bf16[1024,256]{1,0:T(8,128)(2,1)S(1)}, u32[]{:S(2)}, u32[]{:S(2)}) %collective-permute-start.5) | collective-permute-done | bytes 524320 | tf_op jit(solution)/shard_map/ppermute | solution.py:476
  42.9 2.5 %collective-permute-start.7 = (bf16[1024,256]{1,0:T(8,128)(2,1)S(1)}, bf16[1024,256]{1,0:T(8,128)(2,1)S(1)}, u32[]{:S(2)}, u32[]{:S(2)}) collective-permute-start(bf16[1024,256]{1,0:T(8,128)(2,1)S(1)} %get-tuple-element.65.refs_7_), channel_id=1, source_target_pairs={{0,2},{1,3},{2,0},{3,1},{4,6},{5,7},{6,4},{7,5},{8,10},{9,11},{10,... | collective-permute-start | bytes 1572872 | tf_op jit(solution)/shard_map/ppermute | solution.py:476
  45.4 2.1 %shard_map.135 = (bf16[256,1024]{1,0:T(8,128)(2,1)S(1)}, bf16[256,8192]{1,0:T(8,128)(2,1)}, f32[8,128]{1,0:T(8,128)S(1)}) custom-call(s32[26]{0:T(128)S(1)} %stack.107.refs_0_, bf16[256,512]{1,0:T(8,128)(2,1)S(1)} %bitcast.43, bf16[256,512]{1,0:T(8,128)(2,1)S(1)} %collective-permute-done.refs_2_.refs_3_, ...), custom_call_target="tpu_custom_call", output_to_operand_aliasing={{1}: (6, {})} | custom-call | bytes 7140000 | tf_op jit(solution)/shard_map/pallas_call | solution.py:104
  47.6 5.5 %collective-permute-done.13.refs_3_ = bf16[1024,256]{1,0:T(8,128)(2,1)S(1)} collective-permute-done((bf16[1024,256]{1,0:T(8,128)(2,1)S(1)}, bf16[1024,256]{1,0:T(8,128)(2,1)S(1)}, u32[]{:S(2)}, u32[]{:S(2)}) %collective-permute-start.13) | collective-permute-done | bytes 524320 | tf_op jit(solution)/shard_map/ppermute | solution.py:476
  54.1 2.5 %collective-permute-start.16 = (bf16[1024,256]{1,0:T(8,128)(2,1)S(1)}, bf16[1024,256]{1,0:T(8,128)(2,1)S(1)}, u32[]{:S(2)}, u32[]{:S(2)}) collective-permute-start(bf16[1024,256]{1,0:T(8,128)(2,1)S(1)} %get-tuple-element.82), channel_id=1, source_target_pairs={{0,2},{1,3},{2,0},{3,1},{4,6},{5,7},{6,4},{7,5},{8,10},{9,11},{10,... | collective-permute-start | bytes 1572872 | tf_op jit(solution)/shard_map/ppermute | solution.py:476
  56.6 7.7 %collective-permute-done.7.refs_3_ = bf16[1024,256]{1,0:T(8,128)(2,1)S(1)} collective-permute-done((bf16[1024,256]{1,0:T(8,128)(2,1)S(1)}, bf16[1024,256]{1,0:T(8,128)(2,1)S(1)}, u32[]{:S(2)}, u32[]{:S(2)}) %collective-permute-start.7) | collective-permute-done | bytes 524320 | tf_op jit(solution)/shard_map/ppermute | solution.py:476
  65.3 2.1 %shard_map.137 = (bf16[256,1024]{1,0:T(8,128)(2,1)S(1)}, bf16[256,8192]{1,0:T(8,128)(2,1)}, f32[8,128]{1,0:T(8,128)S(1)}) custom-call(s32[26]{0:T(128)S(1)} %stack.107.refs_0_, bf16[256,512]{1,0:T(8,128)(2,1)S(1)} %bitcast.44, bf16[256,512]{1,0:T(8,128)(2,1)S(1)} %collective-permute-done.refs_2_.refs_3_, ...), custom_call_target="tpu_custom_call", output_to_operand_aliasing={{1}: (6, {})} | custom-call | bytes 7140000 | tf_op jit(solution)/shard_map/pallas_call | solution.py:104
  67.5 2.2 %collective-permute-start.8 = (bf16[1024,256]{1,0:T(8,128)(2,1)S(1)}, bf16[1024,256]{1,0:T(8,128)(2,1)S(1)}, u32[]{:S(2)}, u32[]{:S(2)}) collective-permute-start(bf16[1024,256]{1,0:T(8,128)(2,1)S(1)} %get-tuple-element.66.refs_7_), channel_id=1, source_target_pairs={{0,2},{1,3},{2,0},{3,1},{4,6},{5,7},{6,4},{7,5},{8,10},{9,11},{10,... | collective-permute-start | bytes 1572872 | tf_op jit(solution)/shard_map/ppermute | solution.py:476
  69.9 5.7 %collective-permute-done.16.refs_3_ = bf16[1024,256]{1,0:T(8,128)(2,1)S(1)} collective-permute-done((bf16[1024,256]{1,0:T(8,128)(2,1)S(1)}, bf16[1024,256]{1,0:T(8,128)(2,1)S(1)}, u32[]{:S(2)}, u32[]{:S(2)}) %collective-permute-start.16) | collective-permute-done | bytes 524320 | tf_op jit(solution)/shard_map/ppermute | solution.py:476
  76.5 2.1 %shard_map.139 = (bf16[256,1024]{1,0:T(8,128)(2,1)S(1)}, bf16[256,8192]{1,0:T(8,128)(2,1)}, f32[8,128]{1,0:T(8,128)S(1)}) custom-call(s32[26]{0:T(128)S(1)} %stack.107.refs_0_, bf16[256,512]{1,0:T(8,128)(2,1)S(1)} %bitcast.45, bf16[256,512]{1,0:T(8,128)(2,1)S(1)} %collective-permute-done.refs_2_.refs_3_, ...), custom_call_target="tpu_custom_call", output_to_operand_aliasing={{1}: (6, {})} | custom-call | bytes 7140000 | tf_op jit(solution)/shard_map/pallas_call | solution.py:104
  78.7 2.2 %collective-permute-start.24 = (bf16[1024,256]{1,0:T(8,128)(2,1)S(1)}, bf16[1024,256]{1,0:T(8,128)(2,1)S(1)}, u32[]{:S(2)}, u32[]{:S(2)}) collective-permute-start(bf16[1024,256]{1,0:T(8,128)(2,1)S(1)} %get-tuple-element.101), channel_id=1, source_target_pairs={{0,2},{1,3},{2,0},{3,1},{4,6},{5,7},{6,4},{7,5},{8,10},{9,11},{10,... | collective-permute-start | bytes 1572872 | tf_op jit(solution)/shard_map/ppermute | solution.py:476
  81.1 5.7 %collective-permute-done.8.refs_2_ = bf16[1024,256]{1,0:T(8,128)(2,1)S(1)} collective-permute-done((bf16[1024,256]{1,0:T(8,128)(2,1)S(1)}, bf16[1024,256]{1,0:T(8,128)(2,1)S(1)}, u32[]{:S(2)}, u32[]{:S(2)}) %collective-permute-start.8) | collective-permute-done | bytes 524320 | tf_op jit(solution)/shard_map/ppermute | solution.py:476
  91.0 2.3 %shard_map.141 = (f32[1024,512]{1,0:T(8,128)}, f32[1024,512]{1,0:T(8,128)}, f32[1024,512]{1,0:T(8,128)}, bf16[256,8192]{1,0:T(8,128)(2,1)}, f32[8,128]{1,0:T(8,128)S(1)}) custom-call(s32[26]{0:T(128)S(1)} %stack.107.refs_0_, f32[4096,512]{1,0:T(8,128)S(1)} %get-tuple-element.61.refs_1_, ...), custom_call_target="tpu_custom_call", output_to_operand_aliasing={{3}: (10, {})} | custom-call | bytes 6800000 | tf_op jit(solution)/shard_map/pallas_call | solution.py:104
  97.7 3.1 %shard_map.144 = (f32[1024,512]{1,0:T(8,128)}, f32[1024,512]{1,0:T(8,128)}, f32[1024,512]{1,0:T(8,128)}, f32[8,128]{1,0:T(8,128)}) custom-call(s32[26]{0:T(128)S(1)} %stack.107.refs_0_, f32[4096,512]{1,0:T(8,128)S(1)} %get-tuple-element.61.refs_1_, ...), custom_call_target="tpu_custom_call", output_to_operand_aliasing={{0}: (7, {}), {1}: (8, {}), {2}: (9, {})} | custom-call | bytes 10200000 | tf_op jit(solution)/shard_map/pallas_call | solution.py:104
  100.8 1.8 %shard_map.145 = (f32[1024,512]{1,0:T(8,128)}, f32[1024,512]{1,0:T(8,128)}, f32[1024,512]{1,0:T(8,128)}) custom-call(s32[26]{0:T(128)S(1)} %stack.107.refs_0_, bf16[512,128]{1,0:T(8,128)(2,1)S(1)} %shard_map.142.refs_3_.refs_1_, bf16[512,128]{1,0:T(8,128)(2,1)S(1)} %collective-permute-done.21.refs_2_, ...), custom_call_target="tpu_custom_call", output_to_operand_aliasing={{0}: (7, {}), {1}: (8, {}), {2}: (9, {})} | custom-call | bytes 6800000 | tf_op jit(solution)/shard_map/pallas_call | solution.py:104
  (51 shorter events, 17.6 us)
Async XLA Ops:
  0.6 19.8 %collective-permute-start.1 = (bf16[256,8192]{1,0:T(8,128)(2,1)}, bf16[256,8192]{1,0:T(8,128)(2,1)}, u32[]{:S(2)}, u32[]{:S(2)}) collective-permute-start(bf16[256,8192]{1,0:T(8,128)(2,1)} %bitcast.51), channel_id=1, source_target_pairs={{0,1},{1,0},{2,3},{3,2},{4,5},{5,4},{6,7},{7,6},{8,9},{9,8},{10,11... | collective-permute-start | bytes 12582920 | tf_op jit(solution)/shard_map/ppermute | solution.py:476
  2.5 22.4 %collective-permute-start.2 = (bf16[1024,256]{1,0:T(8,128)(2,1)S(1)}, bf16[1024,256]{1,0:T(8,128)(2,1)S(1)}, u32[]{:S(2)}, u32[]{:S(2)}) collective-permute-start(bf16[1024,256]{1,0:T(8,128)(2,1)S(1)} %slice.7.refs_3_), channel_id=1, source_target_pairs={{0,1},{1,0},{2,4},{3,5},{4,2},{5,3},{6,7},{7,6},{8,9},{9,8},{10,12... | collective-permute-start | bytes 1572872 | tf_op jit(solution)/shard_map/ppermute | solution.py:476
  2.6 22.3 %collective-permute-start.3 = (bf16[1024,256]{1,0:T(8,128)(2,1)S(1)}, bf16[1024,256]{1,0:T(8,128)(2,1)S(1)}, u32[]{:S(2)}, u32[]{:S(2)}) collective-permute-start(bf16[1024,256]{1,0:T(8,128)(2,1)S(1)} %slice.7.refs_3_), channel_id=1, source_target_pairs={{0,2},{1,3},{2,0},{3,1},{4,6},{5,7},{6,4},{7,5},{8,10},{9,11},{10,... | collective-permute-start | bytes 1572872 | tf_op jit(solution)/shard_map/ppermute | solution.py:476
  11.0 19.1 %collective-permute-start.10 = (bf16[1024,256]{1,0:T(8,128)(2,1)S(1)}, bf16[1024,256]{1,0:T(8,128)(2,1)S(1)}, u32[]{:S(2)}, u32[]{:S(2)}) collective-permute-start(bf16[1024,256]{1,0:T(8,128)(2,1)S(1)} %shard_map.127.refs_5_.refs_4_), channel_id=1, source_target_pairs={{0,1},{1,0},{2,4},{3,5},{4,2},{5,3},{6,7},{7,6},{8,9},{9,8},{10,12... | collective-permute-start | bytes 1572872 | tf_op jit(solution)/shard_map/ppermute | solution.py:476
  11.2 19.4 %collective-permute-start.11 = (bf16[1024,256]{1,0:T(8,128)(2,1)S(1)}, bf16[1024,256]{1,0:T(8,128)(2,1)S(1)}, u32[]{:S(2)}, u32[]{:S(2)}) collective-permute-start(bf16[1024,256]{1,0:T(8,128)(2,1)S(1)} %shard_map.127.refs_5_.refs_4_), channel_id=1, source_target_pairs={{0,2},{1,3},{2,0},{3,1},{4,6},{5,7},{6,4},{7,5},{8,10},{9,11},{10,... | collective-permute-start | bytes 1572872 | tf_op jit(solution)/shard_map/ppermute | solution.py:476
  25.8 8.2 %collective-permute-start.4 = (bf16[1024,256]{1,0:T(8,128)(2,1)S(1)}, bf16[1024,256]{1,0:T(8,128)(2,1)S(1)}, u32[]{:S(2)}, u32[]{:S(2)}) collective-permute-start(bf16[1024,256]{1,0:T(8,128)(2,1)S(1)} %get-tuple-element.62), channel_id=1, source_target_pairs={{0,1},{1,0},{2,4},{3,5},{4,2},{5,3},{6,7},{7,6},{8,9},{9,8},{10,12... | collective-permute-start | bytes 1572872 | tf_op jit(solution)/shard_map/ppermute | solution.py:476
  25.9 16.0 %collective-permute-start.5 = (bf16[1024,256]{1,0:T(8,128)(2,1)S(1)}, bf16[1024,256]{1,0:T(8,128)(2,1)S(1)}, u32[]{:S(2)}, u32[]{:S(2)}) collective-permute-start(bf16[1024,256]{1,0:T(8,128)(2,1)S(1)} %get-tuple-element.63.refs_5_), channel_id=1, source_target_pairs={{0,2},{1,3},{2,0},{3,1},{4,6},{5,7},{6,4},{7,5},{8,10},{9,11},{10,... | collective-permute-start | bytes 1572872 | tf_op jit(solution)/shard_map/ppermute | solution.py:476
  30.1 15.3 %collective-permute-start.14 = (bf16[256,1024]{1,0:T(8,128)(2,1)S(1)}, bf16[256,1024]{1,0:T(8,128)(2,1)S(1)}, u32[]{:S(2)}, u32[]{:S(2)}) collective-permute-start(bf16[256,1024]{1,0:T(8,128)(2,1)S(1)} %get-tuple-element.78), channel_id=1, source_target_pairs={{0,1},{1,0},{2,3},{3,2},{4,5},{5,4},{6,7},{7,6},{8,9},{9,8},{10,11... | collective-permute-start | bytes 1572872 | tf_op jit(solution)/shard_map/ppermute | solution.py:476
  31.5 16.1 %collective-permute-start.12 = (bf16[1024,256]{1,0:T(8,128)(2,1)S(1)}, bf16[1024,256]{1,0:T(8,128)(2,1)S(1)}, u32[]{:S(2)}, u32[]{:S(2)}) collective-permute-start(bf16[1024,256]{1,0:T(8,128)(2,1)S(1)} %get-tuple-element.74), channel_id=1, source_target_pairs={{0,1},{1,0},{2,4},{3,5},{4,2},{5,3},{6,7},{7,6},{8,9},{9,8},{10,12... | collective-permute-start | bytes 1572872 | tf_op jit(solution)/shard_map/ppermute | solution.py:476
  31.6 21.5 %collective-permute-start.13 = (bf16[1024,256]{1,0:T(8,128)(2,1)S(1)}, bf16[1024,256]{1,0:T(8,128)(2,1)S(1)}, u32[]{:S(2)}, u32[]{:S(2)}) collective-permute-start(bf16[1024,256]{1,0:T(8,128)(2,1)S(1)} %get-tuple-element.75), channel_id=1, source_target_pairs={{0,2},{1,3},{2,0},{3,1},{4,6},{5,7},{6,4},{7,5},{8,10},{9,11},{10,... | collective-permute-start | bytes 1572872 | tf_op jit(solution)/shard_map/ppermute | solution.py:476
  42.8 13.8 %collective-permute-start.6 = (bf16[1024,256]{1,0:T(8,128)(2,1)S(1)}, bf16[1024,256]{1,0:T(8,128)(2,1)S(1)}, u32[]{:S(2)}, u32[]{:S(2)}) collective-permute-start(bf16[1024,256]{1,0:T(8,128)(2,1)S(1)} %get-tuple-element.64), channel_id=1, source_target_pairs={{0,1},{1,0},{2,4},{3,5},{4,2},{5,3},{6,7},{7,6},{8,9},{9,8},{10,12... | collective-permute-start | bytes 1572872 | tf_op jit(solution)/shard_map/ppermute | solution.py:476
  42.9 21.5 %collective-permute-start.7 = (bf16[1024,256]{1,0:T(8,128)(2,1)S(1)}, bf16[1024,256]{1,0:T(8,128)(2,1)S(1)}, u32[]{:S(2)}, u32[]{:S(2)}) collective-permute-start(bf16[1024,256]{1,0:T(8,128)(2,1)S(1)} %get-tuple-element.65.refs_7_), channel_id=1, source_target_pairs={{0,2},{1,3},{2,0},{3,1},{4,6},{5,7},{6,4},{7,5},{8,10},{9,11},{10,... | collective-permute-start | bytes 1572872 | tf_op jit(solution)/shard_map/ppermute | solution.py:476
  47.5 17.8 %collective-permute-start.17 = (bf16[256,1024]{1,0:T(8,128)(2,1)S(1)}, bf16[256,1024]{1,0:T(8,128)(2,1)S(1)}, u32[]{:S(2)}, u32[]{:S(2)}) collective-permute-start(bf16[256,1024]{1,0:T(8,128)(2,1)S(1)} %get-tuple-element.85), channel_id=1, source_target_pairs={{0,1},{1,0},{2,3},{3,2},{4,5},{5,4},{6,7},{7,6},{8,9},{9,8},{10,11... | collective-permute-start | bytes 1572872 | tf_op jit(solution)/shard_map/ppermute | solution.py:476
  54.0 15.8 %collective-permute-start.15 = (bf16[1024,256]{1,0:T(8,128)(2,1)S(1)}, bf16[1024,256]{1,0:T(8,128)(2,1)S(1)}, u32[]{:S(2)}, u32[]{:S(2)}) collective-permute-start(bf16[1024,256]{1,0:T(8,128)(2,1)S(1)} %get-tuple-element.81), channel_id=1, source_target_pairs={{0,1},{1,0},{2,4},{3,5},{4,2},{5,3},{6,7},{7,6},{8,9},{9,8},{10,12... | collective-permute-start | bytes 1572872 | tf_op jit(solution)/shard_map/ppermute | solution.py:476
  54.1 21.5 %collective-permute-start.16 = (bf16[1024,256]{1,0:T(8,128)(2,1)S(1)}, bf16[1024,256]{1,0:T(8,128)(2,1)S(1)}, u32[]{:S(2)}, u32[]{:S(2)}) collective-permute-start(bf16[1024,256]{1,0:T(8,128)(2,1)S(1)} %get-tuple-element.82), channel_id=1, source_target_pairs={{0,2},{1,3},{2,0},{3,1},{4,6},{5,7},{6,4},{7,5},{8,10},{9,11},{10,... | collective-permute-start | bytes 1572872 | tf_op jit(solution)/shard_map/ppermute | solution.py:476
  67.4 9.1 %collective-permute-start.18 = (bf16[256,1024]{1,0:T(8,128)(2,1)S(1)}, bf16[256,1024]{1,0:T(8,128)(2,1)S(1)}, u32[]{:S(2)}, u32[]{:S(2)}) collective-permute-start(bf16[256,1024]{1,0:T(8,128)(2,1)S(1)} %get-tuple-element.89), channel_id=1, source_target_pairs={{0,1},{1,0},{2,3},{3,2},{4,5},{5,4},{6,7},{7,6},{8,9},{9,8},{10,11... | collective-permute-start | bytes 1572872 | tf_op jit(solution)/shard_map/ppermute | solution.py:476
  67.5 19.3 %collective-permute-start.8 = (bf16[1024,256]{1,0:T(8,128)(2,1)S(1)}, bf16[1024,256]{1,0:T(8,128)(2,1)S(1)}, u32[]{:S(2)}, u32[]{:S(2)}) collective-permute-start(bf16[1024,256]{1,0:T(8,128)(2,1)S(1)} %get-tuple-element.66.refs_7_), channel_id=1, source_target_pairs={{0,2},{1,3},{2,0},{3,1},{4,6},{5,7},{6,4},{7,5},{8,10},{9,11},{10,... | collective-permute-start | bytes 1572872 | tf_op jit(solution)/shard_map/ppermute | solution.py:476
  69.7 17.1 %collective-permute-start.9 = (bf16[1024,256]{1,0:T(8,128)(2,1)S(1)}, bf16[1024,256]{1,0:T(8,128)(2,1)S(1)}, u32[]{:S(2)}, u32[]{:S(2)}) collective-permute-start(bf16[1024,256]{1,0:T(8,128)(2,1)S(1)} %get-tuple-element.67), channel_id=1, source_target_pairs={{0,1},{1,0},{2,4},{3,5},{4,2},{5,3},{6,7},{7,6},{8,9},{9,8},{10,12... | collective-permute-start | bytes 1572872 | tf_op jit(solution)/shard_map/ppermute | solution.py:476
  78.6 12.4 %collective-permute-start.19 = (bf16[256,1024]{1,0:T(8,128)(2,1)S(1)}, bf16[256,1024]{1,0:T(8,128)(2,1)S(1)}, u32[]{:S(2)}, u32[]{:S(2)}) collective-permute-start(bf16[256,1024]{1,0:T(8,128)(2,1)S(1)} %get-tuple-element.94), channel_id=1, source_target_pairs={{0,1},{1,0},{2,3},{3,2},{4,5},{5,4},{6,7},{7,6},{8,9},{9,8},{10,11... | collective-permute-start | bytes 1572872 | tf_op jit(solution)/shard_map/ppermute | solution.py:476
  78.7 18.9 %collective-permute-start.24 = (bf16[1024,256]{1,0:T(8,128)(2,1)S(1)}, bf16[1024,256]{1,0:T(8,128)(2,1)S(1)}, u32[]{:S(2)}, u32[]{:S(2)}) collective-permute-start(bf16[1024,256]{1,0:T(8,128)(2,1)S(1)} %get-tuple-element.101), channel_id=1, source_target_pairs={{0,2},{1,3},{2,0},{3,1},{4,6},{5,7},{6,4},{7,5},{8,10},{9,11},{10,... | collective-permute-start | bytes 1572872 | tf_op jit(solution)/shard_map/ppermute | solution.py:476
  80.9 16.7 %collective-permute-start.25 = (bf16[1024,256]{1,0:T(8,128)(2,1)S(1)}, bf16[1024,256]{1,0:T(8,128)(2,1)S(1)}, u32[]{:S(2)}, u32[]{:S(2)}) collective-permute-start(bf16[1024,256]{1,0:T(8,128)(2,1)S(1)} %get-tuple-element.102), channel_id=1, source_target_pairs={{0,1},{1,0},{2,4},{3,5},{4,2},{5,3},{6,7},{7,6},{8,9},{9,8},{10,12... | collective-permute-start | bytes 1572872 | tf_op jit(solution)/shard_map/ppermute | solution.py:476
  87.9 5.4 %collective-permute-start.20 = (bf16[512,128]{1,0:T(8,128)(2,1)S(1)}, bf16[512,128]{1,0:T(8,128)(2,1)S(1)}, u32[]{:S(2)}, u32[]{:S(2)}) collective-permute-start(bf16[512,128]{1,0:T(8,128)(2,1)S(1)} %get-tuple-element.97.refs_1_), channel_id=1, source_target_pairs={{0,8},{8,0},{16,24},{24,16},{1,9},{9,1},{17,25},{25,17},{2,10},{10... | collective-permute-start | bytes 393224 | tf_op jit(solution)/shard_map/ppermute | solution.py:476
  95.0 5.8 %collective-permute-start.23 = (bf16[512,128]{1,0:T(8,128)(2,1)S(1)}, bf16[512,128]{1,0:T(8,128)(2,1)S(1)}, u32[]{:S(2)}, u32[]{:S(2)}) collective-permute-start(bf16[512,128]{1,0:T(8,128)(2,1)S(1)} %shard_map.143.refs_10_.refs_3_), channel_id=1, source_target_pairs={{0,8},{8,0},{16,24},{24,16},{1,9},{9,1},{17,25},{25,17},{2,10},{10... | collective-permute-start | bytes 393224 | tf_op jit(solution)/shard_map/ppermute | solution.py:476
  95.7 5.1 %collective-permute-start.21 = (bf16[512,128]{1,0:T(8,128)(2,1)S(1)}, bf16[512,128]{1,0:T(8,128)(2,1)S(1)}, u32[]{:S(2)}, u32[]{:S(2)}) collective-permute-start(bf16[512,128]{1,0:T(8,128)(2,1)S(1)} %shard_map.142.refs_3_.refs_1_), channel_id=1, source_target_pairs={{0,16},{8,24},{16,0},{24,8},{1,17},{9,25},{17,1},{25,9},{2,18},{10... | collective-permute-start | bytes 393224 | tf_op jit(solution)/shard_map/ppermute | solution.py:476
  (3 other events, 21.2 us)

commit v4 on v3

--- a/solution.py
+++ b/solution.py
@@ -356,6 +356,7 @@
 def rest_body(at, offset, part, within, s, sums_ref, from_e, from_o, w, m, v, *rest):
     stage, sems = rest[-2:]
     rows = from_e.shape[0]
+    tiles = rows // TILE
     copies = []
     if within:
         first_v, second_v, theirs = rest[:3]
@@ -364,21 +365,26 @@
             there = columns_of(outs[1 + k], s[at["pieces"]], HEAD)
             copies.append(start(src, there, sems.at[k]))
         copies.append(start(theirs, columns_of(grads, s[at["grad"] + 7], rows), sems.at[2]))
+        token[...] = jnp.zeros_like(token)
     else:
-        *outs, token = rest[3:-2]
-    token[...] = jnp.zeros_like(token)
+        tiles -= 1
+        *outs, left = rest[3:-2]
     piece = next(k for k, (column, *_) in enumerate(pieces(0)) if column == offset)
-
-    def put(r, stepped, first, second):
-        here = pl.ds(r, stepped.shape[0])
-        stage[0, here, :] = stepped
-        stage[1, here, :] = first
-        stage[2, here, :] = second
-
-    for tile in range(rows // TILE):
-        args = (from_e, from_o, w, m, v, put, TILE, part, slice(within, within + part))
-        adam(at, offset, tile * TILE, s, sums_ref, *args)
-        there = pl.ds(tile * TILE, TILE)
+    args = (from_e, from_o, w, m, v)
+    taken = slice(within, within + part)
+
+    def putter(refs, top):
+        def put(r, *values):
+            here = pl.ds(r - top, values[0].shape[0])
+            for k, value in enumerate(values):
+                refs[k, here, :] = value
+
+        return put
+
+    for tile in range(tiles):
+        first = tile * TILE
+        adam(at, offset, first, s, sums_ref, *args, putter(stage, 0), TILE, part, taken)
+        there = pl.ds(first, TILE)
         for k, out in enumerate(outs):
             copies.append(
                 start(
@@ -387,30 +393,42 @@
                     sems.at[len(copies)],
                 )
             )
+    if not within:
+        first = tiles * TILE
+        adam(at, offset, first, s, sums_ref, *args, putter(left, first), TILE, part, taken)
     for copy in copies:
         copy.wait()
 
 
-def mix_body(s, own, other, out):
-    out[...] = (own[...].astype(F32) + other[...].astype(F32)).astype(BF16)
-
-
-def outer_body(at, s, upper, upper_in, lower, lower_in, anchor, moment, *rest):
-    inner, new_anchor, new_moment, stage, sems = rest[3:]
-    half = upper.shape[0]
+def mix(own, other, token):
+    return (own.astype(F32) + other.astype(F32) + token[:1]).astype(BF16)
+
+
+def outer_body(at, s, left, upper, upper_in, lower, lower_in, anchor, moment, *rest):
+    inner, first, second, new_anchor, new_moment, stage, sems = rest[5:]
+    rows = anchor.shape[0]
+    _, count, part = left.shape
+    there = pl.ds(rows - count, count)
     copies = []
+    for k, out in enumerate((inner, first, second)):
+        last = columns_of(out.at[there], s[at["pieces"] + 2], part)
+        copies.append(start(left.at[k], last, sems.at[k]))
+    half = rows // 2
+    size = 128
     for n, (own, other) in enumerate(((upper, upper_in), (lower, lower_in))):
-        here = pl.ds(n * half, half)
-        average = (own[...].astype(F32) + other[...].astype(F32)) / 4.0
-        momentum = 0.9 * moment[here, :] + average
-        stage[0, here, :] = momentum
-        stage[1, here, :] = anchor[here, :] - 0.7 * (average + 0.9 * momentum)
-        copies += [
-            start(
-                stage.at[k, here], columns_of(out.at[here], s[at["pieces"]], HEAD), sems.at[3 * n + i]
-            )
-            for i, (k, out) in enumerate(((0, new_moment), (1, new_anchor), (1, inner)))
-        ]
+
+        @pl.loop(0, half // size)
+        def _(i):
+            r = pl.multiple_of(i * size, size)
+            here, there = pl.ds(r, size), pl.ds(n * half + r, size)
+            average = (own[here, :].astype(F32) + other[here, :].astype(F32)) / 4.0
+            momentum = 0.9 * moment[there, :] + average
+            stage[0, there, :] = momentum
+            stage[1, there, :] = anchor[there, :] - 0.7 * (average + 0.9 * momentum)
+
+    for k, out in ((0, new_moment), (1, new_anchor), (1, inner)):
+        columns = columns_of(out, s[at["pieces"]], HEAD)
+        copies.append(start(stage.at[k], columns, sems.at[len(copies)]))
     for copy in copies:
         copy.wait()
 
@@ -595,32 +613,38 @@
         {9: 3},
         us=2.0,
     )
-    upper = call(mix_body, s, [Held(upper), Held(upper_in)], [half], after=(token,), us=0.5)[0]
+    upper, lower = mix(upper, upper_in, token), mix(lower, lower_in, token)
     upper_in = permute(upper, y_perm, "group")
-    lower = call(mix_body, s, [Held(lower), Held(lower_in)], [half], after=(upper,), us=0.5)[0]
     lower_in = permute(lower, x_perm, "group")
-    pairs = [upper, upper_in, lower, lower_in]
     offset, part = PARTS[1]
-    *state, token = call(
+    *state, left = call(
         functools.partial(rest_body, at, offset, part, 0),
         s,
         [Held(x) for x in inputs(1)] + state,
-        full + [vmem(8, 128)],
+        full + [vmem(3, TILE, part)],
         [vmem(3, rows, part), dma((3 * rows // TILE,))],
         {6: 0, 7: 1, 8: 2},
-        after=(lower,),
-        us=3.0,
-    )
-    inner, new_anchor, new_momentum = call(
+        after=(upper, lower),
+        us=2.4,
+    )
+    held = [left, upper, upper_in, lower, lower_in, anchor_v, moment_v]
+    inner, new_first, new_second, new_anchor, new_momentum = call(
         functools.partial(outer_body, at),
         s,
-        [Held(x) for x in [*pairs, anchor_v, moment_v]] + [state[0], new_anchor, new_momentum],
-        [hbm(rows, columns)] * 3,
+        [Held(x) for x in held] + [*state, new_anchor, new_momentum],
+        [hbm(rows, columns)] * 5,
         [vmem(2, rows, HEAD), dma((6,))],
-        {6: 0, 7: 1, 8: 2},
+        {len(held) + k: k for k in range(5)},
         us=2.0,
     )
-    return input_grad[None], inner[None], state[1][None], state[2][None], new_anchor, new_momentum
+    return (
+        input_grad[None],
+        inner[None],
+        new_first[None],
+        new_second[None],
+        new_anchor,
+        new_momentum,
+    )
 
 
 def solution(mesh):

time: 103 us -> 102 us (level)
  Pallas kernels: 35.1 us -> 33.3 us
  waiting for transfers between devices: 35.7 us -> 36.9 us
    pallas_call x19 -> x17, Pallas kernels: 35.1 us -> 33.3 us  [call(): pl.pallas_call(inner, in_specs=specs, out_specs=[pl.BlockSpec(memory_spac...]
    ppermute x26, waiting for transfers between devices: 35.7 us -> 36.9 us  [permute(): return lax.ppermute(x, axis, perm)]
  transfers between devices with their start and end apart: 26 -> 26, of which waited for: 9 -> 10; matrix products, arithmetic and copies ran while one was open for 1% -> 2% of each run, Pallas kernels for 32% -> 31%
where the time goes in v4:
time: 102 us
  waiting for transfers between devices  36.9 us (36%)
  Pallas kernels  33.3 us (33%)
  starting transfers between devices  28.7 us (28%)
  between operations  1.72 us (2%)
  local copies, waits for them, and re-layouts  1.45 us (1%)
    ppermute x26, waiting for transfers between devices, permute(): return lax.ppermute(x, axis, perm)  36.9 us
    pallas_call x17, Pallas kernels, call(): pl.pallas_call(inner, in_specs=specs, out_specs=[pl.BlockSpec(memory_spac...  33.3 us
    ppermute x26, starting transfers between devices, permute(): return lax.ppermute(x, axis, perm)  28.7 us
  transfers between devices with their start and end apart: 26, of which 10 were waited for; matrix products, arithmetic and copies ran while one was open for 2% of the time, Pallas kernels for 31%

profile of v4, /device:TPU:0, one launch (start us, length us, event | category | flops | bytes accessed | tf_op | source)
XLA Modules:
  0.0 102.1 jit_solution(3723114032333371114)
XLA Ops:
  2.6 4.1 %collective-permute-start.3 = (bf16[1024,256]{1,0:T(8,128)(2,1)S(1)}, bf16[1024,256]{1,0:T(8,128)(2,1)S(1)}, u32[]{:S(2)}, u32[]{:S(2)}) collective-permute-start(bf16[1024,256]{1,0:T(8,128)(2,1)S(1)} %slice.13.refs_3_), channel_id=1, source_target_pairs={{0,2},{1,3},{2,0},{3,1},{4,6},{5,7},{6,4},{7,5},{8,10},{9,11},{10,... | collective-permute-start | bytes 1572872 | tf_op jit(solution)/shard_map/ppermute | solution.py:494
  9.2 1.8 %shard_map.127.refs_5_.refs_4_ = bf16[1024,256]{1,0:T(8,128)(2,1)S(1)} custom-call(s32[26]{0:T(128)S(1)} %stack.107.refs_0_, f32[1024,512]{1,0:T(8,128)} %bitcast.50, bf16[256,512]{1,0:T(8,128)(2,1)S(1)} %collective-permute-done.refs_2_.refs_3_), custom_call_target="tpu_custom_call" | custom-call | bytes 6800000 | tf_op jit(solution)/shard_map/pallas_call | solution.py:104
  11.2 3.7 %collective-permute-start.11 = (bf16[1024,256]{1,0:T(8,128)(2,1)S(1)}, bf16[1024,256]{1,0:T(8,128)(2,1)S(1)}, u32[]{:S(2)}, u32[]{:S(2)}) collective-permute-start(bf16[1024,256]{1,0:T(8,128)(2,1)S(1)} %shard_map.127.refs_5_.refs_4_), channel_id=1, source_target_pairs={{0,2},{1,3},{2,0},{3,1},{4,6},{5,7},{6,4},{7,5},{8,10},{9,11},{10,... | collective-permute-start | bytes 1572872 | tf_op jit(solution)/shard_map/ppermute | solution.py:494
  14.9 5.5 %shard_map.128 = (f32[4096,512]{1,0:T(8,128)S(1)}, f32[1024,512]{1,0:T(8,128)}, f32[1024,512]{1,0:T(8,128)}) custom-call(s32[26]{0:T(128)S(1)} %stack.107.refs_0_, bf16[256,8192]{1,0:T(8,128)(2,1)} %bitcast.56, bf16[256,512]{1,0:T(8,128)(2,1)S(1)} %bitcast.43, f32[1024,512]{1,0:T(8,128)} %refs_7_.1, f32[1024,512]{1,0:T(8,128)} %refs_8_.1, ...), custom_call_target="tpu_custom_call" | custom-call | bytes 17000000 | tf_op jit(solution)/shard_map/pallas_call | solution.py:104
  20.4 4.5 %shard_map.129 = (f32[4096,512]{1,0:T(8,128)S(1)}, f32[1024,512]{1,0:T(8,128)S(1)}, f32[1024,512]{1,0:T(8,128)S(1)}, f32[1024,512]{1,0:T(8,128)S(1)}, f32[1024,128]{1,0:T(8,128)S(1)}, /*index=5*/f32[1024,128]{1,0:T(8,128)S(1)}) custom-call(s32[26]{0:T(128)S(1)} %stack.107.refs_0_, ...), custom_call_target="tpu_custom_call", output_to_operand_aliasing={{0}: (1, {})} | custom-call | bytes 17000000 | tf_op jit(solution)/shard_map/pallas_call | solution.py:104
  25.9 2.0 %collective-permute-start.5 = (bf16[1024,256]{1,0:T(8,128)(2,1)S(1)}, bf16[1024,256]{1,0:T(8,128)(2,1)S(1)}, u32[]{:S(2)}, u32[]{:S(2)}) collective-permute-start(bf16[1024,256]{1,0:T(8,128)(2,1)S(1)} %get-tuple-element.66.refs_5_), channel_id=1, source_target_pairs={{0,2},{1,3},{2,0},{3,1},{4,6},{5,7},{6,4},{7,5},{8,10},{9,11},{10,... | collective-permute-start | bytes 1572872 | tf_op jit(solution)/shard_map/ppermute | solution.py:494
  28.0 2.1 %shard_map.133 = (bf16[256,1024]{1,0:T(8,128)(2,1)S(1)}, bf16[256,8192]{1,0:T(8,128)(2,1)}, f32[8,128]{1,0:T(8,128)S(1)}) custom-call(s32[26]{0:T(128)S(1)} %stack.107.refs_0_, bf16[256,512]{1,0:T(8,128)(2,1)S(1)} %bitcast.44, bf16[256,512]{1,0:T(8,128)(2,1)S(1)} %collective-permute-done.refs_2_.refs_3_, bf16[1024,256]{1,0:T(8,128)(2,1)S(1)} %slice.13.refs_3_, ...), custom_call_target="tpu_custom_call" | custom-call | bytes 7140000 | tf_op jit(solution)/shard_map/pallas_call | solution.py:104
  31.6 2.5 %collective-permute-start.13 = (bf16[1024,256]{1,0:T(8,128)(2,1)S(1)}, bf16[1024,256]{1,0:T(8,128)(2,1)S(1)}, u32[]{:S(2)}, u32[]{:S(2)}) collective-permute-start(bf16[1024,256]{1,0:T(8,128)(2,1)S(1)} %get-tuple-element.78), channel_id=1, source_target_pairs={{0,2},{1,3},{2,0},{3,1},{4,6},{5,7},{6,4},{7,5},{8,10},{9,11},{10,... | collective-permute-start | bytes 1572872 | tf_op jit(solution)/shard_map/ppermute | solution.py:494
  34.1 7.8 %collective-permute-done.5.refs_3_ = bf16[1024,256]{1,0:T(8,128)(2,1)S(1)} collective-permute-done((bf16[1024,256]{1,0:T(8,128)(2,1)S(1)}, bf16[1024,256]{1,0:T(8,128)(2,1)S(1)}, u32[]{:S(2)}, u32[]{:S(2)}) %collective-permute-start.5) | collective-permute-done | bytes 524320 | tf_op jit(solution)/shard_map/ppermute | solution.py:494
  42.9 2.5 %collective-permute-start.7 = (bf16[1024,256]{1,0:T(8,128)(2,1)S(1)}, bf16[1024,256]{1,0:T(8,128)(2,1)S(1)}, u32[]{:S(2)}, u32[]{:S(2)}) collective-permute-start(bf16[1024,256]{1,0:T(8,128)(2,1)S(1)} %get-tuple-element.68.refs_7_), channel_id=1, source_target_pairs={{0,2},{1,3},{2,0},{3,1},{4,6},{5,7},{6,4},{7,5},{8,10},{9,11},{10,... | collective-permute-start | bytes 1572872 | tf_op jit(solution)/shard_map/ppermute | solution.py:494
  45.4 2.1 %shard_map.135 = (bf16[256,1024]{1,0:T(8,128)(2,1)S(1)}, bf16[256,8192]{1,0:T(8,128)(2,1)}, f32[8,128]{1,0:T(8,128)S(1)}) custom-call(s32[26]{0:T(128)S(1)} %stack.107.refs_0_, bf16[256,512]{1,0:T(8,128)(2,1)S(1)} %bitcast.45, bf16[256,512]{1,0:T(8,128)(2,1)S(1)} %collective-permute-done.refs_2_.refs_3_, ...), custom_call_target="tpu_custom_call", output_to_operand_aliasing={{1}: (6, {})} | custom-call | bytes 7140000 | tf_op jit(solution)/shard_map/pallas_call | solution.py:104
  47.6 5.5 %collective-permute-done.13.refs_3_ = bf16[1024,256]{1,0:T(8,128)(2,1)S(1)} collective-permute-done((bf16[1024,256]{1,0:T(8,128)(2,1)S(1)}, bf16[1024,256]{1,0:T(8,128)(2,1)S(1)}, u32[]{:S(2)}, u32[]{:S(2)}) %collective-permute-start.13) | collective-permute-done | bytes 524320 | tf_op jit(solution)/shard_map/ppermute | solution.py:494
  54.1 2.5 %collective-permute-start.16 = (bf16[1024,256]{1,0:T(8,128)(2,1)S(1)}, bf16[1024,256]{1,0:T(8,128)(2,1)S(1)}, u32[]{:S(2)}, u32[]{:S(2)}) collective-permute-start(bf16[1024,256]{1,0:T(8,128)(2,1)S(1)} %get-tuple-element.85), channel_id=1, source_target_pairs={{0,2},{1,3},{2,0},{3,1},{4,6},{5,7},{6,4},{7,5},{8,10},{9,11},{10,... | collective-permute-start | bytes 1572872 | tf_op jit(solution)/shard_map/ppermute | solution.py:494
  56.6 7.7 %collective-permute-done.7.refs_3_ = bf16[1024,256]{1,0:T(8,128)(2,1)S(1)} collective-permute-done((bf16[1024,256]{1,0:T(8,128)(2,1)S(1)}, bf16[1024,256]{1,0:T(8,128)(2,1)S(1)}, u32[]{:S(2)}, u32[]{:S(2)}) %collective-permute-start.7) | collective-permute-done | bytes 524320 | tf_op jit(solution)/shard_map/ppermute | solution.py:494
  65.3 2.1 %shard_map.137 = (bf16[256,1024]{1,0:T(8,128)(2,1)S(1)}, bf16[256,8192]{1,0:T(8,128)(2,1)}, f32[8,128]{1,0:T(8,128)S(1)}) custom-call(s32[26]{0:T(128)S(1)} %stack.107.refs_0_, bf16[256,512]{1,0:T(8,128)(2,1)S(1)} %bitcast.46, bf16[256,512]{1,0:T(8,128)(2,1)S(1)} %collective-permute-done.refs_2_.refs_3_, ...), custom_call_target="tpu_custom_call", output_to_operand_aliasing={{1}: (6, {})} | custom-call | bytes 7140000 | tf_op jit(solution)/shard_map/pallas_call | solution.py:104
  67.5 2.2 %collective-permute-start.8 = (bf16[1024,256]{1,0:T(8,128)(2,1)S(1)}, bf16[1024,256]{1,0:T(8,128)(2,1)S(1)}, u32[]{:S(2)}, u32[]{:S(2)}) collective-permute-start(bf16[1024,256]{1,0:T(8,128)(2,1)S(1)} %get-tuple-element.69.refs_7_), channel_id=1, source_target_pairs={{0,2},{1,3},{2,0},{3,1},{4,6},{5,7},{6,4},{7,5},{8,10},{9,11},{10,... | collective-permute-start | bytes 1572872 | tf_op jit(solution)/shard_map/ppermute | solution.py:494
  69.9 5.7 %collective-permute-done.16.refs_3_ = bf16[1024,256]{1,0:T(8,128)(2,1)S(1)} collective-permute-done((bf16[1024,256]{1,0:T(8,128)(2,1)S(1)}, bf16[1024,256]{1,0:T(8,128)(2,1)S(1)}, u32[]{:S(2)}, u32[]{:S(2)}) %collective-permute-start.16) | collective-permute-done | bytes 524320 | tf_op jit(solution)/shard_map/ppermute | solution.py:494
  76.5 2.1 %shard_map.139 = (bf16[256,1024]{1,0:T(8,128)(2,1)S(1)}, bf16[256,8192]{1,0:T(8,128)(2,1)}, f32[8,128]{1,0:T(8,128)S(1)}) custom-call(s32[26]{0:T(128)S(1)} %stack.107.refs_0_, bf16[256,512]{1,0:T(8,128)(2,1)S(1)} %bitcast.47, bf16[256,512]{1,0:T(8,128)(2,1)S(1)} %collective-permute-done.refs_2_.refs_3_, ...), custom_call_target="tpu_custom_call", output_to_operand_aliasing={{1}: (6, {})} | custom-call | bytes 7140000 | tf_op jit(solution)/shard_map/pallas_call | solution.py:104
  78.7 2.2 %collective-permute-start.20 = (bf16[1024,256]{1,0:T(8,128)(2,1)S(1)}, bf16[1024,256]{1,0:T(8,128)(2,1)S(1)}, u32[]{:S(2)}, u32[]{:S(2)}) collective-permute-start(bf16[1024,256]{1,0:T(8,128)(2,1)S(1)} %get-tuple-element.100), channel_id=1, source_target_pairs={{0,2},{1,3},{2,0},{3,1},{4,6},{5,7},{6,4},{7,5},{8,10},{9,11},{10,... | collective-permute-start | bytes 1572872 | tf_op jit(solution)/shard_map/ppermute | solution.py:494
  81.1 5.7 %collective-permute-done.8.refs_2_ = bf16[1024,256]{1,0:T(8,128)(2,1)S(1)} collective-permute-done((bf16[1024,256]{1,0:T(8,128)(2,1)S(1)}, bf16[1024,256]{1,0:T(8,128)(2,1)S(1)}, u32[]{:S(2)}, u32[]{:S(2)}) %collective-permute-start.8) | collective-permute-done | bytes 524320 | tf_op jit(solution)/shard_map/ppermute | solution.py:494
  87.9 1.6 %collective-permute-start.23 = (bf16[512,128]{1,0:T(8,128)(2,1)S(1)}, bf16[512,128]{1,0:T(8,128)(2,1)S(1)}, u32[]{:S(2)}, u32[]{:S(2)}) collective-permute-start(bf16[512,128]{1,0:T(8,128)(2,1)S(1)} %get-tuple-element.107), channel_id=1, source_target_pairs={{0,16},{8,24},{16,0},{24,8},{1,17},{9,25},{17,1},{25,9},{2,18},{10... | collective-permute-start | bytes 393224 | tf_op jit(solution)/shard_map/ppermute | solution.py:494
  91.0 2.3 %shard_map.141 = (f32[1024,512]{1,0:T(8,128)}, f32[1024,512]{1,0:T(8,128)}, f32[1024,512]{1,0:T(8,128)}, bf16[256,8192]{1,0:T(8,128)(2,1)}, f32[8,128]{1,0:T(8,128)S(1)}) custom-call(s32[26]{0:T(128)S(1)} %stack.107.refs_0_, f32[4096,512]{1,0:T(8,128)S(1)} %get-tuple-element.64.refs_1_, ...), custom_call_target="tpu_custom_call", output_to_operand_aliasing={{3}: (10, {})} | custom-call | bytes 6800000 | tf_op jit(solution)/shard_map/pallas_call | solution.py:104
  97.7 2.3 %shard_map.142 = (f32[1024,512]{1,0:T(8,128)}, f32[1024,512]{1,0:T(8,128)}, f32[1024,512]{1,0:T(8,128)}, f32[3,256,256]{2,1,0:T(8,128)S(1)}) custom-call(s32[26]{0:T(128)S(1)} %stack.107.refs_0_, f32[4096,512]{1,0:T(8,128)S(1)} %get-tuple-element.64.refs_1_, ...), custom_call_target="tpu_custom_call", output_to_operand_aliasing={{0}: (7, {}), {1}: (8, {}), {2}: (9, {})} | custom-call | bytes 8160000 | tf_op jit(solution)/shard_map/pallas_call | solution.py:104
  100.1 2.0 %shard_map.143 = (f32[1024,512]{1,0:T(8,128)}, f32[1024,512]{1,0:T(8,128)}, f32[1024,512]{1,0:T(8,128)}, f32[1024,512]{1,0:T(8,128)}, f32[1024,512]{1,0:T(8,128)}) custom-call(s32[26]{0:T(128)S(1)} %stack.107.refs_0_, f32[3,256,256]{2,1,0:T(8,128)S(1)} %get-tuple-element.108.refs_1_, ...), custom_call_target="tpu_custom_call", output_to_operand_aliasing={{0}: (8, {}), {1}: (9, {}), {2}: (10, {}), {3}: (11, {}), {... | custom-call | bytes 6800000 | tf_op jit(solution)/shard_map/pallas_call | solution.py:104
  (51 shorter events, 17.7 us)
Async XLA Ops:
  0.6 19.8 %collective-permute-start.1 = (bf16[256,8192]{1,0:T(8,128)(2,1)}, bf16[256,8192]{1,0:T(8,128)(2,1)}, u32[]{:S(2)}, u32[]{:S(2)}) collective-permute-start(bf16[256,8192]{1,0:T(8,128)(2,1)} %bitcast.55), channel_id=1, source_target_pairs={{0,1},{1,0},{2,3},{3,2},{4,5},{5,4},{6,7},{7,6},{8,9},{9,8},{10,11... | collective-permute-start | bytes 12582920 | tf_op jit(solution)/shard_map/ppermute | solution.py:494
  2.5 22.4 %collective-permute-start.2 = (bf16[1024,256]{1,0:T(8,128)(2,1)S(1)}, bf16[1024,256]{1,0:T(8,128)(2,1)S(1)}, u32[]{:S(2)}, u32[]{:S(2)}) collective-permute-start(bf16[1024,256]{1,0:T(8,128)(2,1)S(1)} %slice.13.refs_3_), channel_id=1, source_target_pairs={{0,1},{1,0},{2,4},{3,5},{4,2},{5,3},{6,7},{7,6},{8,9},{9,8},{10,12... | collective-permute-start | bytes 1572872 | tf_op jit(solution)/shard_map/ppermute | solution.py:494
  2.6 22.3 %collective-permute-start.3 = (bf16[1024,256]{1,0:T(8,128)(2,1)S(1)}, bf16[1024,256]{1,0:T(8,128)(2,1)S(1)}, u32[]{:S(2)}, u32[]{:S(2)}) collective-permute-start(bf16[1024,256]{1,0:T(8,128)(2,1)S(1)} %slice.13.refs_3_), channel_id=1, source_target_pairs={{0,2},{1,3},{2,0},{3,1},{4,6},{5,7},{6,4},{7,5},{8,10},{9,11},{10,... | collective-permute-start | bytes 1572872 | tf_op jit(solution)/shard_map/ppermute | solution.py:494
  11.0 19.1 %collective-permute-start.10 = (bf16[1024,256]{1,0:T(8,128)(2,1)S(1)}, bf16[1024,256]{1,0:T(8,128)(2,1)S(1)}, u32[]{:S(2)}, u32[]{:S(2)}) collective-permute-start(bf16[1024,256]{1,0:T(8,128)(2,1)S(1)} %shard_map.127.refs_5_.refs_4_), channel_id=1, source_target_pairs={{0,1},{1,0},{2,4},{3,5},{4,2},{5,3},{6,7},{7,6},{8,9},{9,8},{10,12... | collective-permute-start | bytes 1572872 | tf_op jit(solution)/shard_map/ppermute | solution.py:494
  11.2 19.4 %collective-permute-start.11 = (bf16[1024,256]{1,0:T(8,128)(2,1)S(1)}, bf16[1024,256]{1,0:T(8,128)(2,1)S(1)}, u32[]{:S(2)}, u32[]{:S(2)}) collective-permute-start(bf16[1024,256]{1,0:T(8,128)(2,1)S(1)} %shard_map.127.refs_5_.refs_4_), channel_id=1, source_target_pairs={{0,2},{1,3},{2,0},{3,1},{4,6},{5,7},{6,4},{7,5},{8,10},{9,11},{10,... | collective-permute-start | bytes 1572872 | tf_op jit(solution)/shard_map/ppermute | solution.py:494
  25.8 8.2 %collective-permute-start.4 = (bf16[1024,256]{1,0:T(8,128)(2,1)S(1)}, bf16[1024,256]{1,0:T(8,128)(2,1)S(1)}, u32[]{:S(2)}, u32[]{:S(2)}) collective-permute-start(bf16[1024,256]{1,0:T(8,128)(2,1)S(1)} %get-tuple-element.65), channel_id=1, source_target_pairs={{0,1},{1,0},{2,4},{3,5},{4,2},{5,3},{6,7},{7,6},{8,9},{9,8},{10,12... | collective-permute-start | bytes 1572872 | tf_op jit(solution)/shard_map/ppermute | solution.py:494
  25.9 16.0 %collective-permute-start.5 = (bf16[1024,256]{1,0:T(8,128)(2,1)S(1)}, bf16[1024,256]{1,0:T(8,128)(2,1)S(1)}, u32[]{:S(2)}, u32[]{:S(2)}) collective-permute-start(bf16[1024,256]{1,0:T(8,128)(2,1)S(1)} %get-tuple-element.66.refs_5_), channel_id=1, source_target_pairs={{0,2},{1,3},{2,0},{3,1},{4,6},{5,7},{6,4},{7,5},{8,10},{9,11},{10,... | collective-permute-start | bytes 1572872 | tf_op jit(solution)/shard_map/ppermute | solution.py:494
  30.1 15.3 %collective-permute-start.14 = (bf16[256,1024]{1,0:T(8,128)(2,1)S(1)}, bf16[256,1024]{1,0:T(8,128)(2,1)S(1)}, u32[]{:S(2)}, u32[]{:S(2)}) collective-permute-start(bf16[256,1024]{1,0:T(8,128)(2,1)S(1)} %get-tuple-element.81), channel_id=1, source_target_pairs={{0,1},{1,0},{2,3},{3,2},{4,5},{5,4},{6,7},{7,6},{8,9},{9,8},{10,11... | collective-permute-start | bytes 1572872 | tf_op jit(solution)/shard_map/ppermute | solution.py:494
  31.5 16.1 %collective-permute-start.12 = (bf16[1024,256]{1,0:T(8,128)(2,1)S(1)}, bf16[1024,256]{1,0:T(8,128)(2,1)S(1)}, u32[]{:S(2)}, u32[]{:S(2)}) collective-permute-start(bf16[1024,256]{1,0:T(8,128)(2,1)S(1)} %get-tuple-element.77), channel_id=1, source_target_pairs={{0,1},{1,0},{2,4},{3,5},{4,2},{5,3},{6,7},{7,6},{8,9},{9,8},{10,12... | collective-permute-start | bytes 1572872 | tf_op jit(solution)/shard_map/ppermute | solution.py:494
  31.6 21.5 %collective-permute-start.13 = (bf16[1024,256]{1,0:T(8,128)(2,1)S(1)}, bf16[1024,256]{1,0:T(8,128)(2,1)S(1)}, u32[]{:S(2)}, u32[]{:S(2)}) collective-permute-start(bf16[1024,256]{1,0:T(8,128)(2,1)S(1)} %get-tuple-element.78), channel_id=1, source_target_pairs={{0,2},{1,3},{2,0},{3,1},{4,6},{5,7},{6,4},{7,5},{8,10},{9,11},{10,... | collective-permute-start | bytes 1572872 | tf_op jit(solution)/shard_map/ppermute | solution.py:494
  42.8 13.8 %collective-permute-start.6 = (bf16[1024,256]{1,0:T(8,128)(2,1)S(1)}, bf16[1024,256]{1,0:T(8,128)(2,1)S(1)}, u32[]{:S(2)}, u32[]{:S(2)}) collective-permute-start(bf16[1024,256]{1,0:T(8,128)(2,1)S(1)} %get-tuple-element.67), channel_id=1, source_target_pairs={{0,1},{1,0},{2,4},{3,5},{4,2},{5,3},{6,7},{7,6},{8,9},{9,8},{10,12... | collective-permute-start | bytes 1572872 | tf_op jit(solution)/shard_map/ppermute | solution.py:494
  42.9 21.5 %collective-permute-start.7 = (bf16[1024,256]{1,0:T(8,128)(2,1)S(1)}, bf16[1024,256]{1,0:T(8,128)(2,1)S(1)}, u32[]{:S(2)}, u32[]{:S(2)}) collective-permute-start(bf16[1024,256]{1,0:T(8,128)(2,1)S(1)} %get-tuple-element.68.refs_7_), channel_id=1, source_target_pairs={{0,2},{1,3},{2,0},{3,1},{4,6},{5,7},{6,4},{7,5},{8,10},{9,11},{10,... | collective-permute-start | bytes 1572872 | tf_op jit(solution)/shard_map/ppermute | solution.py:494
  47.5 17.8 %collective-permute-start.17 = (bf16[256,1024]{1,0:T(8,128)(2,1)S(1)}, bf16[256,1024]{1,0:T(8,128)(2,1)S(1)}, u32[]{:S(2)}, u32[]{:S(2)}) collective-permute-start(bf16[256,1024]{1,0:T(8,128)(2,1)S(1)} %get-tuple-element.88), channel_id=1, source_target_pairs={{0,1},{1,0},{2,3},{3,2},{4,5},{5,4},{6,7},{7,6},{8,9},{9,8},{10,11... | collective-permute-start | bytes 1572872 | tf_op jit(solution)/shard_map/ppermute | solution.py:494
  54.0 15.8 %collective-permute-start.15 = (bf16[1024,256]{1,0:T(8,128)(2,1)S(1)}, bf16[1024,256]{1,0:T(8,128)(2,1)S(1)}, u32[]{:S(2)}, u32[]{:S(2)}) collective-permute-start(bf16[1024,256]{1,0:T(8,128)(2,1)S(1)} %get-tuple-element.84), channel_id=1, source_target_pairs={{0,1},{1,0},{2,4},{3,5},{4,2},{5,3},{6,7},{7,6},{8,9},{9,8},{10,12... | collective-permute-start | bytes 1572872 | tf_op jit(solution)/shard_map/ppermute | solution.py:494
  54.1 21.5 %collective-permute-start.16 = (bf16[1024,256]{1,0:T(8,128)(2,1)S(1)}, bf16[1024,256]{1,0:T(8,128)(2,1)S(1)}, u32[]{:S(2)}, u32[]{:S(2)}) collective-permute-start(bf16[1024,256]{1,0:T(8,128)(2,1)S(1)} %get-tuple-element.85), channel_id=1, source_target_pairs={{0,2},{1,3},{2,0},{3,1},{4,6},{5,7},{6,4},{7,5},{8,10},{9,11},{10,... | collective-permute-start | bytes 1572872 | tf_op jit(solution)/shard_map/ppermute | solution.py:494
  67.4 9.1 %collective-permute-start.18 = (bf16[256,1024]{1,0:T(8,128)(2,1)S(1)}, bf16[256,1024]{1,0:T(8,128)(2,1)S(1)}, u32[]{:S(2)}, u32[]{:S(2)}) collective-permute-start(bf16[256,1024]{1,0:T(8,128)(2,1)S(1)} %get-tuple-element.92), channel_id=1, source_target_pairs={{0,1},{1,0},{2,3},{3,2},{4,5},{5,4},{6,7},{7,6},{8,9},{9,8},{10,11... | collective-permute-start | bytes 1572872 | tf_op jit(solution)/shard_map/ppermute | solution.py:494
  67.5 19.3 %collective-permute-start.8 = (bf16[1024,256]{1,0:T(8,128)(2,1)S(1)}, bf16[1024,256]{1,0:T(8,128)(2,1)S(1)}, u32[]{:S(2)}, u32[]{:S(2)}) collective-permute-start(bf16[1024,256]{1,0:T(8,128)(2,1)S(1)} %get-tuple-element.69.refs_7_), channel_id=1, source_target_pairs={{0,2},{1,3},{2,0},{3,1},{4,6},{5,7},{6,4},{7,5},{8,10},{9,11},{10,... | collective-permute-start | bytes 1572872 | tf_op jit(solution)/shard_map/ppermute | solution.py:494
  69.7 17.1 %collective-permute-start.9 = (bf16[1024,256]{1,0:T(8,128)(2,1)S(1)}, bf16[1024,256]{1,0:T(8,128)(2,1)S(1)}, u32[]{:S(2)}, u32[]{:S(2)}) collective-permute-start(bf16[1024,256]{1,0:T(8,128)(2,1)S(1)} %get-tuple-element.70), channel_id=1, source_target_pairs={{0,1},{1,0},{2,4},{3,5},{4,2},{5,3},{6,7},{7,6},{8,9},{9,8},{10,12... | collective-permute-start | bytes 1572872 | tf_op jit(solution)/shard_map/ppermute | solution.py:494
  78.6 12.4 %collective-permute-start.19 = (bf16[256,1024]{1,0:T(8,128)(2,1)S(1)}, bf16[256,1024]{1,0:T(8,128)(2,1)S(1)}, u32[]{:S(2)}, u32[]{:S(2)}) collective-permute-start(bf16[256,1024]{1,0:T(8,128)(2,1)S(1)} %get-tuple-element.97), channel_id=1, source_target_pairs={{0,1},{1,0},{2,3},{3,2},{4,5},{5,4},{6,7},{7,6},{8,9},{9,8},{10,11... | collective-permute-start | bytes 1572872 | tf_op jit(solution)/shard_map/ppermute | solution.py:494
  78.7 18.9 %collective-permute-start.20 = (bf16[1024,256]{1,0:T(8,128)(2,1)S(1)}, bf16[1024,256]{1,0:T(8,128)(2,1)S(1)}, u32[]{:S(2)}, u32[]{:S(2)}) collective-permute-start(bf16[1024,256]{1,0:T(8,128)(2,1)S(1)} %get-tuple-element.100), channel_id=1, source_target_pairs={{0,2},{1,3},{2,0},{3,1},{4,6},{5,7},{6,4},{7,5},{8,10},{9,11},{10,... | collective-permute-start | bytes 1572872 | tf_op jit(solution)/shard_map/ppermute | solution.py:494
  80.9 16.7 %collective-permute-start.21 = (bf16[1024,256]{1,0:T(8,128)(2,1)S(1)}, bf16[1024,256]{1,0:T(8,128)(2,1)S(1)}, u32[]{:S(2)}, u32[]{:S(2)}) collective-permute-start(bf16[1024,256]{1,0:T(8,128)(2,1)S(1)} %get-tuple-element.101), channel_id=1, source_target_pairs={{0,1},{1,0},{2,4},{3,5},{4,2},{5,3},{6,7},{7,6},{8,9},{9,8},{10,12... | collective-permute-start | bytes 1572872 | tf_op jit(solution)/shard_map/ppermute | solution.py:494
  87.9 5.4 %collective-permute-start.23 = (bf16[512,128]{1,0:T(8,128)(2,1)S(1)}, bf16[512,128]{1,0:T(8,128)(2,1)S(1)}, u32[]{:S(2)}, u32[]{:S(2)}) collective-permute-start(bf16[512,128]{1,0:T(8,128)(2,1)S(1)} %get-tuple-element.107), channel_id=1, source_target_pairs={{0,16},{8,24},{16,0},{24,8},{1,17},{9,25},{17,1},{25,9},{2,18},{10... | collective-permute-start | bytes 393224 | tf_op jit(solution)/shard_map/ppermute | solution.py:494
  89.5 5.0 %collective-permute-start.22 = (bf16[512,128]{1,0:T(8,128)(2,1)S(1)}, bf16[512,128]{1,0:T(8,128)(2,1)S(1)}, u32[]{:S(2)}, u32[]{:S(2)}) collective-permute-start(bf16[512,128]{1,0:T(8,128)(2,1)S(1)} %get-tuple-element.105), channel_id=1, source_target_pairs={{0,8},{8,0},{16,24},{24,16},{1,9},{9,1},{17,25},{25,17},{2,10},{10... | collective-permute-start | bytes 393224 | tf_op jit(solution)/shard_map/ppermute | solution.py:494
  94.6 5.4 %collective-permute-start.24 = (bf16[512,128]{1,0:T(8,128)(2,1)S(1)}, bf16[512,128]{1,0:T(8,128)(2,1)S(1)}, u32[]{:S(2)}, u32[]{:S(2)}) collective-permute-start(bf16[512,128]{1,0:T(8,128)(2,1)S(1)} %get-tuple-element.121.refs_10_.refs_2_), channel_id=1, source_target_pairs={{0,16},{8,24},{16,0},{24,8},{1,17},{9,25},{17,1},{25,9},{2,18},{10... | collective-permute-start | bytes 393224 | tf_op jit(solution)/shard_map/ppermute | solution.py:494
  (3 other events, 21.2 us)

commit v5 on v4

--- a/solution.py
+++ b/solution.py
@@ -80,14 +80,24 @@
     return jax.ShapeDtypeStruct(shape, dtype)
 
 
+class Numbers:
+    def __init__(self, ref):
+        self.ref, self.read = ref, {}
+
+    def __getitem__(self, k):
+        if k not in self.read:
+            self.read[k] = self.ref[0, k]
+        return self.read[k]
+
+
 class Held:
     def __init__(self, array):
         self.array = array
 
 
 def call(body, scalars, ins, outs, scratch=(), aliases=None, after=(), us=1.0):
-    arrays, specs = [scalars], [pl.BlockSpec(memory_space=pltpu.SMEM)]
-    for x in ins:
+    arrays, specs = [], []
+    for x in [Held(scalars), *ins]:
         if isinstance(x, Held):
             arrays.append(pltpu.with_memory_space_constraint(x.array, pltpu.VMEM))
             specs.append(pl.BlockSpec(memory_space=pltpu.VMEM))
@@ -99,7 +109,7 @@
     specs += [pl.BlockSpec(memory_space=pltpu.VMEM)] * len(after)
 
     def inner(*refs):
-        body(*refs[:first], *refs[first + len(after) :])
+        body(Numbers(refs[0]), *refs[1:first], *refs[first + len(after) :])
 
     return pl.pallas_call(
         inner,
@@ -317,8 +327,9 @@
 
 def adam(at, offset, first_row, s, sums_ref, from_e, from_o, w, m, v, put, count, width, taken):
     columns = slice(offset, offset + width)
-    size = 128
+    size = 256
     base = pl.multiple_of(s[at["z"]] * from_e.shape[0], TILE)
+    middle = s[at["middle"]] == 1
 
     @pl.loop(0, count // size)
     def _(i):
@@ -326,14 +337,12 @@
         here = pl.ds(r, size)
         one = sums_ref[pl.ds(base + r, size), columns] + from_e[here, taken].astype(F32)
         both = one + from_o[here, taken].astype(F32)
-        gradient = jnp.where(s[at["middle"]] == 1, both, one)
+        gradient = jnp.where(middle, both, one)
         first = 0.9 * m[here, columns] + 0.1 * gradient
         second = 0.95 * v[here, columns] + 0.05 * gradient * gradient
-        scaled = second * (1.0 / CORR_TWO)
-        below = scaled * lax.rsqrt(scaled) + 1e-08
-        over = pl.reciprocal(below, approx=True)
-        over = over * (2.0 - below * over)
-        stepped = (1.0 - 0.1 * 0.1) * w[here, columns] - first * (0.1 / CORR_ONE) * over
+        below = second * lax.rsqrt(second) + 1e-08 * CORR_TWO**0.5
+        moved = first * (0.1 * CORR_TWO**0.5 / CORR_ONE) / below
+        stepped = (1.0 - 0.1 * 0.1) * w[here, columns] - moved
         put(r, stepped, first, second)
 
 
@@ -414,21 +423,17 @@
         last = columns_of(out.at[there], s[at["pieces"] + 2], part)
         copies.append(start(left.at[k], last, sems.at[k]))
     half = rows // 2
-    size = 128
+    size = half // 2
     for n, (own, other) in enumerate(((upper, upper_in), (lower, lower_in))):
-
-        @pl.loop(0, half // size)
-        def _(i):
-            r = pl.multiple_of(i * size, size)
+        for r in (0, size):
             here, there = pl.ds(r, size), pl.ds(n * half + r, size)
-            average = (own[here, :].astype(F32) + other[here, :].astype(F32)) / 4.0
+            average = (own[here, :].astype(F32) + other[here, :].astype(F32)) * 0.25
             momentum = 0.9 * moment[there, :] + average
             stage[0, there, :] = momentum
             stage[1, there, :] = anchor[there, :] - 0.7 * (average + 0.9 * momentum)
-
-    for k, out in ((0, new_moment), (1, new_anchor), (1, inner)):
-        columns = columns_of(out, s[at["pieces"]], HEAD)
-        copies.append(start(stage.at[k], columns, sems.at[len(copies)]))
+            for k, out in ((0, new_moment), (1, new_anchor), (1, inner)):
+                target = columns_of(out.at[there], s[at["pieces"]], HEAD)
+                copies.append(start(stage.at[k, there], target, sems.at[len(copies)]))
     for copy in copies:
         copy.wait()
 
@@ -488,7 +493,7 @@
             jnp.where(even, down_to, up_to),
         ]
     name("hop", *hops)
-    s = jnp.stack(values)
+    s = jnp.pad(jnp.stack(values), (0, 128 - len(values)))[None]
 
     def permute(x, perm, axis="fsdp"):
         return lax.ppermute(x, axis, perm)
@@ -633,7 +638,7 @@
         s,
         [Held(x) for x in held] + [*state, new_anchor, new_momentum],
         [hbm(rows, columns)] * 5,
-        [vmem(2, rows, HEAD), dma((6,))],
+        [vmem(2, rows, HEAD), dma((15,))],
         {len(held) + k: k for k in range(5)},
         us=2.0,
     )

time: 102 us -> 101 us (level)
  Pallas kernels: 33.3 us -> 26.5 us
  waiting for transfers between devices: 36.9 us -> 42.8 us
    pallas_call x17, Pallas kernels: 33.3 us -> 26.5 us  [call(): pl.pallas_call(inner, in_specs=specs, out_specs=[pl.BlockSpec(memory_spac...]
    ppermute x26, waiting for transfers between devices: 36.9 us -> 42.8 us  [permute(): return lax.ppermute(x, axis, perm)]
  transfers between devices with their start and end apart: 26 -> 26, of which waited for: 10 -> 10; matrix products, arithmetic and copies ran while one was open for 2% -> 2% of each run, Pallas kernels for 31% -> 25%
where the time goes in v5:
time: 101 us
  waiting for transfers between devices  42.8 us (42%)
  starting transfers between devices  28.7 us (28%)
  Pallas kernels  26.5 us (26%)
  between operations  1.72 us (2%)
  local copies, waits for them, and re-layouts  1.45 us (1%)
    ppermute x26, waiting for transfers between devices, permute(): return lax.ppermute(x, axis, perm)  42.8 us
    ppermute x26, starting transfers between devices, permute(): return lax.ppermute(x, axis, perm)  28.7 us
    pallas_call x17, Pallas kernels, call(): pl.pallas_call(inner, in_specs=specs, out_specs=[pl.BlockSpec(memory_spac...  26.5 us
  transfers between devices with their start and end apart: 26, of which 10 were waited for; matrix products, arithmetic and copies ran while one was open for 2% of the time, Pallas kernels for 25%

profile of v5, /device:TPU:0, one launch (start us, length us, event | category | flops | bytes accessed | tf_op | source)
XLA Modules:
  0.0 101.3 jit_solution(16310052732487983123)
XLA Ops:
  2.6 4.1 %collective-permute-start.3 = (bf16[1024,256]{1,0:T(8,128)(2,1)S(1)}, bf16[1024,256]{1,0:T(8,128)(2,1)S(1)}, u32[]{:S(2)}, u32[]{:S(2)}) collective-permute-start(bf16[1024,256]{1,0:T(8,128)(2,1)S(1)} %slice.13.refs_3_), channel_id=1, source_target_pairs={{0,2},{1,3},{2,0},{3,1},{4,6},{5,7},{6,4},{7,5},{8,10},{9,11},{10,... | collective-permute-start | bytes 1572872 | tf_op jit(solution)/shard_map/ppermute | solution.py:499
  10.7 3.7 %collective-permute-start.11 = (bf16[1024,256]{1,0:T(8,128)(2,1)S(1)}, bf16[1024,256]{1,0:T(8,128)(2,1)S(1)}, u32[]{:S(2)}, u32[]{:S(2)}) collective-permute-start(bf16[1024,256]{1,0:T(8,128)(2,1)S(1)} %shard_map.127.refs_5_.refs_4_), channel_id=1, source_target_pairs={{0,2},{1,3},{2,0},{3,1},{4,6},{5,7},{6,4},{7,5},{8,10},{9,11},{10,... | collective-permute-start | bytes 1572872 | tf_op jit(solution)/shard_map/ppermute | solution.py:499
  14.4 5.3 %shard_map.128 = (f32[4096,512]{1,0:T(8,128)S(1)}, f32[1024,512]{1,0:T(8,128)}, f32[1024,512]{1,0:T(8,128)}) custom-call(s32[1,128]{1,0:T(1,128)S(1)} %pad_bitcast_fusion.refs_0_, bf16[256,8192]{1,0:T(8,128)(2,1)} %bitcast.58, bf16[256,512]{1,0:T(8,128)(2,1)S(1)} %bitcast.45, f32[1024,512]{1,0:T(8,128)} %refs_7_.1, f32[1024,512]{1,0:T(8,128)} %refs_8_.1, ...), custom_call_target="tpu_custom_call" | custom-call | bytes 17000000 | tf_op jit(solution)/shard_map/pallas_call | solution.py:114
  19.7 4.3 %shard_map.129 = (f32[4096,512]{1,0:T(8,128)S(1)}, f32[1024,512]{1,0:T(8,128)S(1)}, f32[1024,512]{1,0:T(8,128)S(1)}, f32[1024,512]{1,0:T(8,128)S(1)}, f32[1024,128]{1,0:T(8,128)S(1)}, /*index=5*/f32[1024,128]{1,0:T(8,128)S(1)}) custom-call(s32[1,128]{1,0:T(1,128)S(1)} %pad_bitcast_fusion.refs_0_, ...), custom_call_target="tpu_custom_call", output_to_operand_aliasing={{0}: (1, {})} | custom-call | bytes 17000000 | tf_op jit(solution)/shard_map/pallas_call | solution.py:114
  24.6 2.0 %collective-permute-start.5 = (bf16[1024,256]{1,0:T(8,128)(2,1)S(1)}, bf16[1024,256]{1,0:T(8,128)(2,1)S(1)}, u32[]{:S(2)}, u32[]{:S(2)}) collective-permute-start(bf16[1024,256]{1,0:T(8,128)(2,1)S(1)} %get-tuple-element.66.refs_5_), channel_id=1, source_target_pairs={{0,2},{1,3},{2,0},{3,1},{4,6},{5,7},{6,4},{7,5},{8,10},{9,11},{10,... | collective-permute-start | bytes 1572872 | tf_op jit(solution)/shard_map/ppermute | solution.py:499
  28.3 2.3 %collective-permute-done.11.refs_3_ = bf16[1024,256]{1,0:T(8,128)(2,1)S(1)} collective-permute-done((bf16[1024,256]{1,0:T(8,128)(2,1)S(1)}, bf16[1024,256]{1,0:T(8,128)(2,1)S(1)}, u32[]{:S(2)}, u32[]{:S(2)}) %collective-permute-start.11) | collective-permute-done | bytes 524320 | tf_op jit(solution)/shard_map/ppermute | solution.py:499
  31.2 2.5 %collective-permute-start.13 = (bf16[1024,256]{1,0:T(8,128)(2,1)S(1)}, bf16[1024,256]{1,0:T(8,128)(2,1)S(1)}, u32[]{:S(2)}, u32[]{:S(2)}) collective-permute-start(bf16[1024,256]{1,0:T(8,128)(2,1)S(1)} %get-tuple-element.78), channel_id=1, source_target_pairs={{0,2},{1,3},{2,0},{3,1},{4,6},{5,7},{6,4},{7,5},{8,10},{9,11},{10,... | collective-permute-start | bytes 1572872 | tf_op jit(solution)/shard_map/ppermute | solution.py:499
  33.6 8.2 %collective-permute-done.5.refs_3_ = bf16[1024,256]{1,0:T(8,128)(2,1)S(1)} collective-permute-done((bf16[1024,256]{1,0:T(8,128)(2,1)S(1)}, bf16[1024,256]{1,0:T(8,128)(2,1)S(1)}, u32[]{:S(2)}, u32[]{:S(2)}) %collective-permute-start.5) | collective-permute-done | bytes 524320 | tf_op jit(solution)/shard_map/ppermute | solution.py:499
  42.5 2.5 %collective-permute-start.7 = (bf16[1024,256]{1,0:T(8,128)(2,1)S(1)}, bf16[1024,256]{1,0:T(8,128)(2,1)S(1)}, u32[]{:S(2)}, u32[]{:S(2)}) collective-permute-start(bf16[1024,256]{1,0:T(8,128)(2,1)S(1)} %get-tuple-element.68.refs_7_), channel_id=1, source_target_pairs={{0,2},{1,3},{2,0},{3,1},{4,6},{5,7},{6,4},{7,5},{8,10},{9,11},{10,... | collective-permute-start | bytes 1572872 | tf_op jit(solution)/shard_map/ppermute | solution.py:499
  45.0 1.6 %shard_map.135 = (bf16[256,1024]{1,0:T(8,128)(2,1)S(1)}, bf16[256,8192]{1,0:T(8,128)(2,1)}, f32[8,128]{1,0:T(8,128)S(1)}) custom-call(s32[1,128]{1,0:T(1,128)S(1)} %pad_bitcast_fusion.refs_0_, bf16[256,512]{1,0:T(8,128)(2,1)S(1)} %bitcast.47, bf16[256,512]{1,0:T(8,128)(2,1)S(1)} %collective-permute-done.refs_2_.refs_3_, ...), custom_call_target="tpu_custom_call", output_to_operand_aliasing={{1}: (6, {})} | custom-call | bytes 7140000 | tf_op jit(solution)/shard_map/pallas_call | solution.py:114
  46.8 6.3 %collective-permute-done.13.refs_3_ = bf16[1024,256]{1,0:T(8,128)(2,1)S(1)} collective-permute-done((bf16[1024,256]{1,0:T(8,128)(2,1)S(1)}, bf16[1024,256]{1,0:T(8,128)(2,1)S(1)}, u32[]{:S(2)}, u32[]{:S(2)}) %collective-permute-start.13) | collective-permute-done | bytes 524320 | tf_op jit(solution)/shard_map/ppermute | solution.py:499
  53.8 2.5 %collective-permute-start.16 = (bf16[1024,256]{1,0:T(8,128)(2,1)S(1)}, bf16[1024,256]{1,0:T(8,128)(2,1)S(1)}, u32[]{:S(2)}, u32[]{:S(2)}) collective-permute-start(bf16[1024,256]{1,0:T(8,128)(2,1)S(1)} %get-tuple-element.85), channel_id=1, source_target_pairs={{0,2},{1,3},{2,0},{3,1},{4,6},{5,7},{6,4},{7,5},{8,10},{9,11},{10,... | collective-permute-start | bytes 1572872 | tf_op jit(solution)/shard_map/ppermute | solution.py:499
  56.3 8.1 %collective-permute-done.7.refs_3_ = bf16[1024,256]{1,0:T(8,128)(2,1)S(1)} collective-permute-done((bf16[1024,256]{1,0:T(8,128)(2,1)S(1)}, bf16[1024,256]{1,0:T(8,128)(2,1)S(1)}, u32[]{:S(2)}, u32[]{:S(2)}) %collective-permute-start.7) | collective-permute-done | bytes 524320 | tf_op jit(solution)/shard_map/ppermute | solution.py:499
  64.9 1.6 %shard_map.137 = (bf16[256,1024]{1,0:T(8,128)(2,1)S(1)}, bf16[256,8192]{1,0:T(8,128)(2,1)}, f32[8,128]{1,0:T(8,128)S(1)}) custom-call(s32[1,128]{1,0:T(1,128)S(1)} %pad_bitcast_fusion.refs_0_, bf16[256,512]{1,0:T(8,128)(2,1)S(1)} %bitcast.48, bf16[256,512]{1,0:T(8,128)(2,1)S(1)} %collective-permute-done.refs_2_.refs_3_, ...), custom_call_target="tpu_custom_call", output_to_operand_aliasing={{1}: (6, {})} | custom-call | bytes 7140000 | tf_op jit(solution)/shard_map/pallas_call | solution.py:114
  66.7 2.2 %collective-permute-start.8 = (bf16[1024,256]{1,0:T(8,128)(2,1)S(1)}, bf16[1024,256]{1,0:T(8,128)(2,1)S(1)}, u32[]{:S(2)}, u32[]{:S(2)}) collective-permute-start(bf16[1024,256]{1,0:T(8,128)(2,1)S(1)} %get-tuple-element.69.refs_7_), channel_id=1, source_target_pairs={{0,2},{1,3},{2,0},{3,1},{4,6},{5,7},{6,4},{7,5},{8,10},{9,11},{10,... | collective-permute-start | bytes 1572872 | tf_op jit(solution)/shard_map/ppermute | solution.py:499
  69.0 6.6 %collective-permute-done.16.refs_3_ = bf16[1024,256]{1,0:T(8,128)(2,1)S(1)} collective-permute-done((bf16[1024,256]{1,0:T(8,128)(2,1)S(1)}, bf16[1024,256]{1,0:T(8,128)(2,1)S(1)}, u32[]{:S(2)}, u32[]{:S(2)}) %collective-permute-start.16) | collective-permute-done | bytes 524320 | tf_op jit(solution)/shard_map/ppermute | solution.py:499
  76.2 1.6 %shard_map.139 = (bf16[256,1024]{1,0:T(8,128)(2,1)S(1)}, bf16[256,8192]{1,0:T(8,128)(2,1)}, f32[8,128]{1,0:T(8,128)S(1)}) custom-call(s32[1,128]{1,0:T(1,128)S(1)} %pad_bitcast_fusion.refs_0_, bf16[256,512]{1,0:T(8,128)(2,1)S(1)} %bitcast.49, bf16[256,512]{1,0:T(8,128)(2,1)S(1)} %collective-permute-done.refs_2_.refs_3_, ...), custom_call_target="tpu_custom_call", output_to_operand_aliasing={{1}: (6, {})} | custom-call | bytes 7140000 | tf_op jit(solution)/shard_map/pallas_call | solution.py:114
  77.9 2.2 %collective-permute-start.20 = (bf16[1024,256]{1,0:T(8,128)(2,1)S(1)}, bf16[1024,256]{1,0:T(8,128)(2,1)S(1)}, u32[]{:S(2)}, u32[]{:S(2)}) collective-permute-start(bf16[1024,256]{1,0:T(8,128)(2,1)S(1)} %get-tuple-element.100), channel_id=1, source_target_pairs={{0,2},{1,3},{2,0},{3,1},{4,6},{5,7},{6,4},{7,5},{8,10},{9,11},{10,... | collective-permute-start | bytes 1572872 | tf_op jit(solution)/shard_map/ppermute | solution.py:499
  80.3 6.6 %collective-permute-done.8.refs_2_ = bf16[1024,256]{1,0:T(8,128)(2,1)S(1)} collective-permute-done((bf16[1024,256]{1,0:T(8,128)(2,1)S(1)}, bf16[1024,256]{1,0:T(8,128)(2,1)S(1)}, u32[]{:S(2)}, u32[]{:S(2)}) %collective-permute-start.8) | collective-permute-done | bytes 524320 | tf_op jit(solution)/shard_map/ppermute | solution.py:499
  87.4 1.6 %collective-permute-start.23 = (bf16[512,128]{1,0:T(8,128)(2,1)S(1)}, bf16[512,128]{1,0:T(8,128)(2,1)S(1)}, u32[]{:S(2)}, u32[]{:S(2)}) collective-permute-start(bf16[512,128]{1,0:T(8,128)(2,1)S(1)} %get-tuple-element.107), channel_id=1, source_target_pairs={{0,16},{8,24},{16,0},{24,8},{1,17},{9,25},{17,1},{25,9},{2,18},{10... | collective-permute-start | bytes 393224 | tf_op jit(solution)/shard_map/ppermute | solution.py:499
  90.4 1.9 %shard_map.141 = (f32[1024,512]{1,0:T(8,128)}, f32[1024,512]{1,0:T(8,128)}, f32[1024,512]{1,0:T(8,128)}, bf16[256,8192]{1,0:T(8,128)(2,1)}, f32[8,128]{1,0:T(8,128)S(1)}) custom-call(s32[1,128]{1,0:T(1,128)S(1)} %pad_bitcast_fusion.refs_0_, f32[4096,512]{1,0:T(8,128)S(1)} %get-tuple-element.64.refs_1_, ...), custom_call_target="tpu_custom_call", output_to_operand_aliasing={{3}: (10, {})} | custom-call | bytes 6800000 | tf_op jit(solution)/shard_map/pallas_call | solution.py:114
  96.1 1.6 %collective-permute-done.20.refs_2_ = bf16[1024,256]{1,0:T(8,128)(2,1)S(1)} collective-permute-done((bf16[1024,256]{1,0:T(8,128)(2,1)S(1)}, bf16[1024,256]{1,0:T(8,128)(2,1)S(1)}, u32[]{:S(2)}, u32[]{:S(2)}) %collective-permute-start.20) | collective-permute-done | bytes 524320 | tf_op jit(solution)/shard_map/ppermute | solution.py:499
  97.7 1.9 %shard_map.142 = (f32[1024,512]{1,0:T(8,128)}, f32[1024,512]{1,0:T(8,128)}, f32[1024,512]{1,0:T(8,128)}, f32[3,256,256]{2,1,0:T(8,128)S(1)}) custom-call(s32[1,128]{1,0:T(1,128)S(1)} %pad_bitcast_fusion.refs_0_, f32[4096,512]{1,0:T(8,128)S(1)} %get-tuple-element.64.refs_1_, ...), custom_call_target="tpu_custom_call", output_to_operand_aliasing={{0}: (7, {}), {1}: (8, {}), {2}: (9, {})} | custom-call | bytes 8160000 | tf_op jit(solution)/shard_map/pallas_call | solution.py:114
  99.6 1.6 %shard_map.143 = (f32[1024,512]{1,0:T(8,128)}, f32[1024,512]{1,0:T(8,128)}, f32[1024,512]{1,0:T(8,128)}, f32[1024,512]{1,0:T(8,128)}, f32[1024,512]{1,0:T(8,128)}) custom-call(s32[1,128]{1,0:T(1,128)S(1)} %pad_bitcast_fusion.refs_0_, ...), custom_call_target="tpu_custom_call", output_to_operand_aliasing={{0}: (8, {}), {1}: (9, {}), {2}: (10, {}), {3}: (11, {}), {... | custom-call | bytes 6800000 | tf_op jit(solution)/shard_map/pallas_call | solution.py:114
  (52 shorter events, 16.5 us)
Async XLA Ops:
  0.6 19.1 %collective-permute-start.1 = (bf16[256,8192]{1,0:T(8,128)(2,1)}, bf16[256,8192]{1,0:T(8,128)(2,1)}, u32[]{:S(2)}, u32[]{:S(2)}) collective-permute-start(bf16[256,8192]{1,0:T(8,128)(2,1)} %bitcast.57), channel_id=1, source_target_pairs={{0,1},{1,0},{2,3},{3,2},{4,5},{5,4},{6,7},{7,6},{8,9},{9,8},{10,11... | collective-permute-start | bytes 12582920 | tf_op jit(solution)/shard_map/ppermute | solution.py:499
  2.5 21.6 %collective-permute-start.2 = (bf16[1024,256]{1,0:T(8,128)(2,1)S(1)}, bf16[1024,256]{1,0:T(8,128)(2,1)S(1)}, u32[]{:S(2)}, u32[]{:S(2)}) collective-permute-start(bf16[1024,256]{1,0:T(8,128)(2,1)S(1)} %slice.13.refs_3_), channel_id=1, source_target_pairs={{0,1},{1,0},{2,4},{3,5},{4,2},{5,3},{6,7},{7,6},{8,9},{9,8},{10,12... | collective-permute-start | bytes 1572872 | tf_op jit(solution)/shard_map/ppermute | solution.py:499
  2.6 21.5 %collective-permute-start.3 = (bf16[1024,256]{1,0:T(8,128)(2,1)S(1)}, bf16[1024,256]{1,0:T(8,128)(2,1)S(1)}, u32[]{:S(2)}, u32[]{:S(2)}) collective-permute-start(bf16[1024,256]{1,0:T(8,128)(2,1)S(1)} %slice.13.refs_3_), channel_id=1, source_target_pairs={{0,2},{1,3},{2,0},{3,1},{4,6},{5,7},{6,4},{7,5},{8,10},{9,11},{10,... | collective-permute-start | bytes 1572872 | tf_op jit(solution)/shard_map/ppermute | solution.py:499
  10.5 17.9 %collective-permute-start.10 = (bf16[1024,256]{1,0:T(8,128)(2,1)S(1)}, bf16[1024,256]{1,0:T(8,128)(2,1)S(1)}, u32[]{:S(2)}, u32[]{:S(2)}) collective-permute-start(bf16[1024,256]{1,0:T(8,128)(2,1)S(1)} %shard_map.127.refs_5_.refs_4_), channel_id=1, source_target_pairs={{0,1},{1,0},{2,4},{3,5},{4,2},{5,3},{6,7},{7,6},{8,9},{9,8},{10,12... | collective-permute-start | bytes 1572872 | tf_op jit(solution)/shard_map/ppermute | solution.py:499
  10.7 20.0 %collective-permute-start.11 = (bf16[1024,256]{1,0:T(8,128)(2,1)S(1)}, bf16[1024,256]{1,0:T(8,128)(2,1)S(1)}, u32[]{:S(2)}, u32[]{:S(2)}) collective-permute-start(bf16[1024,256]{1,0:T(8,128)(2,1)S(1)} %shard_map.127.refs_5_.refs_4_), channel_id=1, source_target_pairs={{0,2},{1,3},{2,0},{3,1},{4,6},{5,7},{6,4},{7,5},{8,10},{9,11},{10,... | collective-permute-start | bytes 1572872 | tf_op jit(solution)/shard_map/ppermute | solution.py:499
  24.6 9.1 %collective-permute-start.4 = (bf16[1024,256]{1,0:T(8,128)(2,1)S(1)}, bf16[1024,256]{1,0:T(8,128)(2,1)S(1)}, u32[]{:S(2)}, u32[]{:S(2)}) collective-permute-start(bf16[1024,256]{1,0:T(8,128)(2,1)S(1)} %get-tuple-element.65), channel_id=1, source_target_pairs={{0,1},{1,0},{2,4},{3,5},{4,2},{5,3},{6,7},{7,6},{8,9},{9,8},{10,12... | collective-permute-start | bytes 1572872 | tf_op jit(solution)/shard_map/ppermute | solution.py:499
  24.6 17.2 %collective-permute-start.5 = (bf16[1024,256]{1,0:T(8,128)(2,1)S(1)}, bf16[1024,256]{1,0:T(8,128)(2,1)S(1)}, u32[]{:S(2)}, u32[]{:S(2)}) collective-permute-start(bf16[1024,256]{1,0:T(8,128)(2,1)S(1)} %get-tuple-element.66.refs_5_), channel_id=1, source_target_pairs={{0,2},{1,3},{2,0},{3,1},{4,6},{5,7},{6,4},{7,5},{8,10},{9,11},{10,... | collective-permute-start | bytes 1572872 | tf_op jit(solution)/shard_map/ppermute | solution.py:499
  28.3 16.8 %collective-permute-start.14 = (bf16[256,1024]{1,0:T(8,128)(2,1)S(1)}, bf16[256,1024]{1,0:T(8,128)(2,1)S(1)}, u32[]{:S(2)}, u32[]{:S(2)}) collective-permute-start(bf16[256,1024]{1,0:T(8,128)(2,1)S(1)} %get-tuple-element.81), channel_id=1, source_target_pairs={{0,1},{1,0},{2,3},{3,2},{4,5},{5,4},{6,7},{7,6},{8,9},{9,8},{10,11... | collective-permute-start | bytes 1572872 | tf_op jit(solution)/shard_map/ppermute | solution.py:499
  31.1 15.7 %collective-permute-start.12 = (bf16[1024,256]{1,0:T(8,128)(2,1)S(1)}, bf16[1024,256]{1,0:T(8,128)(2,1)S(1)}, u32[]{:S(2)}, u32[]{:S(2)}) collective-permute-start(bf16[1024,256]{1,0:T(8,128)(2,1)S(1)} %get-tuple-element.77), channel_id=1, source_target_pairs={{0,1},{1,0},{2,4},{3,5},{4,2},{5,3},{6,7},{7,6},{8,9},{9,8},{10,12... | collective-permute-start | bytes 1572872 | tf_op jit(solution)/shard_map/ppermute | solution.py:499
  31.2 21.9 %collective-permute-start.13 = (bf16[1024,256]{1,0:T(8,128)(2,1)S(1)}, bf16[1024,256]{1,0:T(8,128)(2,1)S(1)}, u32[]{:S(2)}, u32[]{:S(2)}) collective-permute-start(bf16[1024,256]{1,0:T(8,128)(2,1)S(1)} %get-tuple-element.78), channel_id=1, source_target_pairs={{0,2},{1,3},{2,0},{3,1},{4,6},{5,7},{6,4},{7,5},{8,10},{9,11},{10,... | collective-permute-start | bytes 1572872 | tf_op jit(solution)/shard_map/ppermute | solution.py:499
  42.4 13.8 %collective-permute-start.6 = (bf16[1024,256]{1,0:T(8,128)(2,1)S(1)}, bf16[1024,256]{1,0:T(8,128)(2,1)S(1)}, u32[]{:S(2)}, u32[]{:S(2)}) collective-permute-start(bf16[1024,256]{1,0:T(8,128)(2,1)S(1)} %get-tuple-element.67), channel_id=1, source_target_pairs={{0,1},{1,0},{2,4},{3,5},{4,2},{5,3},{6,7},{7,6},{8,9},{9,8},{10,12... | collective-permute-start | bytes 1572872 | tf_op jit(solution)/shard_map/ppermute | solution.py:499
  42.5 21.8 %collective-permute-start.7 = (bf16[1024,256]{1,0:T(8,128)(2,1)S(1)}, bf16[1024,256]{1,0:T(8,128)(2,1)S(1)}, u32[]{:S(2)}, u32[]{:S(2)}) collective-permute-start(bf16[1024,256]{1,0:T(8,128)(2,1)S(1)} %get-tuple-element.68.refs_7_), channel_id=1, source_target_pairs={{0,2},{1,3},{2,0},{3,1},{4,6},{5,7},{6,4},{7,5},{8,10},{9,11},{10,... | collective-permute-start | bytes 1572872 | tf_op jit(solution)/shard_map/ppermute | solution.py:499
  46.7 18.2 %collective-permute-start.17 = (bf16[256,1024]{1,0:T(8,128)(2,1)S(1)}, bf16[256,1024]{1,0:T(8,128)(2,1)S(1)}, u32[]{:S(2)}, u32[]{:S(2)}) collective-permute-start(bf16[256,1024]{1,0:T(8,128)(2,1)S(1)} %get-tuple-element.88), channel_id=1, source_target_pairs={{0,1},{1,0},{2,3},{3,2},{4,5},{5,4},{6,7},{7,6},{8,9},{9,8},{10,11... | collective-permute-start | bytes 1572872 | tf_op jit(solution)/shard_map/ppermute | solution.py:499
  53.7 15.3 %collective-permute-start.15 = (bf16[1024,256]{1,0:T(8,128)(2,1)S(1)}, bf16[1024,256]{1,0:T(8,128)(2,1)S(1)}, u32[]{:S(2)}, u32[]{:S(2)}) collective-permute-start(bf16[1024,256]{1,0:T(8,128)(2,1)S(1)} %get-tuple-element.84), channel_id=1, source_target_pairs={{0,1},{1,0},{2,4},{3,5},{4,2},{5,3},{6,7},{7,6},{8,9},{9,8},{10,12... | collective-permute-start | bytes 1572872 | tf_op jit(solution)/shard_map/ppermute | solution.py:499
  53.8 21.8 %collective-permute-start.16 = (bf16[1024,256]{1,0:T(8,128)(2,1)S(1)}, bf16[1024,256]{1,0:T(8,128)(2,1)S(1)}, u32[]{:S(2)}, u32[]{:S(2)}) collective-permute-start(bf16[1024,256]{1,0:T(8,128)(2,1)S(1)} %get-tuple-element.85), channel_id=1, source_target_pairs={{0,2},{1,3},{2,0},{3,1},{4,6},{5,7},{6,4},{7,5},{8,10},{9,11},{10,... | collective-permute-start | bytes 1572872 | tf_op jit(solution)/shard_map/ppermute | solution.py:499
  66.6 9.6 %collective-permute-start.18 = (bf16[256,1024]{1,0:T(8,128)(2,1)S(1)}, bf16[256,1024]{1,0:T(8,128)(2,1)S(1)}, u32[]{:S(2)}, u32[]{:S(2)}) collective-permute-start(bf16[256,1024]{1,0:T(8,128)(2,1)S(1)} %get-tuple-element.92), channel_id=1, source_target_pairs={{0,1},{1,0},{2,3},{3,2},{4,5},{5,4},{6,7},{7,6},{8,9},{9,8},{10,11... | collective-permute-start | bytes 1572872 | tf_op jit(solution)/shard_map/ppermute | solution.py:499
  66.7 20.2 %collective-permute-start.8 = (bf16[1024,256]{1,0:T(8,128)(2,1)S(1)}, bf16[1024,256]{1,0:T(8,128)(2,1)S(1)}, u32[]{:S(2)}, u32[]{:S(2)}) collective-permute-start(bf16[1024,256]{1,0:T(8,128)(2,1)S(1)} %get-tuple-element.69.refs_7_), channel_id=1, source_target_pairs={{0,2},{1,3},{2,0},{3,1},{4,6},{5,7},{6,4},{7,5},{8,10},{9,11},{10,... | collective-permute-start | bytes 1572872 | tf_op jit(solution)/shard_map/ppermute | solution.py:499
  68.9 18.0 %collective-permute-start.9 = (bf16[1024,256]{1,0:T(8,128)(2,1)S(1)}, bf16[1024,256]{1,0:T(8,128)(2,1)S(1)}, u32[]{:S(2)}, u32[]{:S(2)}) collective-permute-start(bf16[1024,256]{1,0:T(8,128)(2,1)S(1)} %get-tuple-element.70), channel_id=1, source_target_pairs={{0,1},{1,0},{2,4},{3,5},{4,2},{5,3},{6,7},{7,6},{8,9},{9,8},{10,12... | collective-permute-start | bytes 1572872 | tf_op jit(solution)/shard_map/ppermute | solution.py:499
  77.8 12.6 %collective-permute-start.19 = (bf16[256,1024]{1,0:T(8,128)(2,1)S(1)}, bf16[256,1024]{1,0:T(8,128)(2,1)S(1)}, u32[]{:S(2)}, u32[]{:S(2)}) collective-permute-start(bf16[256,1024]{1,0:T(8,128)(2,1)S(1)} %get-tuple-element.97), channel_id=1, source_target_pairs={{0,1},{1,0},{2,3},{3,2},{4,5},{5,4},{6,7},{7,6},{8,9},{9,8},{10,11... | collective-permute-start | bytes 1572872 | tf_op jit(solution)/shard_map/ppermute | solution.py:499
  77.9 19.8 %collective-permute-start.20 = (bf16[1024,256]{1,0:T(8,128)(2,1)S(1)}, bf16[1024,256]{1,0:T(8,128)(2,1)S(1)}, u32[]{:S(2)}, u32[]{:S(2)}) collective-permute-start(bf16[1024,256]{1,0:T(8,128)(2,1)S(1)} %get-tuple-element.100), channel_id=1, source_target_pairs={{0,2},{1,3},{2,0},{3,1},{4,6},{5,7},{6,4},{7,5},{8,10},{9,11},{10,... | collective-permute-start | bytes 1572872 | tf_op jit(solution)/shard_map/ppermute | solution.py:499
  80.1 17.6 %collective-permute-start.21 = (bf16[1024,256]{1,0:T(8,128)(2,1)S(1)}, bf16[1024,256]{1,0:T(8,128)(2,1)S(1)}, u32[]{:S(2)}, u32[]{:S(2)}) collective-permute-start(bf16[1024,256]{1,0:T(8,128)(2,1)S(1)} %get-tuple-element.101), channel_id=1, source_target_pairs={{0,1},{1,0},{2,4},{3,5},{4,2},{5,3},{6,7},{7,6},{8,9},{9,8},{10,12... | collective-permute-start | bytes 1572872 | tf_op jit(solution)/shard_map/ppermute | solution.py:499
  87.4 5.0 %collective-permute-start.23 = (bf16[512,128]{1,0:T(8,128)(2,1)S(1)}, bf16[512,128]{1,0:T(8,128)(2,1)S(1)}, u32[]{:S(2)}, u32[]{:S(2)}) collective-permute-start(bf16[512,128]{1,0:T(8,128)(2,1)S(1)} %get-tuple-element.107), channel_id=1, source_target_pairs={{0,16},{8,24},{16,0},{24,8},{1,17},{9,25},{17,1},{25,9},{2,18},{10... | collective-permute-start | bytes 393224 | tf_op jit(solution)/shard_map/ppermute | solution.py:499
  94.0 5.6 %collective-permute-start.24 = (bf16[512,128]{1,0:T(8,128)(2,1)S(1)}, bf16[512,128]{1,0:T(8,128)(2,1)S(1)}, u32[]{:S(2)}, u32[]{:S(2)}) collective-permute-start(bf16[512,128]{1,0:T(8,128)(2,1)S(1)} %get-tuple-element.121.refs_10_.refs_2_), channel_id=1, source_target_pairs={{0,16},{8,24},{16,0},{24,8},{1,17},{9,25},{17,1},{25,9},{2,18},{10... | collective-permute-start | bytes 393224 | tf_op jit(solution)/shard_map/ppermute | solution.py:499
  94.6 5.0 %collective-permute-start.25 = (bf16[512,128]{1,0:T(8,128)(2,1)S(1)}, bf16[512,128]{1,0:T(8,128)(2,1)S(1)}, u32[]{:S(2)}, u32[]{:S(2)}) collective-permute-start(bf16[512,128]{1,0:T(8,128)(2,1)S(1)} %get-tuple-element.120.refs_11_.refs_4_), channel_id=1, source_target_pairs={{0,8},{8,0},{16,24},{24,16},{1,9},{9,1},{17,25},{25,17},{2,10},{10... | collective-permute-start | bytes 393224 | tf_op jit(solution)/shard_map/ppermute | solution.py:499
  (3 other events, 20.7 us)

commit v6 on v5

--- a/solution.py
+++ b/solution.py
@@ -409,8 +409,13 @@
         copy.wait()
 
 
-def mix(own, other, token):
-    return (own.astype(F32) + other.astype(F32) + token[:1]).astype(BF16)
+def mix_body(s, own, other, out):
+    size = 128
+
+    @pl.loop(0, out.shape[0] // size)
+    def _(i):
+        here = pl.ds(pl.multiple_of(i * size, size), size)
+        out[here, :] = (own[here, :].astype(F32) + other[here, :].astype(F32)).astype(BF16)
 
 
 def outer_body(at, s, left, upper, upper_in, lower, lower_in, anchor, moment, *rest):
@@ -618,8 +623,9 @@
         {9: 3},
         us=2.0,
     )
-    upper, lower = mix(upper, upper_in, token), mix(lower, lower_in, token)
+    upper = call(mix_body, s, [Held(upper), Held(upper_in)], [half], after=(token,), us=0.5)[0]
     upper_in = permute(upper, y_perm, "group")
+    lower = call(mix_body, s, [Held(lower), Held(lower_in)], [half], after=(upper,), us=0.5)[0]
     lower_in = permute(lower, x_perm, "group")
     offset, part = PARTS[1]
     *state, left = call(

time: 101 us -> 101 us (level)
  waiting for transfers between devices: 42.8 us -> 41.7 us
    ppermute x26, waiting for transfers between devices: 42.8 us -> 41.7 us  [permute(): return lax.ppermute(x, axis, perm)]
    ppermute x26, starting transfers between devices: 28.7 us -> 29.7 us  [permute(): return lax.ppermute(x, axis, perm)]
    pallas_call x17 -> x19, Pallas kernels: 26.5 us -> 26.6 us  [call(): pl.pallas_call(inner, in_specs=specs, out_specs=[pl.BlockSpec(memory_spac...]
  transfers between devices with their start and end apart: 26 -> 26, of which waited for: 10 -> 9; matrix products, arithmetic and copies ran while one was open for 2% -> 1% of each run, Pallas kernels for 25% -> 25%
where the time goes in v6:
time: 101 us
  waiting for transfers between devices  41.7 us (41%)
  starting transfers between devices  29.7 us (29%)
  Pallas kernels  26.6 us (26%)
  between operations  1.73 us (2%)
  local copies, waits for them, and re-layouts  1.45 us (1%)
    ppermute x26, waiting for transfers between devices, permute(): return lax.ppermute(x, axis, perm)  41.7 us
    ppermute x26, starting transfers between devices, permute(): return lax.ppermute(x, axis, perm)  29.7 us
    pallas_call x19, Pallas kernels, call(): pl.pallas_call(inner, in_specs=specs, out_specs=[pl.BlockSpec(memory_spac...  26.6 us
  transfers between devices with their start and end apart: 26, of which 9 were waited for; matrix products, arithmetic and copies ran while one was open for 1% of the time, Pallas kernels for 25%

profile of v6, /device:TPU:0, one launch (start us, length us, event | category | flops | bytes accessed | tf_op | source)
XLA Modules:
  0.0 101.3 jit_solution(10966569452733273746)
XLA Ops:
  2.6 4.1 %collective-permute-start.3 = (bf16[1024,256]{1,0:T(8,128)(2,1)S(1)}, bf16[1024,256]{1,0:T(8,128)(2,1)S(1)}, u32[]{:S(2)}, u32[]{:S(2)}) collective-permute-start(bf16[1024,256]{1,0:T(8,128)(2,1)S(1)} %slice.7.refs_3_), channel_id=1, source_target_pairs={{0,2},{1,3},{2,0},{3,1},{4,6},{5,7},{6,4},{7,5},{8,10},{9,11},{10,... | collective-permute-start | bytes 1572872 | tf_op jit(solution)/shard_map/ppermute | solution.py:504
  10.7 3.7 %collective-permute-start.11 = (bf16[1024,256]{1,0:T(8,128)(2,1)S(1)}, bf16[1024,256]{1,0:T(8,128)(2,1)S(1)}, u32[]{:S(2)}, u32[]{:S(2)}) collective-permute-start(bf16[1024,256]{1,0:T(8,128)(2,1)S(1)} %shard_map.127.refs_5_.refs_4_), channel_id=1, source_target_pairs={{0,2},{1,3},{2,0},{3,1},{4,6},{5,7},{6,4},{7,5},{8,10},{9,11},{10,... | collective-permute-start | bytes 1572872 | tf_op jit(solution)/shard_map/ppermute | solution.py:504
  14.4 5.3 %shard_map.128 = (f32[4096,512]{1,0:T(8,128)S(1)}, f32[1024,512]{1,0:T(8,128)}, f32[1024,512]{1,0:T(8,128)}) custom-call(s32[1,128]{1,0:T(1,128)S(1)} %pad_bitcast_fusion.refs_0_, bf16[256,8192]{1,0:T(8,128)(2,1)} %bitcast.56, bf16[256,512]{1,0:T(8,128)(2,1)S(1)} %bitcast.43, f32[1024,512]{1,0:T(8,128)} %refs_7_.1, f32[1024,512]{1,0:T(8,128)} %refs_8_.1, ...), custom_call_target="tpu_custom_call" | custom-call | bytes 17000000 | tf_op jit(solution)/shard_map/pallas_call | solution.py:114
  19.7 4.3 %shard_map.129 = (f32[4096,512]{1,0:T(8,128)S(1)}, f32[1024,512]{1,0:T(8,128)S(1)}, f32[1024,512]{1,0:T(8,128)S(1)}, f32[1024,512]{1,0:T(8,128)S(1)}, f32[1024,128]{1,0:T(8,128)S(1)}, /*index=5*/f32[1024,128]{1,0:T(8,128)S(1)}) custom-call(s32[1,128]{1,0:T(1,128)S(1)} %pad_bitcast_fusion.refs_0_, ...), custom_call_target="tpu_custom_call", output_to_operand_aliasing={{0}: (1, {})} | custom-call | bytes 17000000 | tf_op jit(solution)/shard_map/pallas_call | solution.py:114
  24.6 2.0 %collective-permute-start.5 = (bf16[1024,256]{1,0:T(8,128)(2,1)S(1)}, bf16[1024,256]{1,0:T(8,128)(2,1)S(1)}, u32[]{:S(2)}, u32[]{:S(2)}) collective-permute-start(bf16[1024,256]{1,0:T(8,128)(2,1)S(1)} %get-tuple-element.66.refs_5_), channel_id=1, source_target_pairs={{0,2},{1,3},{2,0},{3,1},{4,6},{5,7},{6,4},{7,5},{8,10},{9,11},{10,... | collective-permute-start | bytes 1572872 | tf_op jit(solution)/shard_map/ppermute | solution.py:504
  28.3 2.3 %collective-permute-done.11.refs_3_ = bf16[1024,256]{1,0:T(8,128)(2,1)S(1)} collective-permute-done((bf16[1024,256]{1,0:T(8,128)(2,1)S(1)}, bf16[1024,256]{1,0:T(8,128)(2,1)S(1)}, u32[]{:S(2)}, u32[]{:S(2)}) %collective-permute-start.11) | collective-permute-done | bytes 524320 | tf_op jit(solution)/shard_map/ppermute | solution.py:504
  31.2 2.5 %collective-permute-start.13 = (bf16[1024,256]{1,0:T(8,128)(2,1)S(1)}, bf16[1024,256]{1,0:T(8,128)(2,1)S(1)}, u32[]{:S(2)}, u32[]{:S(2)}) collective-permute-start(bf16[1024,256]{1,0:T(8,128)(2,1)S(1)} %get-tuple-element.78), channel_id=1, source_target_pairs={{0,2},{1,3},{2,0},{3,1},{4,6},{5,7},{6,4},{7,5},{8,10},{9,11},{10,... | collective-permute-start | bytes 1572872 | tf_op jit(solution)/shard_map/ppermute | solution.py:504
  33.6 8.2 %collective-permute-done.5.refs_3_ = bf16[1024,256]{1,0:T(8,128)(2,1)S(1)} collective-permute-done((bf16[1024,256]{1,0:T(8,128)(2,1)S(1)}, bf16[1024,256]{1,0:T(8,128)(2,1)S(1)}, u32[]{:S(2)}, u32[]{:S(2)}) %collective-permute-start.5) | collective-permute-done | bytes 524320 | tf_op jit(solution)/shard_map/ppermute | solution.py:504
  42.5 2.5 %collective-permute-start.7 = (bf16[1024,256]{1,0:T(8,128)(2,1)S(1)}, bf16[1024,256]{1,0:T(8,128)(2,1)S(1)}, u32[]{:S(2)}, u32[]{:S(2)}) collective-permute-start(bf16[1024,256]{1,0:T(8,128)(2,1)S(1)} %get-tuple-element.68.refs_7_), channel_id=1, source_target_pairs={{0,2},{1,3},{2,0},{3,1},{4,6},{5,7},{6,4},{7,5},{8,10},{9,11},{10,... | collective-permute-start | bytes 1572872 | tf_op jit(solution)/shard_map/ppermute | solution.py:504
  45.0 1.6 %shard_map.135 = (bf16[256,1024]{1,0:T(8,128)(2,1)S(1)}, bf16[256,8192]{1,0:T(8,128)(2,1)}, f32[8,128]{1,0:T(8,128)S(1)}) custom-call(s32[1,128]{1,0:T(1,128)S(1)} %pad_bitcast_fusion.refs_0_, bf16[256,512]{1,0:T(8,128)(2,1)S(1)} %bitcast.45, bf16[256,512]{1,0:T(8,128)(2,1)S(1)} %collective-permute-done.refs_2_.refs_3_, ...), custom_call_target="tpu_custom_call", output_to_operand_aliasing={{1}: (6, {})} | custom-call | bytes 7140000 | tf_op jit(solution)/shard_map/pallas_call | solution.py:114
  46.8 6.3 %collective-permute-done.13.refs_3_ = bf16[1024,256]{1,0:T(8,128)(2,1)S(1)} collective-permute-done((bf16[1024,256]{1,0:T(8,128)(2,1)S(1)}, bf16[1024,256]{1,0:T(8,128)(2,1)S(1)}, u32[]{:S(2)}, u32[]{:S(2)}) %collective-permute-start.13) | collective-permute-done | bytes 524320 | tf_op jit(solution)/shard_map/ppermute | solution.py:504
  53.8 2.5 %collective-permute-start.16 = (bf16[1024,256]{1,0:T(8,128)(2,1)S(1)}, bf16[1024,256]{1,0:T(8,128)(2,1)S(1)}, u32[]{:S(2)}, u32[]{:S(2)}) collective-permute-start(bf16[1024,256]{1,0:T(8,128)(2,1)S(1)} %get-tuple-element.85), channel_id=1, source_target_pairs={{0,2},{1,3},{2,0},{3,1},{4,6},{5,7},{6,4},{7,5},{8,10},{9,11},{10,... | collective-permute-start | bytes 1572872 | tf_op jit(solution)/shard_map/ppermute | solution.py:504
  56.3 8.1 %collective-permute-done.7.refs_3_ = bf16[1024,256]{1,0:T(8,128)(2,1)S(1)} collective-permute-done((bf16[1024,256]{1,0:T(8,128)(2,1)S(1)}, bf16[1024,256]{1,0:T(8,128)(2,1)S(1)}, u32[]{:S(2)}, u32[]{:S(2)}) %collective-permute-start.7) | collective-permute-done | bytes 524320 | tf_op jit(solution)/shard_map/ppermute | solution.py:504
  64.9 1.6 %shard_map.137 = (bf16[256,1024]{1,0:T(8,128)(2,1)S(1)}, bf16[256,8192]{1,0:T(8,128)(2,1)}, f32[8,128]{1,0:T(8,128)S(1)}) custom-call(s32[1,128]{1,0:T(1,128)S(1)} %pad_bitcast_fusion.refs_0_, bf16[256,512]{1,0:T(8,128)(2,1)S(1)} %bitcast.46, bf16[256,512]{1,0:T(8,128)(2,1)S(1)} %collective-permute-done.refs_2_.refs_3_, ...), custom_call_target="tpu_custom_call", output_to_operand_aliasing={{1}: (6, {})} | custom-call | bytes 7140000 | tf_op jit(solution)/shard_map/pallas_call | solution.py:114
  66.7 2.2 %collective-permute-start.8 = (bf16[1024,256]{1,0:T(8,128)(2,1)S(1)}, bf16[1024,256]{1,0:T(8,128)(2,1)S(1)}, u32[]{:S(2)}, u32[]{:S(2)}) collective-permute-start(bf16[1024,256]{1,0:T(8,128)(2,1)S(1)} %get-tuple-element.69.refs_7_), channel_id=1, source_target_pairs={{0,2},{1,3},{2,0},{3,1},{4,6},{5,7},{6,4},{7,5},{8,10},{9,11},{10,... | collective-permute-start | bytes 1572872 | tf_op jit(solution)/shard_map/ppermute | solution.py:504
  69.0 6.6 %collective-permute-done.16.refs_3_ = bf16[1024,256]{1,0:T(8,128)(2,1)S(1)} collective-permute-done((bf16[1024,256]{1,0:T(8,128)(2,1)S(1)}, bf16[1024,256]{1,0:T(8,128)(2,1)S(1)}, u32[]{:S(2)}, u32[]{:S(2)}) %collective-permute-start.16) | collective-permute-done | bytes 524320 | tf_op jit(solution)/shard_map/ppermute | solution.py:504
  76.2 1.6 %shard_map.139 = (bf16[256,1024]{1,0:T(8,128)(2,1)S(1)}, bf16[256,8192]{1,0:T(8,128)(2,1)}, f32[8,128]{1,0:T(8,128)S(1)}) custom-call(s32[1,128]{1,0:T(1,128)S(1)} %pad_bitcast_fusion.refs_0_, bf16[256,512]{1,0:T(8,128)(2,1)S(1)} %bitcast.47, bf16[256,512]{1,0:T(8,128)(2,1)S(1)} %collective-permute-done.refs_2_.refs_3_, ...), custom_call_target="tpu_custom_call", output_to_operand_aliasing={{1}: (6, {})} | custom-call | bytes 7140000 | tf_op jit(solution)/shard_map/pallas_call | solution.py:114
  77.9 2.2 %collective-permute-start.20 = (bf16[1024,256]{1,0:T(8,128)(2,1)S(1)}, bf16[1024,256]{1,0:T(8,128)(2,1)S(1)}, u32[]{:S(2)}, u32[]{:S(2)}) collective-permute-start(bf16[1024,256]{1,0:T(8,128)(2,1)S(1)} %get-tuple-element.100), channel_id=1, source_target_pairs={{0,2},{1,3},{2,0},{3,1},{4,6},{5,7},{6,4},{7,5},{8,10},{9,11},{10,... | collective-permute-start | bytes 1572872 | tf_op jit(solution)/shard_map/ppermute | solution.py:504
  80.3 6.6 %collective-permute-done.8.refs_2_ = bf16[1024,256]{1,0:T(8,128)(2,1)S(1)} collective-permute-done((bf16[1024,256]{1,0:T(8,128)(2,1)S(1)}, bf16[1024,256]{1,0:T(8,128)(2,1)S(1)}, u32[]{:S(2)}, u32[]{:S(2)}) %collective-permute-start.8) | collective-permute-done | bytes 524320 | tf_op jit(solution)/shard_map/ppermute | solution.py:504
  90.4 1.9 %shard_map.141 = (f32[1024,512]{1,0:T(8,128)}, f32[1024,512]{1,0:T(8,128)}, f32[1024,512]{1,0:T(8,128)}, bf16[256,8192]{1,0:T(8,128)(2,1)}, f32[8,128]{1,0:T(8,128)S(1)}) custom-call(s32[1,128]{1,0:T(1,128)S(1)} %pad_bitcast_fusion.refs_0_, f32[4096,512]{1,0:T(8,128)S(1)} %get-tuple-element.64.refs_1_, ...), custom_call_target="tpu_custom_call", output_to_operand_aliasing={{3}: (10, {})} | custom-call | bytes 6800000 | tf_op jit(solution)/shard_map/pallas_call | solution.py:114
  92.4 1.6 %collective-permute-start.24 = (bf16[512,128]{1,0:T(8,128)(2,1)S(1)}, bf16[512,128]{1,0:T(8,128)(2,1)S(1)}, u32[]{:S(2)}, u32[]{:S(2)}) collective-permute-start(bf16[512,128]{1,0:T(8,128)(2,1)S(1)} %shard_map.142.refs_3_.refs_10_.refs_2_), channel_id=1, source_target_pairs={{0,16},{8,24},{16,0},{24,8},{1,17},{9,25},{17,1},{25,9},{2,18},{10... | collective-permute-start | bytes 393224 | tf_op jit(solution)/shard_map/ppermute | solution.py:504
  95.6 2.0 %collective-permute-done.20.refs_2_ = bf16[1024,256]{1,0:T(8,128)(2,1)S(1)} collective-permute-done((bf16[1024,256]{1,0:T(8,128)(2,1)S(1)}, bf16[1024,256]{1,0:T(8,128)(2,1)S(1)}, u32[]{:S(2)}, u32[]{:S(2)}) %collective-permute-start.20) | collective-permute-done | bytes 524320 | tf_op jit(solution)/shard_map/ppermute | solution.py:504
  97.7 1.9 %shard_map.144 = (f32[1024,512]{1,0:T(8,128)}, f32[1024,512]{1,0:T(8,128)}, f32[1024,512]{1,0:T(8,128)}, f32[3,256,256]{2,1,0:T(8,128)S(1)}) custom-call(s32[1,128]{1,0:T(1,128)S(1)} %pad_bitcast_fusion.refs_0_, f32[4096,512]{1,0:T(8,128)S(1)} %get-tuple-element.64.refs_1_, ...), custom_call_target="tpu_custom_call", output_to_operand_aliasing={{0}: (7, {}), {1}: (8, {}), {2}: (9, {})} | custom-call | bytes 8160000 | tf_op jit(solution)/shard_map/pallas_call | solution.py:114
  99.6 1.6 %shard_map.145 = (f32[1024,512]{1,0:T(8,128)}, f32[1024,512]{1,0:T(8,128)}, f32[1024,512]{1,0:T(8,128)}, f32[1024,512]{1,0:T(8,128)}, f32[1024,512]{1,0:T(8,128)}) custom-call(s32[1,128]{1,0:T(1,128)S(1)} %pad_bitcast_fusion.refs_0_, ...), custom_call_target="tpu_custom_call", output_to_operand_aliasing={{0}: (8, {}), {1}: (9, {}), {2}: (10, {}), {3}: (11, {}), {... | custom-call | bytes 6800000 | tf_op jit(solution)/shard_map/pallas_call | solution.py:114
  (52 shorter events, 16.1 us)
Async XLA Ops:
  0.6 19.1 %collective-permute-start.1 = (bf16[256,8192]{1,0:T(8,128)(2,1)}, bf16[256,8192]{1,0:T(8,128)(2,1)}, u32[]{:S(2)}, u32[]{:S(2)}) collective-permute-start(bf16[256,8192]{1,0:T(8,128)(2,1)} %bitcast.55), channel_id=1, source_target_pairs={{0,1},{1,0},{2,3},{3,2},{4,5},{5,4},{6,7},{7,6},{8,9},{9,8},{10,11... | collective-permute-start | bytes 12582920 | tf_op jit(solution)/shard_map/ppermute | solution.py:504
  2.5 21.6 %collective-permute-start.2 = (bf16[1024,256]{1,0:T(8,128)(2,1)S(1)}, bf16[1024,256]{1,0:T(8,128)(2,1)S(1)}, u32[]{:S(2)}, u32[]{:S(2)}) collective-permute-start(bf16[1024,256]{1,0:T(8,128)(2,1)S(1)} %slice.7.refs_3_), channel_id=1, source_target_pairs={{0,1},{1,0},{2,4},{3,5},{4,2},{5,3},{6,7},{7,6},{8,9},{9,8},{10,12... | collective-permute-start | bytes 1572872 | tf_op jit(solution)/shard_map/ppermute | solution.py:504
  2.6 21.5 %collective-permute-start.3 = (bf16[1024,256]{1,0:T(8,128)(2,1)S(1)}, bf16[1024,256]{1,0:T(8,128)(2,1)S(1)}, u32[]{:S(2)}, u32[]{:S(2)}) collective-permute-start(bf16[1024,256]{1,0:T(8,128)(2,1)S(1)} %slice.7.refs_3_), channel_id=1, source_target_pairs={{0,2},{1,3},{2,0},{3,1},{4,6},{5,7},{6,4},{7,5},{8,10},{9,11},{10,... | collective-permute-start | bytes 1572872 | tf_op jit(solution)/shard_map/ppermute | solution.py:504
  10.5 17.9 %collective-permute-start.10 = (bf16[1024,256]{1,0:T(8,128)(2,1)S(1)}, bf16[1024,256]{1,0:T(8,128)(2,1)S(1)}, u32[]{:S(2)}, u32[]{:S(2)}) collective-permute-start(bf16[1024,256]{1,0:T(8,128)(2,1)S(1)} %shard_map.127.refs_5_.refs_4_), channel_id=1, source_target_pairs={{0,1},{1,0},{2,4},{3,5},{4,2},{5,3},{6,7},{7,6},{8,9},{9,8},{10,12... | collective-permute-start | bytes 1572872 | tf_op jit(solution)/shard_map/ppermute | solution.py:504
  10.7 20.0 %collective-permute-start.11 = (bf16[1024,256]{1,0:T(8,128)(2,1)S(1)}, bf16[1024,256]{1,0:T(8,128)(2,1)S(1)}, u32[]{:S(2)}, u32[]{:S(2)}) collective-permute-start(bf16[1024,256]{1,0:T(8,128)(2,1)S(1)} %shard_map.127.refs_5_.refs_4_), channel_id=1, source_target_pairs={{0,2},{1,3},{2,0},{3,1},{4,6},{5,7},{6,4},{7,5},{8,10},{9,11},{10,... | collective-permute-start | bytes 1572872 | tf_op jit(solution)/shard_map/ppermute | solution.py:504
  24.6 9.1 %collective-permute-start.4 = (bf16[1024,256]{1,0:T(8,128)(2,1)S(1)}, bf16[1024,256]{1,0:T(8,128)(2,1)S(1)}, u32[]{:S(2)}, u32[]{:S(2)}) collective-permute-start(bf16[1024,256]{1,0:T(8,128)(2,1)S(1)} %get-tuple-element.65), channel_id=1, source_target_pairs={{0,1},{1,0},{2,4},{3,5},{4,2},{5,3},{6,7},{7,6},{8,9},{9,8},{10,12... | collective-permute-start | bytes 1572872 | tf_op jit(solution)/shard_map/ppermute | solution.py:504
  24.6 17.2 %collective-permute-start.5 = (bf16[1024,256]{1,0:T(8,128)(2,1)S(1)}, bf16[1024,256]{1,0:T(8,128)(2,1)S(1)}, u32[]{:S(2)}, u32[]{:S(2)}) collective-permute-start(bf16[1024,256]{1,0:T(8,128)(2,1)S(1)} %get-tuple-element.66.refs_5_), channel_id=1, source_target_pairs={{0,2},{1,3},{2,0},{3,1},{4,6},{5,7},{6,4},{7,5},{8,10},{9,11},{10,... | collective-permute-start | bytes 1572872 | tf_op jit(solution)/shard_map/ppermute | solution.py:504
  28.3 16.8 %collective-permute-start.14 = (bf16[256,1024]{1,0:T(8,128)(2,1)S(1)}, bf16[256,1024]{1,0:T(8,128)(2,1)S(1)}, u32[]{:S(2)}, u32[]{:S(2)}) collective-permute-start(bf16[256,1024]{1,0:T(8,128)(2,1)S(1)} %get-tuple-element.81), channel_id=1, source_target_pairs={{0,1},{1,0},{2,3},{3,2},{4,5},{5,4},{6,7},{7,6},{8,9},{9,8},{10,11... | collective-permute-start | bytes 1572872 | tf_op jit(solution)/shard_map/ppermute | solution.py:504
  31.1 15.7 %collective-permute-start.12 = (bf16[1024,256]{1,0:T(8,128)(2,1)S(1)}, bf16[1024,256]{1,0:T(8,128)(2,1)S(1)}, u32[]{:S(2)}, u32[]{:S(2)}) collective-permute-start(bf16[1024,256]{1,0:T(8,128)(2,1)S(1)} %get-tuple-element.77), channel_id=1, source_target_pairs={{0,1},{1,0},{2,4},{3,5},{4,2},{5,3},{6,7},{7,6},{8,9},{9,8},{10,12... | collective-permute-start | bytes 1572872 | tf_op jit(solution)/shard_map/ppermute | solution.py:504
  31.2 21.9 %collective-permute-start.13 = (bf16[1024,256]{1,0:T(8,128)(2,1)S(1)}, bf16[1024,256]{1,0:T(8,128)(2,1)S(1)}, u32[]{:S(2)}, u32[]{:S(2)}) collective-permute-start(bf16[1024,256]{1,0:T(8,128)(2,1)S(1)} %get-tuple-element.78), channel_id=1, source_target_pairs={{0,2},{1,3},{2,0},{3,1},{4,6},{5,7},{6,4},{7,5},{8,10},{9,11},{10,... | collective-permute-start | bytes 1572872 | tf_op jit(solution)/shard_map/ppermute | solution.py:504
  42.4 13.8 %collective-permute-start.6 = (bf16[1024,256]{1,0:T(8,128)(2,1)S(1)}, bf16[1024,256]{1,0:T(8,128)(2,1)S(1)}, u32[]{:S(2)}, u32[]{:S(2)}) collective-permute-start(bf16[1024,256]{1,0:T(8,128)(2,1)S(1)} %get-tuple-element.67), channel_id=1, source_target_pairs={{0,1},{1,0},{2,4},{3,5},{4,2},{5,3},{6,7},{7,6},{8,9},{9,8},{10,12... | collective-permute-start | bytes 1572872 | tf_op jit(solution)/shard_map/ppermute | solution.py:504
  42.5 21.8 %collective-permute-start.7 = (bf16[1024,256]{1,0:T(8,128)(2,1)S(1)}, bf16[1024,256]{1,0:T(8,128)(2,1)S(1)}, u32[]{:S(2)}, u32[]{:S(2)}) collective-permute-start(bf16[1024,256]{1,0:T(8,128)(2,1)S(1)} %get-tuple-element.68.refs_7_), channel_id=1, source_target_pairs={{0,2},{1,3},{2,0},{3,1},{4,6},{5,7},{6,4},{7,5},{8,10},{9,11},{10,... | collective-permute-start | bytes 1572872 | tf_op jit(solution)/shard_map/ppermute | solution.py:504
  46.7 18.2 %collective-permute-start.17 = (bf16[256,1024]{1,0:T(8,128)(2,1)S(1)}, bf16[256,1024]{1,0:T(8,128)(2,1)S(1)}, u32[]{:S(2)}, u32[]{:S(2)}) collective-permute-start(bf16[256,1024]{1,0:T(8,128)(2,1)S(1)} %get-tuple-element.88), channel_id=1, source_target_pairs={{0,1},{1,0},{2,3},{3,2},{4,5},{5,4},{6,7},{7,6},{8,9},{9,8},{10,11... | collective-permute-start | bytes 1572872 | tf_op jit(solution)/shard_map/ppermute | solution.py:504
  53.7 15.3 %collective-permute-start.15 = (bf16[1024,256]{1,0:T(8,128)(2,1)S(1)}, bf16[1024,256]{1,0:T(8,128)(2,1)S(1)}, u32[]{:S(2)}, u32[]{:S(2)}) collective-permute-start(bf16[1024,256]{1,0:T(8,128)(2,1)S(1)} %get-tuple-element.84), channel_id=1, source_target_pairs={{0,1},{1,0},{2,4},{3,5},{4,2},{5,3},{6,7},{7,6},{8,9},{9,8},{10,12... | collective-permute-start | bytes 1572872 | tf_op jit(solution)/shard_map/ppermute | solution.py:504
  53.8 21.8 %collective-permute-start.16 = (bf16[1024,256]{1,0:T(8,128)(2,1)S(1)}, bf16[1024,256]{1,0:T(8,128)(2,1)S(1)}, u32[]{:S(2)}, u32[]{:S(2)}) collective-permute-start(bf16[1024,256]{1,0:T(8,128)(2,1)S(1)} %get-tuple-element.85), channel_id=1, source_target_pairs={{0,2},{1,3},{2,0},{3,1},{4,6},{5,7},{6,4},{7,5},{8,10},{9,11},{10,... | collective-permute-start | bytes 1572872 | tf_op jit(solution)/shard_map/ppermute | solution.py:504
  66.6 9.6 %collective-permute-start.18 = (bf16[256,1024]{1,0:T(8,128)(2,1)S(1)}, bf16[256,1024]{1,0:T(8,128)(2,1)S(1)}, u32[]{:S(2)}, u32[]{:S(2)}) collective-permute-start(bf16[256,1024]{1,0:T(8,128)(2,1)S(1)} %get-tuple-element.92), channel_id=1, source_target_pairs={{0,1},{1,0},{2,3},{3,2},{4,5},{5,4},{6,7},{7,6},{8,9},{9,8},{10,11... | collective-permute-start | bytes 1572872 | tf_op jit(solution)/shard_map/ppermute | solution.py:504
  66.7 20.2 %collective-permute-start.8 = (bf16[1024,256]{1,0:T(8,128)(2,1)S(1)}, bf16[1024,256]{1,0:T(8,128)(2,1)S(1)}, u32[]{:S(2)}, u32[]{:S(2)}) collective-permute-start(bf16[1024,256]{1,0:T(8,128)(2,1)S(1)} %get-tuple-element.69.refs_7_), channel_id=1, source_target_pairs={{0,2},{1,3},{2,0},{3,1},{4,6},{5,7},{6,4},{7,5},{8,10},{9,11},{10,... | collective-permute-start | bytes 1572872 | tf_op jit(solution)/shard_map/ppermute | solution.py:504
  68.9 18.0 %collective-permute-start.9 = (bf16[1024,256]{1,0:T(8,128)(2,1)S(1)}, bf16[1024,256]{1,0:T(8,128)(2,1)S(1)}, u32[]{:S(2)}, u32[]{:S(2)}) collective-permute-start(bf16[1024,256]{1,0:T(8,128)(2,1)S(1)} %get-tuple-element.70), channel_id=1, source_target_pairs={{0,1},{1,0},{2,4},{3,5},{4,2},{5,3},{6,7},{7,6},{8,9},{9,8},{10,12... | collective-permute-start | bytes 1572872 | tf_op jit(solution)/shard_map/ppermute | solution.py:504
  77.8 12.6 %collective-permute-start.19 = (bf16[256,1024]{1,0:T(8,128)(2,1)S(1)}, bf16[256,1024]{1,0:T(8,128)(2,1)S(1)}, u32[]{:S(2)}, u32[]{:S(2)}) collective-permute-start(bf16[256,1024]{1,0:T(8,128)(2,1)S(1)} %get-tuple-element.97), channel_id=1, source_target_pairs={{0,1},{1,0},{2,3},{3,2},{4,5},{5,4},{6,7},{7,6},{8,9},{9,8},{10,11... | collective-permute-start | bytes 1572872 | tf_op jit(solution)/shard_map/ppermute | solution.py:504
  77.9 19.8 %collective-permute-start.20 = (bf16[1024,256]{1,0:T(8,128)(2,1)S(1)}, bf16[1024,256]{1,0:T(8,128)(2,1)S(1)}, u32[]{:S(2)}, u32[]{:S(2)}) collective-permute-start(bf16[1024,256]{1,0:T(8,128)(2,1)S(1)} %get-tuple-element.100), channel_id=1, source_target_pairs={{0,2},{1,3},{2,0},{3,1},{4,6},{5,7},{6,4},{7,5},{8,10},{9,11},{10,... | collective-permute-start | bytes 1572872 | tf_op jit(solution)/shard_map/ppermute | solution.py:504
  80.1 17.6 %collective-permute-start.21 = (bf16[1024,256]{1,0:T(8,128)(2,1)S(1)}, bf16[1024,256]{1,0:T(8,128)(2,1)S(1)}, u32[]{:S(2)}, u32[]{:S(2)}) collective-permute-start(bf16[1024,256]{1,0:T(8,128)(2,1)S(1)} %get-tuple-element.101), channel_id=1, source_target_pairs={{0,1},{1,0},{2,4},{3,5},{4,2},{5,3},{6,7},{7,6},{8,9},{9,8},{10,12... | collective-permute-start | bytes 1572872 | tf_op jit(solution)/shard_map/ppermute | solution.py:504
  88.9 5.1 %collective-permute-start.23 = (bf16[512,128]{1,0:T(8,128)(2,1)S(1)}, bf16[512,128]{1,0:T(8,128)(2,1)S(1)}, u32[]{:S(2)}, u32[]{:S(2)}) collective-permute-start(bf16[512,128]{1,0:T(8,128)(2,1)S(1)} %get-tuple-element.107.refs_1_), channel_id=1, source_target_pairs={{0,16},{8,24},{16,0},{24,8},{1,17},{9,25},{17,1},{25,9},{2,18},{10... | collective-permute-start | bytes 393224 | tf_op jit(solution)/shard_map/ppermute | solution.py:504
  92.4 7.1 %collective-permute-start.24 = (bf16[512,128]{1,0:T(8,128)(2,1)S(1)}, bf16[512,128]{1,0:T(8,128)(2,1)S(1)}, u32[]{:S(2)}, u32[]{:S(2)}) collective-permute-start(bf16[512,128]{1,0:T(8,128)(2,1)S(1)} %shard_map.142.refs_3_.refs_10_.refs_2_), channel_id=1, source_target_pairs={{0,16},{8,24},{16,0},{24,8},{1,17},{9,25},{17,1},{25,9},{2,18},{10... | collective-permute-start | bytes 393224 | tf_op jit(solution)/shard_map/ppermute | solution.py:504
  94.1 5.5 %collective-permute-start.25 = (bf16[512,128]{1,0:T(8,128)(2,1)S(1)}, bf16[512,128]{1,0:T(8,128)(2,1)S(1)}, u32[]{:S(2)}, u32[]{:S(2)}) collective-permute-start(bf16[512,128]{1,0:T(8,128)(2,1)S(1)} %shard_map.143.refs_11_.refs_4_), channel_id=1, source_target_pairs={{0,8},{8,0},{16,24},{24,16},{1,9},{9,1},{17,25},{25,17},{2,10},{10... | collective-permute-start | bytes 393224 | tf_op jit(solution)/shard_map/ppermute | solution.py:504
  (3 other events, 20.7 us)

commit v7 on v5

--- a/solution.py
+++ b/solution.py
@@ -97,7 +97,7 @@
 
 def call(body, scalars, ins, outs, scratch=(), aliases=None, after=(), us=1.0):
     arrays, specs = [], []
-    for x in [Held(scalars), *ins]:
+    for x in [*([] if scalars is None else [Held(scalars)]), *ins]:
         if isinstance(x, Held):
             arrays.append(pltpu.with_memory_space_constraint(x.array, pltpu.VMEM))
             specs.append(pl.BlockSpec(memory_space=pltpu.VMEM))
@@ -109,7 +109,8 @@
     specs += [pl.BlockSpec(memory_space=pltpu.VMEM)] * len(after)
 
     def inner(*refs):
-        body(Numbers(refs[0]), *refs[1:first], *refs[first + len(after) :])
+        rest = refs[:first] + refs[first + len(after) :]
+        body(*rest) if scalars is None else body(Numbers(rest[0]), *rest[1:])
 
     return pl.pallas_call(
         inner,
@@ -153,16 +154,17 @@
     ]
 
 
-def cast_body(offset, s, w, low, wide, sems):
+def cast_body(offset, w, low, wide, sems):
     rows, part = low.shape
-    step = rows // 2
+    chunks = 4
+    step = rows // chunks
     copies = [
         start(
             w.at[pl.ds(i * step, step), pl.ds(offset, part)],
             wide.at[pl.ds(i * step, step)],
             sems.at[i],
         )
-        for i in range(2)
+        for i in range(chunks)
     ]
     for i, copy in enumerate(copies):
         copy.wait()
@@ -501,17 +503,17 @@
     dma = pltpu.SemaphoreType.DMA
     from_e, from_o = [[]], [[]]
     act_sib, cot_sib = permute(act, swap), permute(cot, swap)
-    (_, first), (offset, part) = PARTS
-    low = [weights[:, :first].astype(BF16)]
-    low += call(
-        functools.partial(cast_body, offset),
-        s,
-        [weights],
-        [vmem(rows, part, dtype=BF16)],
-        [vmem(rows, part), dma((2,))],
-        after=[cot_sib],
-        us=2.0,
-    )
+    low = []
+    for (offset, part), after in zip(PARTS, ([], [cot_sib])):
+        low += call(
+            functools.partial(cast_body, offset),
+            None,
+            [weights],
+            [vmem(rows, part, dtype=BF16)],
+            [vmem(rows, part), dma((4,))],
+            after=after,
+            us=1.2,
+        )
     for x in low:
         from_e[0].append(permute(x, e_perm))
         from_o[0].append(permute(x, o_perm))

time: 101 us -> 101 us (level)
  local copies, waits for them, and re-layouts: 1.45 us -> 0.13 us
  Pallas kernels: 26.5 us -> 27.7 us
    slice x1 -> x0, local copies, waits for them, and re-layouts: 1.32 us -> none  [line(): low = [weights[:, :first].astype(BF16)]]
    pallas_call x17 -> x18, Pallas kernels: 26.5 us -> 27.7 us  [call(): pl.pallas_call(inner, in_specs=specs, out_specs=[pl.BlockSpec(memory_spac...]
  transfers between devices with their start and end apart: 26 -> 26, of which waited for: 10 -> 10; matrix products, arithmetic and copies ran while one was open for 2% -> 0% of each run, Pallas kernels for 25% -> 26%
where the time goes in v7:
time: 101 us
  waiting for transfers between devices  42.6 us (42%)
  starting transfers between devices  28.9 us (29%)
  Pallas kernels  27.7 us (27%)
  between operations  1.74 us (2%)
    ppermute x26, waiting for transfers between devices, permute(): return lax.ppermute(x, axis, perm)  42.6 us
    ppermute x26, starting transfers between devices, permute(): return lax.ppermute(x, axis, perm)  28.9 us
    pallas_call x18, Pallas kernels, call(): pl.pallas_call(inner, in_specs=specs, out_specs=[pl.BlockSpec(memory_spac...  27.7 us
  transfers between devices with their start and end apart: 26, of which 10 were waited for; matrix products, arithmetic and copies ran while one was open for 0% of the time, Pallas kernels for 26%

profile of v7, /device:TPU:0, one launch (start us, length us, event | category | flops | bytes accessed | tf_op | source)
XLA Modules:
  0.0 101.2 jit_solution(11700471030277599490)
XLA Ops:
  2.5 4.1 %collective-permute-start.3 = (bf16[1024,256]{1,0:T(8,128)(2,1)S(1)}, bf16[1024,256]{1,0:T(8,128)(2,1)S(1)}, u32[]{:S(2)}, u32[]{:S(2)}) collective-permute-start(bf16[1024,256]{1,0:T(8,128)(2,1)S(1)} %shard_map.130.refs_3_), channel_id=1, source_target_pairs={{0,2},{1,3},{2,0},{3,1},{4,6},{5,7},{6,4},{7,5},{8,10},{9,11},{10,... | collective-permute-start | bytes 1572872 | tf_op jit(solution)/shard_map/ppermute | solution.py:501
  10.8 3.4 %collective-permute-start.11 = (bf16[1024,256]{1,0:T(8,128)(2,1)S(1)}, bf16[1024,256]{1,0:T(8,128)(2,1)S(1)}, u32[]{:S(2)}, u32[]{:S(2)}) collective-permute-start(bf16[1024,256]{1,0:T(8,128)(2,1)S(1)} %shard_map.127.refs_5_.refs_4_), channel_id=1, source_target_pairs={{0,2},{1,3},{2,0},{3,1},{4,6},{5,7},{6,4},{7,5},{8,10},{9,11},{10,... | collective-permute-start | bytes 1572872 | tf_op jit(solution)/shard_map/ppermute | solution.py:501
  14.2 5.3 %shard_map.128 = (f32[4096,512]{1,0:T(8,128)S(1)}, f32[1024,512]{1,0:T(8,128)}, f32[1024,512]{1,0:T(8,128)}) custom-call(s32[1,128]{1,0:T(1,128)S(1)} %pad_bitcast_fusion.refs_0_, bf16[256,8192]{1,0:T(8,128)(2,1)} %bitcast.58, bf16[256,512]{1,0:T(8,128)(2,1)S(1)} %bitcast.45, f32[1024,512]{1,0:T(8,128)} %refs_7_.1, f32[1024,512]{1,0:T(8,128)} %refs_8_.1, ...), custom_call_target="tpu_custom_call" | custom-call | bytes 17000000 | tf_op jit(solution)/shard_map/pallas_call | solution.py:115
  19.5 4.3 %shard_map.129 = (f32[4096,512]{1,0:T(8,128)S(1)}, f32[1024,512]{1,0:T(8,128)S(1)}, f32[1024,512]{1,0:T(8,128)S(1)}, f32[1024,512]{1,0:T(8,128)S(1)}, f32[1024,128]{1,0:T(8,128)S(1)}, /*index=5*/f32[1024,128]{1,0:T(8,128)S(1)}) custom-call(s32[1,128]{1,0:T(1,128)S(1)} %pad_bitcast_fusion.refs_0_, ...), custom_call_target="tpu_custom_call", output_to_operand_aliasing={{0}: (1, {})} | custom-call | bytes 17000000 | tf_op jit(solution)/shard_map/pallas_call | solution.py:115
  24.4 2.4 %collective-permute-start.5 = (bf16[1024,256]{1,0:T(8,128)(2,1)S(1)}, bf16[1024,256]{1,0:T(8,128)(2,1)S(1)}, u32[]{:S(2)}, u32[]{:S(2)}) collective-permute-start(bf16[1024,256]{1,0:T(8,128)(2,1)S(1)} %get-tuple-element.66.refs_5_), channel_id=1, source_target_pairs={{0,2},{1,3},{2,0},{3,1},{4,6},{5,7},{6,4},{7,5},{8,10},{9,11},{10,... | collective-permute-start | bytes 1572872 | tf_op jit(solution)/shard_map/ppermute | solution.py:501
  28.5 2.1 %collective-permute-done.11.refs_3_ = bf16[1024,256]{1,0:T(8,128)(2,1)S(1)} collective-permute-done((bf16[1024,256]{1,0:T(8,128)(2,1)S(1)}, bf16[1024,256]{1,0:T(8,128)(2,1)S(1)}, u32[]{:S(2)}, u32[]{:S(2)}) %collective-permute-start.11) | collective-permute-done | bytes 524320 | tf_op jit(solution)/shard_map/ppermute | solution.py:501
  31.1 2.5 %collective-permute-start.13 = (bf16[1024,256]{1,0:T(8,128)(2,1)S(1)}, bf16[1024,256]{1,0:T(8,128)(2,1)S(1)}, u32[]{:S(2)}, u32[]{:S(2)}) collective-permute-start(bf16[1024,256]{1,0:T(8,128)(2,1)S(1)} %get-tuple-element.78), channel_id=1, source_target_pairs={{0,2},{1,3},{2,0},{3,1},{4,6},{5,7},{6,4},{7,5},{8,10},{9,11},{10,... | collective-permute-start | bytes 1572872 | tf_op jit(solution)/shard_map/ppermute | solution.py:501
  33.6 8.2 %collective-permute-done.5.refs_3_ = bf16[1024,256]{1,0:T(8,128)(2,1)S(1)} collective-permute-done((bf16[1024,256]{1,0:T(8,128)(2,1)S(1)}, bf16[1024,256]{1,0:T(8,128)(2,1)S(1)}, u32[]{:S(2)}, u32[]{:S(2)}) %collective-permute-start.5) | collective-permute-done | bytes 524320 | tf_op jit(solution)/shard_map/ppermute | solution.py:501
  42.5 2.5 %collective-permute-start.7 = (bf16[1024,256]{1,0:T(8,128)(2,1)S(1)}, bf16[1024,256]{1,0:T(8,128)(2,1)S(1)}, u32[]{:S(2)}, u32[]{:S(2)}) collective-permute-start(bf16[1024,256]{1,0:T(8,128)(2,1)S(1)} %get-tuple-element.68.refs_7_), channel_id=1, source_target_pairs={{0,2},{1,3},{2,0},{3,1},{4,6},{5,7},{6,4},{7,5},{8,10},{9,11},{10,... | collective-permute-start | bytes 1572872 | tf_op jit(solution)/shard_map/ppermute | solution.py:501
  45.0 1.6 %shard_map.136 = (bf16[256,1024]{1,0:T(8,128)(2,1)S(1)}, bf16[256,8192]{1,0:T(8,128)(2,1)}, f32[8,128]{1,0:T(8,128)S(1)}) custom-call(s32[1,128]{1,0:T(1,128)S(1)} %pad_bitcast_fusion.refs_0_, bf16[256,512]{1,0:T(8,128)(2,1)S(1)} %bitcast.47, bf16[256,512]{1,0:T(8,128)(2,1)S(1)} %collective-permute-done.refs_1_.refs_3_.refs_2_, ...), custom_call_target="tpu_custom_call", output_to_operand_aliasing={{1}: (6, {})} | custom-call | bytes 7140000 | tf_op jit(solution)/shard_map/pallas_call | solution.py:115
  46.7 6.3 %collective-permute-done.13.refs_3_ = bf16[1024,256]{1,0:T(8,128)(2,1)S(1)} collective-permute-done((bf16[1024,256]{1,0:T(8,128)(2,1)S(1)}, bf16[1024,256]{1,0:T(8,128)(2,1)S(1)}, u32[]{:S(2)}, u32[]{:S(2)}) %collective-permute-start.13) | collective-permute-done | bytes 524320 | tf_op jit(solution)/shard_map/ppermute | solution.py:501
  53.7 2.5 %collective-permute-start.16 = (bf16[1024,256]{1,0:T(8,128)(2,1)S(1)}, bf16[1024,256]{1,0:T(8,128)(2,1)S(1)}, u32[]{:S(2)}, u32[]{:S(2)}) collective-permute-start(bf16[1024,256]{1,0:T(8,128)(2,1)S(1)} %get-tuple-element.85), channel_id=1, source_target_pairs={{0,2},{1,3},{2,0},{3,1},{4,6},{5,7},{6,4},{7,5},{8,10},{9,11},{10,... | collective-permute-start | bytes 1572872 | tf_op jit(solution)/shard_map/ppermute | solution.py:501
  56.2 8.1 %collective-permute-done.7.refs_3_ = bf16[1024,256]{1,0:T(8,128)(2,1)S(1)} collective-permute-done((bf16[1024,256]{1,0:T(8,128)(2,1)S(1)}, bf16[1024,256]{1,0:T(8,128)(2,1)S(1)}, u32[]{:S(2)}, u32[]{:S(2)}) %collective-permute-start.7) | collective-permute-done | bytes 524320 | tf_op jit(solution)/shard_map/ppermute | solution.py:501
  64.9 1.6 %shard_map.138 = (bf16[256,1024]{1,0:T(8,128)(2,1)S(1)}, bf16[256,8192]{1,0:T(8,128)(2,1)}, f32[8,128]{1,0:T(8,128)S(1)}) custom-call(s32[1,128]{1,0:T(1,128)S(1)} %pad_bitcast_fusion.refs_0_, bf16[256,512]{1,0:T(8,128)(2,1)S(1)} %bitcast.48, bf16[256,512]{1,0:T(8,128)(2,1)S(1)} %collective-permute-done.refs_1_.refs_3_.refs_2_, ...), custom_call_target="tpu_custom_call", output_to_operand_aliasing={{1}: (6, {})} | custom-call | bytes 7140000 | tf_op jit(solution)/shard_map/pallas_call | solution.py:115
  66.6 2.2 %collective-permute-start.8 = (bf16[1024,256]{1,0:T(8,128)(2,1)S(1)}, bf16[1024,256]{1,0:T(8,128)(2,1)S(1)}, u32[]{:S(2)}, u32[]{:S(2)}) collective-permute-start(bf16[1024,256]{1,0:T(8,128)(2,1)S(1)} %get-tuple-element.69.refs_7_), channel_id=1, source_target_pairs={{0,2},{1,3},{2,0},{3,1},{4,6},{5,7},{6,4},{7,5},{8,10},{9,11},{10,... | collective-permute-start | bytes 1572872 | tf_op jit(solution)/shard_map/ppermute | solution.py:501
  69.0 6.6 %collective-permute-done.16.refs_3_ = bf16[1024,256]{1,0:T(8,128)(2,1)S(1)} collective-permute-done((bf16[1024,256]{1,0:T(8,128)(2,1)S(1)}, bf16[1024,256]{1,0:T(8,128)(2,1)S(1)}, u32[]{:S(2)}, u32[]{:S(2)}) %collective-permute-start.16) | collective-permute-done | bytes 524320 | tf_op jit(solution)/shard_map/ppermute | solution.py:501
  76.1 1.6 %shard_map.140 = (bf16[256,1024]{1,0:T(8,128)(2,1)S(1)}, bf16[256,8192]{1,0:T(8,128)(2,1)}, f32[8,128]{1,0:T(8,128)S(1)}) custom-call(s32[1,128]{1,0:T(1,128)S(1)} %pad_bitcast_fusion.refs_0_, bf16[256,512]{1,0:T(8,128)(2,1)S(1)} %bitcast.49, bf16[256,512]{1,0:T(8,128)(2,1)S(1)} %collective-permute-done.refs_1_.refs_3_.refs_2_, ...), custom_call_target="tpu_custom_call", output_to_operand_aliasing={{1}: (6, {})} | custom-call | bytes 7140000 | tf_op jit(solution)/shard_map/pallas_call | solution.py:115
  77.8 2.2 %collective-permute-start.20 = (bf16[1024,256]{1,0:T(8,128)(2,1)S(1)}, bf16[1024,256]{1,0:T(8,128)(2,1)S(1)}, u32[]{:S(2)}, u32[]{:S(2)}) collective-permute-start(bf16[1024,256]{1,0:T(8,128)(2,1)S(1)} %get-tuple-element.100), channel_id=1, source_target_pairs={{0,2},{1,3},{2,0},{3,1},{4,6},{5,7},{6,4},{7,5},{8,10},{9,11},{10,... | collective-permute-start | bytes 1572872 | tf_op jit(solution)/shard_map/ppermute | solution.py:501
  80.2 6.6 %collective-permute-done.8.refs_2_ = bf16[1024,256]{1,0:T(8,128)(2,1)S(1)} collective-permute-done((bf16[1024,256]{1,0:T(8,128)(2,1)S(1)}, bf16[1024,256]{1,0:T(8,128)(2,1)S(1)}, u32[]{:S(2)}, u32[]{:S(2)}) %collective-permute-start.8) | collective-permute-done | bytes 524320 | tf_op jit(solution)/shard_map/ppermute | solution.py:501
  87.3 1.6 %collective-permute-start.23 = (bf16[512,128]{1,0:T(8,128)(2,1)S(1)}, bf16[512,128]{1,0:T(8,128)(2,1)S(1)}, u32[]{:S(2)}, u32[]{:S(2)}) collective-permute-start(bf16[512,128]{1,0:T(8,128)(2,1)S(1)} %get-tuple-element.107), channel_id=1, source_target_pairs={{0,16},{8,24},{16,0},{24,8},{1,17},{9,25},{17,1},{25,9},{2,18},{10... | collective-permute-start | bytes 393224 | tf_op jit(solution)/shard_map/ppermute | solution.py:501
  90.4 1.9 %shard_map.142 = (f32[1024,512]{1,0:T(8,128)}, f32[1024,512]{1,0:T(8,128)}, f32[1024,512]{1,0:T(8,128)}, bf16[256,8192]{1,0:T(8,128)(2,1)}, f32[8,128]{1,0:T(8,128)S(1)}) custom-call(s32[1,128]{1,0:T(1,128)S(1)} %pad_bitcast_fusion.refs_0_, f32[4096,512]{1,0:T(8,128)S(1)} %get-tuple-element.64.refs_1_, ...), custom_call_target="tpu_custom_call", output_to_operand_aliasing={{3}: (10, {})} | custom-call | bytes 6800000 | tf_op jit(solution)/shard_map/pallas_call | solution.py:115
  96.0 1.6 %collective-permute-done.20.refs_2_ = bf16[1024,256]{1,0:T(8,128)(2,1)S(1)} collective-permute-done((bf16[1024,256]{1,0:T(8,128)(2,1)S(1)}, bf16[1024,256]{1,0:T(8,128)(2,1)S(1)}, u32[]{:S(2)}, u32[]{:S(2)}) %collective-permute-start.20) | collective-permute-done | bytes 524320 | tf_op jit(solution)/shard_map/ppermute | solution.py:501
  97.6 1.9 %shard_map.143 = (f32[1024,512]{1,0:T(8,128)}, f32[1024,512]{1,0:T(8,128)}, f32[1024,512]{1,0:T(8,128)}, f32[3,256,256]{2,1,0:T(8,128)S(1)}) custom-call(s32[1,128]{1,0:T(1,128)S(1)} %pad_bitcast_fusion.refs_0_, f32[4096,512]{1,0:T(8,128)S(1)} %get-tuple-element.64.refs_1_, ...), custom_call_target="tpu_custom_call", output_to_operand_aliasing={{0}: (7, {}), {1}: (8, {}), {2}: (9, {})} | custom-call | bytes 8160000 | tf_op jit(solution)/shard_map/pallas_call | solution.py:115
  99.5 1.6 %shard_map.144 = (f32[1024,512]{1,0:T(8,128)}, f32[1024,512]{1,0:T(8,128)}, f32[1024,512]{1,0:T(8,128)}, f32[1024,512]{1,0:T(8,128)}, f32[1024,512]{1,0:T(8,128)}) custom-call(s32[1,128]{1,0:T(1,128)S(1)} %pad_bitcast_fusion.refs_0_, ...), custom_call_target="tpu_custom_call", output_to_operand_aliasing={{0}: (8, {}), {1}: (9, {}), {2}: (10, {}), {3}: (11, {}), {... | custom-call | bytes 6800000 | tf_op jit(solution)/shard_map/pallas_call | solution.py:115
  (52 shorter events, 16.6 us)
Async XLA Ops:
  0.6 18.9 %collective-permute-start.1 = (bf16[256,8192]{1,0:T(8,128)(2,1)}, bf16[256,8192]{1,0:T(8,128)(2,1)}, u32[]{:S(2)}, u32[]{:S(2)}) collective-permute-start(bf16[256,8192]{1,0:T(8,128)(2,1)} %bitcast.57), channel_id=1, source_target_pairs={{0,1},{1,0},{2,3},{3,2},{4,5},{5,4},{6,7},{7,6},{8,9},{9,8},{10,11... | collective-permute-start | bytes 12582920 | tf_op jit(solution)/shard_map/ppermute | solution.py:501
  2.4 21.5 %collective-permute-start.2 = (bf16[1024,256]{1,0:T(8,128)(2,1)S(1)}, bf16[1024,256]{1,0:T(8,128)(2,1)S(1)}, u32[]{:S(2)}, u32[]{:S(2)}) collective-permute-start(bf16[1024,256]{1,0:T(8,128)(2,1)S(1)} %shard_map.130.refs_3_), channel_id=1, source_target_pairs={{0,1},{1,0},{2,4},{3,5},{4,2},{5,3},{6,7},{7,6},{8,9},{9,8},{10,12... | collective-permute-start | bytes 1572872 | tf_op jit(solution)/shard_map/ppermute | solution.py:501
  2.5 21.3 %collective-permute-start.3 = (bf16[1024,256]{1,0:T(8,128)(2,1)S(1)}, bf16[1024,256]{1,0:T(8,128)(2,1)S(1)}, u32[]{:S(2)}, u32[]{:S(2)}) collective-permute-start(bf16[1024,256]{1,0:T(8,128)(2,1)S(1)} %shard_map.130.refs_3_), channel_id=1, source_target_pairs={{0,2},{1,3},{2,0},{3,1},{4,6},{5,7},{6,4},{7,5},{8,10},{9,11},{10,... | collective-permute-start | bytes 1572872 | tf_op jit(solution)/shard_map/ppermute | solution.py:501
  10.3 18.2 %collective-permute-start.10 = (bf16[1024,256]{1,0:T(8,128)(2,1)S(1)}, bf16[1024,256]{1,0:T(8,128)(2,1)S(1)}, u32[]{:S(2)}, u32[]{:S(2)}) collective-permute-start(bf16[1024,256]{1,0:T(8,128)(2,1)S(1)} %shard_map.127.refs_5_.refs_4_), channel_id=1, source_target_pairs={{0,1},{1,0},{2,4},{3,5},{4,2},{5,3},{6,7},{7,6},{8,9},{9,8},{10,12... | collective-permute-start | bytes 1572872 | tf_op jit(solution)/shard_map/ppermute | solution.py:501
  10.8 19.8 %collective-permute-start.11 = (bf16[1024,256]{1,0:T(8,128)(2,1)S(1)}, bf16[1024,256]{1,0:T(8,128)(2,1)S(1)}, u32[]{:S(2)}, u32[]{:S(2)}) collective-permute-start(bf16[1024,256]{1,0:T(8,128)(2,1)S(1)} %shard_map.127.refs_5_.refs_4_), channel_id=1, source_target_pairs={{0,2},{1,3},{2,0},{3,1},{4,6},{5,7},{6,4},{7,5},{8,10},{9,11},{10,... | collective-permute-start | bytes 1572872 | tf_op jit(solution)/shard_map/ppermute | solution.py:501
  24.3 9.2 %collective-permute-start.4 = (bf16[1024,256]{1,0:T(8,128)(2,1)S(1)}, bf16[1024,256]{1,0:T(8,128)(2,1)S(1)}, u32[]{:S(2)}, u32[]{:S(2)}) collective-permute-start(bf16[1024,256]{1,0:T(8,128)(2,1)S(1)} %get-tuple-element.65), channel_id=1, source_target_pairs={{0,1},{1,0},{2,4},{3,5},{4,2},{5,3},{6,7},{7,6},{8,9},{9,8},{10,12... | collective-permute-start | bytes 1572872 | tf_op jit(solution)/shard_map/ppermute | solution.py:501
  24.4 17.4 %collective-permute-start.5 = (bf16[1024,256]{1,0:T(8,128)(2,1)S(1)}, bf16[1024,256]{1,0:T(8,128)(2,1)S(1)}, u32[]{:S(2)}, u32[]{:S(2)}) collective-permute-start(bf16[1024,256]{1,0:T(8,128)(2,1)S(1)} %get-tuple-element.66.refs_5_), channel_id=1, source_target_pairs={{0,2},{1,3},{2,0},{3,1},{4,6},{5,7},{6,4},{7,5},{8,10},{9,11},{10,... | collective-permute-start | bytes 1572872 | tf_op jit(solution)/shard_map/ppermute | solution.py:501
  28.4 16.6 %collective-permute-start.14 = (bf16[256,1024]{1,0:T(8,128)(2,1)S(1)}, bf16[256,1024]{1,0:T(8,128)(2,1)S(1)}, u32[]{:S(2)}, u32[]{:S(2)}) collective-permute-start(bf16[256,1024]{1,0:T(8,128)(2,1)S(1)} %get-tuple-element.81), channel_id=1, source_target_pairs={{0,1},{1,0},{2,3},{3,2},{4,5},{5,4},{6,7},{7,6},{8,9},{9,8},{10,11... | collective-permute-start | bytes 1572872 | tf_op jit(solution)/shard_map/ppermute | solution.py:501
  31.0 15.7 %collective-permute-start.12 = (bf16[1024,256]{1,0:T(8,128)(2,1)S(1)}, bf16[1024,256]{1,0:T(8,128)(2,1)S(1)}, u32[]{:S(2)}, u32[]{:S(2)}) collective-permute-start(bf16[1024,256]{1,0:T(8,128)(2,1)S(1)} %get-tuple-element.77), channel_id=1, source_target_pairs={{0,1},{1,0},{2,4},{3,5},{4,2},{5,3},{6,7},{7,6},{8,9},{9,8},{10,12... | collective-permute-start | bytes 1572872 | tf_op jit(solution)/shard_map/ppermute | solution.py:501
  31.1 21.9 %collective-permute-start.13 = (bf16[1024,256]{1,0:T(8,128)(2,1)S(1)}, bf16[1024,256]{1,0:T(8,128)(2,1)S(1)}, u32[]{:S(2)}, u32[]{:S(2)}) collective-permute-start(bf16[1024,256]{1,0:T(8,128)(2,1)S(1)} %get-tuple-element.78), channel_id=1, source_target_pairs={{0,2},{1,3},{2,0},{3,1},{4,6},{5,7},{6,4},{7,5},{8,10},{9,11},{10,... | collective-permute-start | bytes 1572872 | tf_op jit(solution)/shard_map/ppermute | solution.py:501
  42.4 13.8 %collective-permute-start.6 = (bf16[1024,256]{1,0:T(8,128)(2,1)S(1)}, bf16[1024,256]{1,0:T(8,128)(2,1)S(1)}, u32[]{:S(2)}, u32[]{:S(2)}) collective-permute-start(bf16[1024,256]{1,0:T(8,128)(2,1)S(1)} %get-tuple-element.67), channel_id=1, source_target_pairs={{0,1},{1,0},{2,4},{3,5},{4,2},{5,3},{6,7},{7,6},{8,9},{9,8},{10,12... | collective-permute-start | bytes 1572872 | tf_op jit(solution)/shard_map/ppermute | solution.py:501
  42.5 21.8 %collective-permute-start.7 = (bf16[1024,256]{1,0:T(8,128)(2,1)S(1)}, bf16[1024,256]{1,0:T(8,128)(2,1)S(1)}, u32[]{:S(2)}, u32[]{:S(2)}) collective-permute-start(bf16[1024,256]{1,0:T(8,128)(2,1)S(1)} %get-tuple-element.68.refs_7_), channel_id=1, source_target_pairs={{0,2},{1,3},{2,0},{3,1},{4,6},{5,7},{6,4},{7,5},{8,10},{9,11},{10,... | collective-permute-start | bytes 1572872 | tf_op jit(solution)/shard_map/ppermute | solution.py:501
  46.6 18.2 %collective-permute-start.17 = (bf16[256,1024]{1,0:T(8,128)(2,1)S(1)}, bf16[256,1024]{1,0:T(8,128)(2,1)S(1)}, u32[]{:S(2)}, u32[]{:S(2)}) collective-permute-start(bf16[256,1024]{1,0:T(8,128)(2,1)S(1)} %get-tuple-element.88), channel_id=1, source_target_pairs={{0,1},{1,0},{2,3},{3,2},{4,5},{5,4},{6,7},{7,6},{8,9},{9,8},{10,11... | collective-permute-start | bytes 1572872 | tf_op jit(solution)/shard_map/ppermute | solution.py:501
  53.6 15.3 %collective-permute-start.15 = (bf16[1024,256]{1,0:T(8,128)(2,1)S(1)}, bf16[1024,256]{1,0:T(8,128)(2,1)S(1)}, u32[]{:S(2)}, u32[]{:S(2)}) collective-permute-start(bf16[1024,256]{1,0:T(8,128)(2,1)S(1)} %get-tuple-element.84), channel_id=1, source_target_pairs={{0,1},{1,0},{2,4},{3,5},{4,2},{5,3},{6,7},{7,6},{8,9},{9,8},{10,12... | collective-permute-start | bytes 1572872 | tf_op jit(solution)/shard_map/ppermute | solution.py:501
  53.7 21.8 %collective-permute-start.16 = (bf16[1024,256]{1,0:T(8,128)(2,1)S(1)}, bf16[1024,256]{1,0:T(8,128)(2,1)S(1)}, u32[]{:S(2)}, u32[]{:S(2)}) collective-permute-start(bf16[1024,256]{1,0:T(8,128)(2,1)S(1)} %get-tuple-element.85), channel_id=1, source_target_pairs={{0,2},{1,3},{2,0},{3,1},{4,6},{5,7},{6,4},{7,5},{8,10},{9,11},{10,... | collective-permute-start | bytes 1572872 | tf_op jit(solution)/shard_map/ppermute | solution.py:501
  66.5 9.6 %collective-permute-start.18 = (bf16[256,1024]{1,0:T(8,128)(2,1)S(1)}, bf16[256,1024]{1,0:T(8,128)(2,1)S(1)}, u32[]{:S(2)}, u32[]{:S(2)}) collective-permute-start(bf16[256,1024]{1,0:T(8,128)(2,1)S(1)} %get-tuple-element.92), channel_id=1, source_target_pairs={{0,1},{1,0},{2,3},{3,2},{4,5},{5,4},{6,7},{7,6},{8,9},{9,8},{10,11... | collective-permute-start | bytes 1572872 | tf_op jit(solution)/shard_map/ppermute | solution.py:501
  66.6 20.2 %collective-permute-start.8 = (bf16[1024,256]{1,0:T(8,128)(2,1)S(1)}, bf16[1024,256]{1,0:T(8,128)(2,1)S(1)}, u32[]{:S(2)}, u32[]{:S(2)}) collective-permute-start(bf16[1024,256]{1,0:T(8,128)(2,1)S(1)} %get-tuple-element.69.refs_7_), channel_id=1, source_target_pairs={{0,2},{1,3},{2,0},{3,1},{4,6},{5,7},{6,4},{7,5},{8,10},{9,11},{10,... | collective-permute-start | bytes 1572872 | tf_op jit(solution)/shard_map/ppermute | solution.py:501
  68.8 18.0 %collective-permute-start.9 = (bf16[1024,256]{1,0:T(8,128)(2,1)S(1)}, bf16[1024,256]{1,0:T(8,128)(2,1)S(1)}, u32[]{:S(2)}, u32[]{:S(2)}) collective-permute-start(bf16[1024,256]{1,0:T(8,128)(2,1)S(1)} %get-tuple-element.70), channel_id=1, source_target_pairs={{0,1},{1,0},{2,4},{3,5},{4,2},{5,3},{6,7},{7,6},{8,9},{9,8},{10,12... | collective-permute-start | bytes 1572872 | tf_op jit(solution)/shard_map/ppermute | solution.py:501
  77.7 12.6 %collective-permute-start.19 = (bf16[256,1024]{1,0:T(8,128)(2,1)S(1)}, bf16[256,1024]{1,0:T(8,128)(2,1)S(1)}, u32[]{:S(2)}, u32[]{:S(2)}) collective-permute-start(bf16[256,1024]{1,0:T(8,128)(2,1)S(1)} %get-tuple-element.97), channel_id=1, source_target_pairs={{0,1},{1,0},{2,3},{3,2},{4,5},{5,4},{6,7},{7,6},{8,9},{9,8},{10,11... | collective-permute-start | bytes 1572872 | tf_op jit(solution)/shard_map/ppermute | solution.py:501
  77.8 19.8 %collective-permute-start.20 = (bf16[1024,256]{1,0:T(8,128)(2,1)S(1)}, bf16[1024,256]{1,0:T(8,128)(2,1)S(1)}, u32[]{:S(2)}, u32[]{:S(2)}) collective-permute-start(bf16[1024,256]{1,0:T(8,128)(2,1)S(1)} %get-tuple-element.100), channel_id=1, source_target_pairs={{0,2},{1,3},{2,0},{3,1},{4,6},{5,7},{6,4},{7,5},{8,10},{9,11},{10,... | collective-permute-start | bytes 1572872 | tf_op jit(solution)/shard_map/ppermute | solution.py:501
  80.0 17.6 %collective-permute-start.21 = (bf16[1024,256]{1,0:T(8,128)(2,1)S(1)}, bf16[1024,256]{1,0:T(8,128)(2,1)S(1)}, u32[]{:S(2)}, u32[]{:S(2)}) collective-permute-start(bf16[1024,256]{1,0:T(8,128)(2,1)S(1)} %get-tuple-element.101), channel_id=1, source_target_pairs={{0,1},{1,0},{2,4},{3,5},{4,2},{5,3},{6,7},{7,6},{8,9},{9,8},{10,12... | collective-permute-start | bytes 1572872 | tf_op jit(solution)/shard_map/ppermute | solution.py:501
  87.3 5.0 %collective-permute-start.23 = (bf16[512,128]{1,0:T(8,128)(2,1)S(1)}, bf16[512,128]{1,0:T(8,128)(2,1)S(1)}, u32[]{:S(2)}, u32[]{:S(2)}) collective-permute-start(bf16[512,128]{1,0:T(8,128)(2,1)S(1)} %get-tuple-element.107), channel_id=1, source_target_pairs={{0,16},{8,24},{16,0},{24,8},{1,17},{9,25},{17,1},{25,9},{2,18},{10... | collective-permute-start | bytes 393224 | tf_op jit(solution)/shard_map/ppermute | solution.py:501
  93.9 5.6 %collective-permute-start.24 = (bf16[512,128]{1,0:T(8,128)(2,1)S(1)}, bf16[512,128]{1,0:T(8,128)(2,1)S(1)}, u32[]{:S(2)}, u32[]{:S(2)}) collective-permute-start(bf16[512,128]{1,0:T(8,128)(2,1)S(1)} %get-tuple-element.121.refs_10_.refs_2_), channel_id=1, source_target_pairs={{0,16},{8,24},{16,0},{24,8},{1,17},{9,25},{17,1},{25,9},{2,18},{10... | collective-permute-start | bytes 393224 | tf_op jit(solution)/shard_map/ppermute | solution.py:501
  94.5 5.0 %collective-permute-start.25 = (bf16[512,128]{1,0:T(8,128)(2,1)S(1)}, bf16[512,128]{1,0:T(8,128)(2,1)S(1)}, u32[]{:S(2)}, u32[]{:S(2)}) collective-permute-start(bf16[512,128]{1,0:T(8,128)(2,1)S(1)} %get-tuple-element.120.refs_11_.refs_4_), channel_id=1, source_target_pairs={{0,8},{8,0},{16,24},{24,16},{1,9},{9,1},{17,25},{25,17},{2,10},{10... | collective-permute-start | bytes 393224 | tf_op jit(solution)/shard_map/ppermute | solution.py:501
  (3 other events, 13.4 us)

commit v8 on v7

--- a/solution.py
+++ b/solution.py
@@ -425,17 +425,15 @@
         last = columns_of(out.at[there], s[at["pieces"] + 2], part)
         copies.append(start(left.at[k], last, sems.at[k]))
     half = rows // 2
-    size = half // 2
     for n, (own, other) in enumerate(((upper, upper_in), (lower, lower_in))):
-        for r in (0, size):
-            here, there = pl.ds(r, size), pl.ds(n * half + r, size)
-            average = (own[here, :].astype(F32) + other[here, :].astype(F32)) * 0.25
-            momentum = 0.9 * moment[there, :] + average
-            stage[0, there, :] = momentum
-            stage[1, there, :] = anchor[there, :] - 0.7 * (average + 0.9 * momentum)
-            for k, out in ((0, new_moment), (1, new_anchor), (1, inner)):
-                target = columns_of(out.at[there], s[at["pieces"]], HEAD)
-                copies.append(start(stage.at[k, there], target, sems.at[len(copies)]))
+        there = pl.ds(n * half, half)
+        average = (own[...].astype(F32) + other[...].astype(F32)) * 0.25
+        momentum = 0.9 * moment[there, :] + average
+        stage[0, there, :] = momentum
+        stage[1, there, :] = anchor[there, :] - 0.7 * (average + 0.9 * momentum)
+        for k, out in ((0, new_moment), (1, new_anchor), (1, inner)):
+            target = columns_of(out.at[there], s[at["pieces"]], HEAD)
+            copies.append(start(stage.at[k, there], target, sems.at[len(copies)]))
     for copy in copies:
         copy.wait()
 
@@ -640,7 +638,7 @@
         s,
         [Held(x) for x in held] + [*state, new_anchor, new_momentum],
         [hbm(rows, columns)] * 5,
-        [vmem(2, rows, HEAD), dma((15,))],
+        [vmem(2, rows, HEAD), dma((9,))],
         {len(held) + k: k for k in range(5)},
         us=2.0,
     )

time: 101 us -> 101 us (level)
  no operation moved by 1% of the time
where the time goes in v8:
time: 101 us
  waiting for transfers between devices  42.6 us (42%)
  starting transfers between devices  28.9 us (29%)
  Pallas kernels  27.7 us (27%)
  between operations  1.74 us (2%)
    ppermute x26, waiting for transfers between devices, permute(): return lax.ppermute(x, axis, perm)  42.6 us
    ppermute x26, starting transfers between devices, permute(): return lax.ppermute(x, axis, perm)  28.9 us
    pallas_call x18, Pallas kernels, call(): pl.pallas_call(inner, in_specs=specs, out_specs=[pl.BlockSpec(memory_spac...  27.7 us
  transfers between devices with their start and end apart: 26, of which 10 were waited for; matrix products, arithmetic and copies ran while one was open for 0% of the time, Pallas kernels for 26%

profile of v8, /device:TPU:0, one launch (start us, length us, event | category | flops | bytes accessed | tf_op | source)
XLA Modules:
  0.0 101.2 jit_solution(2478383226918600884)
XLA Ops:
  2.5 4.1 %collective-permute-start.3 = (bf16[1024,256]{1,0:T(8,128)(2,1)S(1)}, bf16[1024,256]{1,0:T(8,128)(2,1)S(1)}, u32[]{:S(2)}, u32[]{:S(2)}) collective-permute-start(bf16[1024,256]{1,0:T(8,128)(2,1)S(1)} %shard_map.130.refs_3_), channel_id=1, source_target_pairs={{0,2},{1,3},{2,0},{3,1},{4,6},{5,7},{6,4},{7,5},{8,10},{9,11},{10,... | collective-permute-start | bytes 1572872 | tf_op jit(solution)/shard_map/ppermute | solution.py:499
  10.8 3.4 %collective-permute-start.11 = (bf16[1024,256]{1,0:T(8,128)(2,1)S(1)}, bf16[1024,256]{1,0:T(8,128)(2,1)S(1)}, u32[]{:S(2)}, u32[]{:S(2)}) collective-permute-start(bf16[1024,256]{1,0:T(8,128)(2,1)S(1)} %shard_map.127.refs_5_.refs_4_), channel_id=1, source_target_pairs={{0,2},{1,3},{2,0},{3,1},{4,6},{5,7},{6,4},{7,5},{8,10},{9,11},{10,... | collective-permute-start | bytes 1572872 | tf_op jit(solution)/shard_map/ppermute | solution.py:499
  14.2 5.3 %shard_map.128 = (f32[4096,512]{1,0:T(8,128)S(1)}, f32[1024,512]{1,0:T(8,128)}, f32[1024,512]{1,0:T(8,128)}) custom-call(s32[1,128]{1,0:T(1,128)S(1)} %pad_bitcast_fusion.refs_0_, bf16[256,8192]{1,0:T(8,128)(2,1)} %bitcast.58, bf16[256,512]{1,0:T(8,128)(2,1)S(1)} %bitcast.45, f32[1024,512]{1,0:T(8,128)} %refs_7_.1, f32[1024,512]{1,0:T(8,128)} %refs_8_.1, ...), custom_call_target="tpu_custom_call" | custom-call | bytes 17000000 | tf_op jit(solution)/shard_map/pallas_call | solution.py:115
  19.5 4.3 %shard_map.129 = (f32[4096,512]{1,0:T(8,128)S(1)}, f32[1024,512]{1,0:T(8,128)S(1)}, f32[1024,512]{1,0:T(8,128)S(1)}, f32[1024,512]{1,0:T(8,128)S(1)}, f32[1024,128]{1,0:T(8,128)S(1)}, /*index=5*/f32[1024,128]{1,0:T(8,128)S(1)}) custom-call(s32[1,128]{1,0:T(1,128)S(1)} %pad_bitcast_fusion.refs_0_, ...), custom_call_target="tpu_custom_call", output_to_operand_aliasing={{0}: (1, {})} | custom-call | bytes 17000000 | tf_op jit(solution)/shard_map/pallas_call | solution.py:115
  24.4 2.4 %collective-permute-start.5 = (bf16[1024,256]{1,0:T(8,128)(2,1)S(1)}, bf16[1024,256]{1,0:T(8,128)(2,1)S(1)}, u32[]{:S(2)}, u32[]{:S(2)}) collective-permute-start(bf16[1024,256]{1,0:T(8,128)(2,1)S(1)} %get-tuple-element.66.refs_5_), channel_id=1, source_target_pairs={{0,2},{1,3},{2,0},{3,1},{4,6},{5,7},{6,4},{7,5},{8,10},{9,11},{10,... | collective-permute-start | bytes 1572872 | tf_op jit(solution)/shard_map/ppermute | solution.py:499
  28.5 2.1 %collective-permute-done.11.refs_3_ = bf16[1024,256]{1,0:T(8,128)(2,1)S(1)} collective-permute-done((bf16[1024,256]{1,0:T(8,128)(2,1)S(1)}, bf16[1024,256]{1,0:T(8,128)(2,1)S(1)}, u32[]{:S(2)}, u32[]{:S(2)}) %collective-permute-start.11) | collective-permute-done | bytes 524320 | tf_op jit(solution)/shard_map/ppermute | solution.py:499
  31.1 2.5 %collective-permute-start.13 = (bf16[1024,256]{1,0:T(8,128)(2,1)S(1)}, bf16[1024,256]{1,0:T(8,128)(2,1)S(1)}, u32[]{:S(2)}, u32[]{:S(2)}) collective-permute-start(bf16[1024,256]{1,0:T(8,128)(2,1)S(1)} %get-tuple-element.78), channel_id=1, source_target_pairs={{0,2},{1,3},{2,0},{3,1},{4,6},{5,7},{6,4},{7,5},{8,10},{9,11},{10,... | collective-permute-start | bytes 1572872 | tf_op jit(solution)/shard_map/ppermute | solution.py:499
  33.6 8.2 %collective-permute-done.5.refs_3_ = bf16[1024,256]{1,0:T(8,128)(2,1)S(1)} collective-permute-done((bf16[1024,256]{1,0:T(8,128)(2,1)S(1)}, bf16[1024,256]{1,0:T(8,128)(2,1)S(1)}, u32[]{:S(2)}, u32[]{:S(2)}) %collective-permute-start.5) | collective-permute-done | bytes 524320 | tf_op jit(solution)/shard_map/ppermute | solution.py:499
  42.5 2.5 %collective-permute-start.7 = (bf16[1024,256]{1,0:T(8,128)(2,1)S(1)}, bf16[1024,256]{1,0:T(8,128)(2,1)S(1)}, u32[]{:S(2)}, u32[]{:S(2)}) collective-permute-start(bf16[1024,256]{1,0:T(8,128)(2,1)S(1)} %get-tuple-element.68.refs_7_), channel_id=1, source_target_pairs={{0,2},{1,3},{2,0},{3,1},{4,6},{5,7},{6,4},{7,5},{8,10},{9,11},{10,... | collective-permute-start | bytes 1572872 | tf_op jit(solution)/shard_map/ppermute | solution.py:499
  45.0 1.6 %shard_map.136 = (bf16[256,1024]{1,0:T(8,128)(2,1)S(1)}, bf16[256,8192]{1,0:T(8,128)(2,1)}, f32[8,128]{1,0:T(8,128)S(1)}) custom-call(s32[1,128]{1,0:T(1,128)S(1)} %pad_bitcast_fusion.refs_0_, bf16[256,512]{1,0:T(8,128)(2,1)S(1)} %bitcast.47, bf16[256,512]{1,0:T(8,128)(2,1)S(1)} %collective-permute-done.refs_1_.refs_3_.refs_2_, ...), custom_call_target="tpu_custom_call", output_to_operand_aliasing={{1}: (6, {})} | custom-call | bytes 7140000 | tf_op jit(solution)/shard_map/pallas_call | solution.py:115
  46.7 6.3 %collective-permute-done.13.refs_3_ = bf16[1024,256]{1,0:T(8,128)(2,1)S(1)} collective-permute-done((bf16[1024,256]{1,0:T(8,128)(2,1)S(1)}, bf16[1024,256]{1,0:T(8,128)(2,1)S(1)}, u32[]{:S(2)}, u32[]{:S(2)}) %collective-permute-start.13) | collective-permute-done | bytes 524320 | tf_op jit(solution)/shard_map/ppermute | solution.py:499
  53.7 2.5 %collective-permute-start.16 = (bf16[1024,256]{1,0:T(8,128)(2,1)S(1)}, bf16[1024,256]{1,0:T(8,128)(2,1)S(1)}, u32[]{:S(2)}, u32[]{:S(2)}) collective-permute-start(bf16[1024,256]{1,0:T(8,128)(2,1)S(1)} %get-tuple-element.85), channel_id=1, source_target_pairs={{0,2},{1,3},{2,0},{3,1},{4,6},{5,7},{6,4},{7,5},{8,10},{9,11},{10,... | collective-permute-start | bytes 1572872 | tf_op jit(solution)/shard_map/ppermute | solution.py:499
  56.2 8.1 %collective-permute-done.7.refs_3_ = bf16[1024,256]{1,0:T(8,128)(2,1)S(1)} collective-permute-done((bf16[1024,256]{1,0:T(8,128)(2,1)S(1)}, bf16[1024,256]{1,0:T(8,128)(2,1)S(1)}, u32[]{:S(2)}, u32[]{:S(2)}) %collective-permute-start.7) | collective-permute-done | bytes 524320 | tf_op jit(solution)/shard_map/ppermute | solution.py:499
  64.9 1.6 %shard_map.138 = (bf16[256,1024]{1,0:T(8,128)(2,1)S(1)}, bf16[256,8192]{1,0:T(8,128)(2,1)}, f32[8,128]{1,0:T(8,128)S(1)}) custom-call(s32[1,128]{1,0:T(1,128)S(1)} %pad_bitcast_fusion.refs_0_, bf16[256,512]{1,0:T(8,128)(2,1)S(1)} %bitcast.48, bf16[256,512]{1,0:T(8,128)(2,1)S(1)} %collective-permute-done.refs_1_.refs_3_.refs_2_, ...), custom_call_target="tpu_custom_call", output_to_operand_aliasing={{1}: (6, {})} | custom-call | bytes 7140000 | tf_op jit(solution)/shard_map/pallas_call | solution.py:115
  66.6 2.2 %collective-permute-start.8 = (bf16[1024,256]{1,0:T(8,128)(2,1)S(1)}, bf16[1024,256]{1,0:T(8,128)(2,1)S(1)}, u32[]{:S(2)}, u32[]{:S(2)}) collective-permute-start(bf16[1024,256]{1,0:T(8,128)(2,1)S(1)} %get-tuple-element.69.refs_7_), channel_id=1, source_target_pairs={{0,2},{1,3},{2,0},{3,1},{4,6},{5,7},{6,4},{7,5},{8,10},{9,11},{10,... | collective-permute-start | bytes 1572872 | tf_op jit(solution)/shard_map/ppermute | solution.py:499
  69.0 6.6 %collective-permute-done.16.refs_3_ = bf16[1024,256]{1,0:T(8,128)(2,1)S(1)} collective-permute-done((bf16[1024,256]{1,0:T(8,128)(2,1)S(1)}, bf16[1024,256]{1,0:T(8,128)(2,1)S(1)}, u32[]{:S(2)}, u32[]{:S(2)}) %collective-permute-start.16) | collective-permute-done | bytes 524320 | tf_op jit(solution)/shard_map/ppermute | solution.py:499
  76.1 1.6 %shard_map.140 = (bf16[256,1024]{1,0:T(8,128)(2,1)S(1)}, bf16[256,8192]{1,0:T(8,128)(2,1)}, f32[8,128]{1,0:T(8,128)S(1)}) custom-call(s32[1,128]{1,0:T(1,128)S(1)} %pad_bitcast_fusion.refs_0_, bf16[256,512]{1,0:T(8,128)(2,1)S(1)} %bitcast.49, bf16[256,512]{1,0:T(8,128)(2,1)S(1)} %collective-permute-done.refs_1_.refs_3_.refs_2_, ...), custom_call_target="tpu_custom_call", output_to_operand_aliasing={{1}: (6, {})} | custom-call | bytes 7140000 | tf_op jit(solution)/shard_map/pallas_call | solution.py:115
  77.8 2.2 %collective-permute-start.20 = (bf16[1024,256]{1,0:T(8,128)(2,1)S(1)}, bf16[1024,256]{1,0:T(8,128)(2,1)S(1)}, u32[]{:S(2)}, u32[]{:S(2)}) collective-permute-start(bf16[1024,256]{1,0:T(8,128)(2,1)S(1)} %get-tuple-element.100), channel_id=1, source_target_pairs={{0,2},{1,3},{2,0},{3,1},{4,6},{5,7},{6,4},{7,5},{8,10},{9,11},{10,... | collective-permute-start | bytes 1572872 | tf_op jit(solution)/shard_map/ppermute | solution.py:499
  80.2 6.6 %collective-permute-done.8.refs_2_ = bf16[1024,256]{1,0:T(8,128)(2,1)S(1)} collective-permute-done((bf16[1024,256]{1,0:T(8,128)(2,1)S(1)}, bf16[1024,256]{1,0:T(8,128)(2,1)S(1)}, u32[]{:S(2)}, u32[]{:S(2)}) %collective-permute-start.8) | collective-permute-done | bytes 524320 | tf_op jit(solution)/shard_map/ppermute | solution.py:499
  87.3 1.6 %collective-permute-start.23 = (bf16[512,128]{1,0:T(8,128)(2,1)S(1)}, bf16[512,128]{1,0:T(8,128)(2,1)S(1)}, u32[]{:S(2)}, u32[]{:S(2)}) collective-permute-start(bf16[512,128]{1,0:T(8,128)(2,1)S(1)} %get-tuple-element.107), channel_id=1, source_target_pairs={{0,16},{8,24},{16,0},{24,8},{1,17},{9,25},{17,1},{25,9},{2,18},{10... | collective-permute-start | bytes 393224 | tf_op jit(solution)/shard_map/ppermute | solution.py:499
  90.4 1.9 %shard_map.142 = (f32[1024,512]{1,0:T(8,128)}, f32[1024,512]{1,0:T(8,128)}, f32[1024,512]{1,0:T(8,128)}, bf16[256,8192]{1,0:T(8,128)(2,1)}, f32[8,128]{1,0:T(8,128)S(1)}) custom-call(s32[1,128]{1,0:T(1,128)S(1)} %pad_bitcast_fusion.refs_0_, f32[4096,512]{1,0:T(8,128)S(1)} %get-tuple-element.64.refs_1_, ...), custom_call_target="tpu_custom_call", output_to_operand_aliasing={{3}: (10, {})} | custom-call | bytes 6800000 | tf_op jit(solution)/shard_map/pallas_call | solution.py:115
  96.0 1.6 %collective-permute-done.20.refs_2_ = bf16[1024,256]{1,0:T(8,128)(2,1)S(1)} collective-permute-done((bf16[1024,256]{1,0:T(8,128)(2,1)S(1)}, bf16[1024,256]{1,0:T(8,128)(2,1)S(1)}, u32[]{:S(2)}, u32[]{:S(2)}) %collective-permute-start.20) | collective-permute-done | bytes 524320 | tf_op jit(solution)/shard_map/ppermute | solution.py:499
  97.6 1.9 %shard_map.143 = (f32[1024,512]{1,0:T(8,128)}, f32[1024,512]{1,0:T(8,128)}, f32[1024,512]{1,0:T(8,128)}, f32[3,256,256]{2,1,0:T(8,128)S(1)}) custom-call(s32[1,128]{1,0:T(1,128)S(1)} %pad_bitcast_fusion.refs_0_, f32[4096,512]{1,0:T(8,128)S(1)} %get-tuple-element.64.refs_1_, ...), custom_call_target="tpu_custom_call", output_to_operand_aliasing={{0}: (7, {}), {1}: (8, {}), {2}: (9, {})} | custom-call | bytes 8160000 | tf_op jit(solution)/shard_map/pallas_call | solution.py:115
  99.5 1.6 %shard_map.144 = (f32[1024,512]{1,0:T(8,128)}, f32[1024,512]{1,0:T(8,128)}, f32[1024,512]{1,0:T(8,128)}, f32[1024,512]{1,0:T(8,128)}, f32[1024,512]{1,0:T(8,128)}) custom-call(s32[1,128]{1,0:T(1,128)S(1)} %pad_bitcast_fusion.refs_0_, ...), custom_call_target="tpu_custom_call", output_to_operand_aliasing={{0}: (8, {}), {1}: (9, {}), {2}: (10, {}), {3}: (11, {}), {... | custom-call | bytes 6800000 | tf_op jit(solution)/shard_map/pallas_call | solution.py:115
  (52 shorter events, 16.6 us)
Async XLA Ops:
  0.6 18.9 %collective-permute-start.1 = (bf16[256,8192]{1,0:T(8,128)(2,1)}, bf16[256,8192]{1,0:T(8,128)(2,1)}, u32[]{:S(2)}, u32[]{:S(2)}) collective-permute-start(bf16[256,8192]{1,0:T(8,128)(2,1)} %bitcast.57), channel_id=1, source_target_pairs={{0,1},{1,0},{2,3},{3,2},{4,5},{5,4},{6,7},{7,6},{8,9},{9,8},{10,11... | collective-permute-start | bytes 12582920 | tf_op jit(solution)/shard_map/ppermute | solution.py:499
  2.4 21.5 %collective-permute-start.2 = (bf16[1024,256]{1,0:T(8,128)(2,1)S(1)}, bf16[1024,256]{1,0:T(8,128)(2,1)S(1)}, u32[]{:S(2)}, u32[]{:S(2)}) collective-permute-start(bf16[1024,256]{1,0:T(8,128)(2,1)S(1)} %shard_map.130.refs_3_), channel_id=1, source_target_pairs={{0,1},{1,0},{2,4},{3,5},{4,2},{5,3},{6,7},{7,6},{8,9},{9,8},{10,12... | collective-permute-start | bytes 1572872 | tf_op jit(solution)/shard_map/ppermute | solution.py:499
  2.5 21.3 %collective-permute-start.3 = (bf16[1024,256]{1,0:T(8,128)(2,1)S(1)}, bf16[1024,256]{1,0:T(8,128)(2,1)S(1)}, u32[]{:S(2)}, u32[]{:S(2)}) collective-permute-start(bf16[1024,256]{1,0:T(8,128)(2,1)S(1)} %shard_map.130.refs_3_), channel_id=1, source_target_pairs={{0,2},{1,3},{2,0},{3,1},{4,6},{5,7},{6,4},{7,5},{8,10},{9,11},{10,... | collective-permute-start | bytes 1572872 | tf_op jit(solution)/shard_map/ppermute | solution.py:499
  10.3 18.2 %collective-permute-start.10 = (bf16[1024,256]{1,0:T(8,128)(2,1)S(1)}, bf16[1024,256]{1,0:T(8,128)(2,1)S(1)}, u32[]{:S(2)}, u32[]{:S(2)}) collective-permute-start(bf16[1024,256]{1,0:T(8,128)(2,1)S(1)} %shard_map.127.refs_5_.refs_4_), channel_id=1, source_target_pairs={{0,1},{1,0},{2,4},{3,5},{4,2},{5,3},{6,7},{7,6},{8,9},{9,8},{10,12... | collective-permute-start | bytes 1572872 | tf_op jit(solution)/shard_map/ppermute | solution.py:499
  10.8 19.8 %collective-permute-start.11 = (bf16[1024,256]{1,0:T(8,128)(2,1)S(1)}, bf16[1024,256]{1,0:T(8,128)(2,1)S(1)}, u32[]{:S(2)}, u32[]{:S(2)}) collective-permute-start(bf16[1024,256]{1,0:T(8,128)(2,1)S(1)} %shard_map.127.refs_5_.refs_4_), channel_id=1, source_target_pairs={{0,2},{1,3},{2,0},{3,1},{4,6},{5,7},{6,4},{7,5},{8,10},{9,11},{10,... | collective-permute-start | bytes 1572872 | tf_op jit(solution)/shard_map/ppermute | solution.py:499
  24.3 9.2 %collective-permute-start.4 = (bf16[1024,256]{1,0:T(8,128)(2,1)S(1)}, bf16[1024,256]{1,0:T(8,128)(2,1)S(1)}, u32[]{:S(2)}, u32[]{:S(2)}) collective-permute-start(bf16[1024,256]{1,0:T(8,128)(2,1)S(1)} %get-tuple-element.65), channel_id=1, source_target_pairs={{0,1},{1,0},{2,4},{3,5},{4,2},{5,3},{6,7},{7,6},{8,9},{9,8},{10,12... | collective-permute-start | bytes 1572872 | tf_op jit(solution)/shard_map/ppermute | solution.py:499
  24.4 17.4 %collective-permute-start.5 = (bf16[1024,256]{1,0:T(8,128)(2,1)S(1)}, bf16[1024,256]{1,0:T(8,128)(2,1)S(1)}, u32[]{:S(2)}, u32[]{:S(2)}) collective-permute-start(bf16[1024,256]{1,0:T(8,128)(2,1)S(1)} %get-tuple-element.66.refs_5_), channel_id=1, source_target_pairs={{0,2},{1,3},{2,0},{3,1},{4,6},{5,7},{6,4},{7,5},{8,10},{9,11},{10,... | collective-permute-start | bytes 1572872 | tf_op jit(solution)/shard_map/ppermute | solution.py:499
  28.4 16.6 %collective-permute-start.14 = (bf16[256,1024]{1,0:T(8,128)(2,1)S(1)}, bf16[256,1024]{1,0:T(8,128)(2,1)S(1)}, u32[]{:S(2)}, u32[]{:S(2)}) collective-permute-start(bf16[256,1024]{1,0:T(8,128)(2,1)S(1)} %get-tuple-element.81), channel_id=1, source_target_pairs={{0,1},{1,0},{2,3},{3,2},{4,5},{5,4},{6,7},{7,6},{8,9},{9,8},{10,11... | collective-permute-start | bytes 1572872 | tf_op jit(solution)/shard_map/ppermute | solution.py:499
  31.0 15.7 %collective-permute-start.12 = (bf16[1024,256]{1,0:T(8,128)(2,1)S(1)}, bf16[1024,256]{1,0:T(8,128)(2,1)S(1)}, u32[]{:S(2)}, u32[]{:S(2)}) collective-permute-start(bf16[1024,256]{1,0:T(8,128)(2,1)S(1)} %get-tuple-element.77), channel_id=1, source_target_pairs={{0,1},{1,0},{2,4},{3,5},{4,2},{5,3},{6,7},{7,6},{8,9},{9,8},{10,12... | collective-permute-start | bytes 1572872 | tf_op jit(solution)/shard_map/ppermute | solution.py:499
  31.1 21.9 %collective-permute-start.13 = (bf16[1024,256]{1,0:T(8,128)(2,1)S(1)}, bf16[1024,256]{1,0:T(8,128)(2,1)S(1)}, u32[]{:S(2)}, u32[]{:S(2)}) collective-permute-start(bf16[1024,256]{1,0:T(8,128)(2,1)S(1)} %get-tuple-element.78), channel_id=1, source_target_pairs={{0,2},{1,3},{2,0},{3,1},{4,6},{5,7},{6,4},{7,5},{8,10},{9,11},{10,... | collective-permute-start | bytes 1572872 | tf_op jit(solution)/shard_map/ppermute | solution.py:499
  42.4 13.8 %collective-permute-start.6 = (bf16[1024,256]{1,0:T(8,128)(2,1)S(1)}, bf16[1024,256]{1,0:T(8,128)(2,1)S(1)}, u32[]{:S(2)}, u32[]{:S(2)}) collective-permute-start(bf16[1024,256]{1,0:T(8,128)(2,1)S(1)} %get-tuple-element.67), channel_id=1, source_target_pairs={{0,1},{1,0},{2,4},{3,5},{4,2},{5,3},{6,7},{7,6},{8,9},{9,8},{10,12... | collective-permute-start | bytes 1572872 | tf_op jit(solution)/shard_map/ppermute | solution.py:499
  42.5 21.8 %collective-permute-start.7 = (bf16[1024,256]{1,0:T(8,128)(2,1)S(1)}, bf16[1024,256]{1,0:T(8,128)(2,1)S(1)}, u32[]{:S(2)}, u32[]{:S(2)}) collective-permute-start(bf16[1024,256]{1,0:T(8,128)(2,1)S(1)} %get-tuple-element.68.refs_7_), channel_id=1, source_target_pairs={{0,2},{1,3},{2,0},{3,1},{4,6},{5,7},{6,4},{7,5},{8,10},{9,11},{10,... | collective-permute-start | bytes 1572872 | tf_op jit(solution)/shard_map/ppermute | solution.py:499
  46.6 18.2 %collective-permute-start.17 = (bf16[256,1024]{1,0:T(8,128)(2,1)S(1)}, bf16[256,1024]{1,0:T(8,128)(2,1)S(1)}, u32[]{:S(2)}, u32[]{:S(2)}) collective-permute-start(bf16[256,1024]{1,0:T(8,128)(2,1)S(1)} %get-tuple-element.88), channel_id=1, source_target_pairs={{0,1},{1,0},{2,3},{3,2},{4,5},{5,4},{6,7},{7,6},{8,9},{9,8},{10,11... | collective-permute-start | bytes 1572872 | tf_op jit(solution)/shard_map/ppermute | solution.py:499
  53.6 15.3 %collective-permute-start.15 = (bf16[1024,256]{1,0:T(8,128)(2,1)S(1)}, bf16[1024,256]{1,0:T(8,128)(2,1)S(1)}, u32[]{:S(2)}, u32[]{:S(2)}) collective-permute-start(bf16[1024,256]{1,0:T(8,128)(2,1)S(1)} %get-tuple-element.84), channel_id=1, source_target_pairs={{0,1},{1,0},{2,4},{3,5},{4,2},{5,3},{6,7},{7,6},{8,9},{9,8},{10,12... | collective-permute-start | bytes 1572872 | tf_op jit(solution)/shard_map/ppermute | solution.py:499
  53.7 21.8 %collective-permute-start.16 = (bf16[1024,256]{1,0:T(8,128)(2,1)S(1)}, bf16[1024,256]{1,0:T(8,128)(2,1)S(1)}, u32[]{:S(2)}, u32[]{:S(2)}) collective-permute-start(bf16[1024,256]{1,0:T(8,128)(2,1)S(1)} %get-tuple-element.85), channel_id=1, source_target_pairs={{0,2},{1,3},{2,0},{3,1},{4,6},{5,7},{6,4},{7,5},{8,10},{9,11},{10,... | collective-permute-start | bytes 1572872 | tf_op jit(solution)/shard_map/ppermute | solution.py:499
  66.5 9.6 %collective-permute-start.18 = (bf16[256,1024]{1,0:T(8,128)(2,1)S(1)}, bf16[256,1024]{1,0:T(8,128)(2,1)S(1)}, u32[]{:S(2)}, u32[]{:S(2)}) collective-permute-start(bf16[256,1024]{1,0:T(8,128)(2,1)S(1)} %get-tuple-element.92), channel_id=1, source_target_pairs={{0,1},{1,0},{2,3},{3,2},{4,5},{5,4},{6,7},{7,6},{8,9},{9,8},{10,11... | collective-permute-start | bytes 1572872 | tf_op jit(solution)/shard_map/ppermute | solution.py:499
  66.6 20.2 %collective-permute-start.8 = (bf16[1024,256]{1,0:T(8,128)(2,1)S(1)}, bf16[1024,256]{1,0:T(8,128)(2,1)S(1)}, u32[]{:S(2)}, u32[]{:S(2)}) collective-permute-start(bf16[1024,256]{1,0:T(8,128)(2,1)S(1)} %get-tuple-element.69.refs_7_), channel_id=1, source_target_pairs={{0,2},{1,3},{2,0},{3,1},{4,6},{5,7},{6,4},{7,5},{8,10},{9,11},{10,... | collective-permute-start | bytes 1572872 | tf_op jit(solution)/shard_map/ppermute | solution.py:499
  68.8 18.0 %collective-permute-start.9 = (bf16[1024,256]{1,0:T(8,128)(2,1)S(1)}, bf16[1024,256]{1,0:T(8,128)(2,1)S(1)}, u32[]{:S(2)}, u32[]{:S(2)}) collective-permute-start(bf16[1024,256]{1,0:T(8,128)(2,1)S(1)} %get-tuple-element.70), channel_id=1, source_target_pairs={{0,1},{1,0},{2,4},{3,5},{4,2},{5,3},{6,7},{7,6},{8,9},{9,8},{10,12... | collective-permute-start | bytes 1572872 | tf_op jit(solution)/shard_map/ppermute | solution.py:499
  77.7 12.6 %collective-permute-start.19 = (bf16[256,1024]{1,0:T(8,128)(2,1)S(1)}, bf16[256,1024]{1,0:T(8,128)(2,1)S(1)}, u32[]{:S(2)}, u32[]{:S(2)}) collective-permute-start(bf16[256,1024]{1,0:T(8,128)(2,1)S(1)} %get-tuple-element.97), channel_id=1, source_target_pairs={{0,1},{1,0},{2,3},{3,2},{4,5},{5,4},{6,7},{7,6},{8,9},{9,8},{10,11... | collective-permute-start | bytes 1572872 | tf_op jit(solution)/shard_map/ppermute | solution.py:499
  77.8 19.8 %collective-permute-start.20 = (bf16[1024,256]{1,0:T(8,128)(2,1)S(1)}, bf16[1024,256]{1,0:T(8,128)(2,1)S(1)}, u32[]{:S(2)}, u32[]{:S(2)}) collective-permute-start(bf16[1024,256]{1,0:T(8,128)(2,1)S(1)} %get-tuple-element.100), channel_id=1, source_target_pairs={{0,2},{1,3},{2,0},{3,1},{4,6},{5,7},{6,4},{7,5},{8,10},{9,11},{10,... | collective-permute-start | bytes 1572872 | tf_op jit(solution)/shard_map/ppermute | solution.py:499
  80.0 17.6 %collective-permute-start.21 = (bf16[1024,256]{1,0:T(8,128)(2,1)S(1)}, bf16[1024,256]{1,0:T(8,128)(2,1)S(1)}, u32[]{:S(2)}, u32[]{:S(2)}) collective-permute-start(bf16[1024,256]{1,0:T(8,128)(2,1)S(1)} %get-tuple-element.101), channel_id=1, source_target_pairs={{0,1},{1,0},{2,4},{3,5},{4,2},{5,3},{6,7},{7,6},{8,9},{9,8},{10,12... | collective-permute-start | bytes 1572872 | tf_op jit(solution)/shard_map/ppermute | solution.py:499
  87.3 5.0 %collective-permute-start.23 = (bf16[512,128]{1,0:T(8,128)(2,1)S(1)}, bf16[512,128]{1,0:T(8,128)(2,1)S(1)}, u32[]{:S(2)}, u32[]{:S(2)}) collective-permute-start(bf16[512,128]{1,0:T(8,128)(2,1)S(1)} %get-tuple-element.107), channel_id=1, source_target_pairs={{0,16},{8,24},{16,0},{24,8},{1,17},{9,25},{17,1},{25,9},{2,18},{10... | collective-permute-start | bytes 393224 | tf_op jit(solution)/shard_map/ppermute | solution.py:499
  93.9 5.6 %collective-permute-start.24 = (bf16[512,128]{1,0:T(8,128)(2,1)S(1)}, bf16[512,128]{1,0:T(8,128)(2,1)S(1)}, u32[]{:S(2)}, u32[]{:S(2)}) collective-permute-start(bf16[512,128]{1,0:T(8,128)(2,1)S(1)} %get-tuple-element.121.refs_10_.refs_2_), channel_id=1, source_target_pairs={{0,16},{8,24},{16,0},{24,8},{1,17},{9,25},{17,1},{25,9},{2,18},{10... | collective-permute-start | bytes 393224 | tf_op jit(solution)/shard_map/ppermute | solution.py:499
  94.5 5.0 %collective-permute-start.25 = (bf16[512,128]{1,0:T(8,128)(2,1)S(1)}, bf16[512,128]{1,0:T(8,128)(2,1)S(1)}, u32[]{:S(2)}, u32[]{:S(2)}) collective-permute-start(bf16[512,128]{1,0:T(8,128)(2,1)S(1)} %get-tuple-element.120.refs_11_.refs_4_), channel_id=1, source_target_pairs={{0,8},{8,0},{16,24},{24,16},{1,9},{9,1},{17,25},{25,17},{2,10},{10... | collective-permute-start | bytes 393224 | tf_op jit(solution)/shard_map/ppermute | solution.py:499
  (3 other events, 13.4 us)
